TPU v7x, 256 devices: a whole 4x4x8 slice. The times are simulated.
256 devices in a mesh: row: 8 (over x, core), col: 32 (over z, y).
Axes of the slice: x: 4, y: 4, z: 8, core: 2. Of those that a mesh axis runs over, the one named last changes fastest.
Arguments:
- field_start: float32 [8192, 24576], P('row', 'col'), may hold values from -6 to 6
- w_sensor: bfloat16 [512, 512], replicated, may hold values from -0.25 to 0.25
- bias_sensor: float32 [512], replicated, may hold values from -3 to 3
- w_middle: bfloat16 [512, 512], replicated, may hold values from -0.25 to 0.25
- bias_middle: float32 [512], replicated, may hold values from -3 to 3
- w_latent: bfloat16 [512, 512], replicated, may hold values from -0.25 to 0.25
- bias_latent: float32 [512], replicated, may hold values from -3 to 3
- trunk_basis: bfloat16 [512, 4096], replicated, may hold values from -1 to 1
- coarse_matrix: float32 [3072, 3072], P(('row', 'col')), may hold values from -0.4375 to 0.4375
Outputs:
- field_final: float32 [8192, 24576], P('row', 'col')
All inputs are finite; a program needn't handle non-finite values.
Results may differ from a plain program's by a relative error of at most 0.024.
Values may be sent and summed in bfloat16 or wider, within the bound.
No kernel may reach another device: no remote copies, remote signals or barrier semaphores. Data moves between devices by JAX's collectives and lax.ppermute only.
A program may use at most 128 MiB of HBM per device.

v0:
```python
import jax
import jax.numpy as jnp
from jax import lax
from jax.sharding import PartitionSpec as P

TILE = 64
ITERS = 4
CELL = 256


def padded_2(cells, sides, width):
    for axis, dim in sides:
        count = lax.axis_size(axis)
        ends = count - 1
        head = lax.slice_in_dim(cells, 0, width, axis=dim)
        tail = lax.slice_in_dim(cells, cells.shape[dim] - width, cells.shape[dim], axis=dim)
        cells = jnp.concatenate(
            [
                lax.ppermute(tail, axis, [(i, (i + 1) % count) for i in range(ends)]),
                cells,
                lax.ppermute(head, axis, [((i + 1) % count, i) for i in range(ends)]),
            ],
            axis=dim,
        )
    return cells


def strip_windows(strips, count, tile):
    blocks = strips.reshape(strips.shape[0], count + 1, tile)
    return jnp.concatenate([blocks[:, :-1], blocks[:, 1:]], axis=2)


def cycle_values(padded, tile, count_x, count_y):
    side = 2 * tile
    top_rows = padded[0 : count_x * tile : tile, :]
    bottom_rows = padded[side - 1 : side - 1 + count_x * tile : tile, :]
    left_cols = padded[:, 0 : count_y * tile : tile].T
    right_cols = padded[:, side - 1 : side - 1 + count_y * tile : tile].T
    tops = strip_windows(top_rows, count_y, tile)
    bottoms = strip_windows(bottom_rows, count_y, tile)
    lefts = strip_windows(left_cols, count_x, tile).transpose(1, 0, 2)
    rights = strip_windows(right_cols, count_x, tile).transpose(1, 0, 2)
    joined = jnp.concatenate([tops, bottoms, lefts, rights], axis=2)
    return joined.reshape(count_x * count_y, 4 * side)


def branch_net(cycle, w_sensor, bias_sensor, w_middle, bias_middle, w_latent, bias_latent):
    hidden = jnp.tanh(
        jnp.dot(cycle, w_sensor, preferred_element_type=jnp.float32) + bias_sensor
    ).astype(jnp.bfloat16)
    hidden = jnp.tanh(
        jnp.dot(hidden, w_middle, preferred_element_type=jnp.float32) + bias_middle
    ).astype(jnp.bfloat16)
    return (jnp.dot(hidden, w_latent, preferred_element_type=jnp.float32) + bias_latent).astype(
        jnp.bfloat16
    )


def body(
    field_start,
    w_sensor,
    bias_sensor,
    w_middle,
    bias_middle,
    w_latent,
    bias_latent,
    trunk_basis,
    coarse_matrix,
):
    tile = TILE
    rows_here, cols_here = field_start.shape
    count_x = rows_here // tile
    count_y = cols_here // tile
    coarse_x = rows_here // CELL
    coarse_y = cols_here // CELL
    field = field_start
    for step in range(ITERS):
        sensor_field = field.astype(jnp.bfloat16)
        padded = padded_2(sensor_field, (("row", 0), ("col", 1)), tile // 2)
        cycle = cycle_values(padded, tile, count_x, count_y)
        coeffs = branch_net(
            cycle, w_sensor, bias_sensor, w_middle, bias_middle, w_latent, bias_latent
        )
        values = jnp.dot(coeffs, trunk_basis, preferred_element_type=jnp.float32)
        prediction = (
            values.reshape(count_x, count_y, tile, tile)
            .transpose(0, 2, 1, 3)
            .reshape(rows_here, cols_here)
        )
        blocks = prediction.reshape(coarse_x, CELL, coarse_y, CELL)
        means = jnp.mean(blocks, axis=(1, 3)).reshape(coarse_x * coarse_y)
        all_means = lax.all_gather(means, ("row", "col"), axis=0, tiled=True)
        correction = jnp.dot(coarse_matrix, all_means, precision=lax.Precision.HIGHEST)
        field = (blocks + correction.reshape(coarse_x, 1, coarse_y, 1)).reshape(
            rows_here, cols_here
        )
    return field


def solution(mesh):
    placed = (P("row", "col"), P(), P(), P(), P(), P(), P(), P(), P(("row", "col"), None))
    return jax.shard_map(
        body, mesh=mesh, in_specs=placed, out_specs=P("row", "col"), check_vma=False
    )
```

profile of v0, /device:TPU:1, one launch (start us, length us, event | category | flops | bytes accessed | tf_op | source)
XLA Modules:
  0.0 616.8 jit_solution(2281350520898988673)
XLA Ops:
  0.0 2.1 convert_element_type.48
  2.1 4.5 collective-permute-start
  6.6 1.9 collective-permute-start.1
  8.6 3.5 collective-permute-done.1
  12.2 3.2 collective-permute-start.2
  16.7 3.3 collective-permute-done.2
  20.1 4.1 collective-permute-done.3
  24.2 2.4 pad_maximum_fusion
  26.5 3.9 slice.202
  30.5 4.1 slice.205
  39.9 5.0 fusion.23
  45.0 6.1 reshape.120
  51.1 7.0 %copy.96 = f32[16,12,64,64]{2,0,3,1:T(8,128)} copy(f32[16,12,64,64]{3,2,1,0:T(8,128)} %reshape.120) | data formatting | bytes 6291456 | tf_op jit(solution)/shard_map/reshape | solution.py:86
  58.0 3.3 bitcast_reduce_fusion.3
  62.0 83.0 %all-reduce = f32[3072]{0:T(1024)S(1)} all-reduce(f32[3072]{0:T(1024)S(1)} %dynamic-update-slice), channel_id=1, replica_groups=mesh['row'=8,'col'=32] {'row','col'}, use_global_device_ids=true, to_apply=%add | all-reduce | flops 3072 | bytes 24576
  145.9 2.4 copy.164
  148.4 6.3 %reshape_reshape.12 = f32[1024,768]{0,1:T(8,128)} reshape(f32[16,64,12,64]{1,0,3,2:T(8,128)} %bitcast.131) | data formatting | bytes 6291456 | tf_op jit(solution)/shard_map/reshape;reshape | solution.py:90
  154.7 3.4 add_convert_fusion.2
  158.2 3.3 collective-permute-start.4
  164.0 4.4 collective-permute-done.5
  168.4 2.8 concatenate.65
  175.0 3.8 collective-permute-done.7
  178.8 2.9 pad_maximum_fusion.1
  184.7 3.2 slice.212
  187.9 3.2 slice.215
  194.2 5.0 fusion.22
  199.2 6.1 reshape.126
  205.3 7.0 %copy.106 = f32[16,12,64,64]{2,0,3,1:T(8,128)} copy(f32[16,12,64,64]{3,2,1,0:T(8,128)} %reshape.126) | data formatting | bytes 6291456 | tf_op jit(solution)/shard_map/reshape | solution.py:86
  212.3 3.3 bitcast_reduce_fusion.2
  216.2 79.6 %all-reduce.1 = f32[3072]{0:T(1024)S(1)} all-reduce(f32[3072]{0:T(1024)S(1)} %dynamic-update-slice.1), channel_id=1, replica_groups=mesh['row'=8,'col'=32] {'row','col'}, use_global_device_ids=true, to_apply=%add.1 | all-reduce | flops 3072 | bytes 24576
  296.8 2.4 copy.165
  299.2 6.3 %reshape_reshape.13 = f32[1024,768]{0,1:T(8,128)} reshape(f32[16,64,12,64]{1,0,3,2:T(8,128)} %bitcast.132) | data formatting | bytes 6291456 | tf_op jit(solution)/shard_map/reshape;reshape | solution.py:90
  305.5 3.4 add_convert_fusion.1
  309.0 3.0 collective-permute-start.8
  314.6 4.4 collective-permute-done.9
  319.0 2.8 concatenate.70
  325.6 3.8 collective-permute-done.11
  329.4 2.9 pad_maximum_fusion.2
  335.3 3.2 slice.228
  338.5 3.2 slice.231
  344.8 5.0 fusion.21
  349.8 6.1 reshape.132
  355.9 7.0 %copy.116 = f32[16,12,64,64]{2,0,3,1:T(8,128)} copy(f32[16,12,64,64]{3,2,1,0:T(8,128)} %reshape.132) | data formatting | bytes 6291456 | tf_op jit(solution)/shard_map/reshape | solution.py:86
  362.9 3.3 bitcast_reduce_fusion.1
  366.8 79.9 %all-reduce.2 = f32[3072]{0:T(1024)S(1)} all-reduce(f32[3072]{0:T(1024)S(1)} %dynamic-update-slice.2), channel_id=1, replica_groups=mesh['row'=8,'col'=32] {'row','col'}, use_global_device_ids=true, to_apply=%add.2 | all-reduce | flops 3072 | bytes 24576
  447.6 2.4 copy.166
  450.1 6.3 %reshape_reshape.14 = f32[1024,768]{0,1:T(8,128)} reshape(f32[16,64,12,64]{1,0,3,2:T(8,128)} %bitcast.133) | data formatting | bytes 6291456 | tf_op jit(solution)/shard_map/reshape;reshape | solution.py:90
  456.4 3.4 add_convert_fusion
  459.9 2.8 collective-permute-start.12
  465.3 4.4 collective-permute-done.13
  469.6 2.8 concatenate.75
  476.5 3.5 collective-permute-done.15
  480.0 2.9 pad_maximum_fusion.3
  486.0 3.2 slice.244
  489.2 3.2 slice.247
  495.4 5.1 fusion.20
  500.5 6.1 reshape.138
  506.6 7.0 %copy.126 = f32[16,12,64,64]{2,0,3,1:T(8,128)} copy(f32[16,12,64,64]{3,2,1,0:T(8,128)} %reshape.138) | data formatting | bytes 6291456 | tf_op jit(solution)/shard_map/reshape | solution.py:86
  513.5 3.3 bitcast_reduce_fusion
  517.4 80.3 %all-reduce.3 = f32[3072]{0:T(1024)S(1)} all-reduce(f32[3072]{0:T(1024)S(1)} %dynamic-update-slice.3), channel_id=1, replica_groups=mesh['row'=8,'col'=32] {'row','col'}, use_global_device_ids=true, to_apply=%add.3 | all-reduce | flops 3072 | bytes 24576
  598.7 2.4 copy.167
  601.1 6.3 %reshape_reshape.15 = f32[1024,768]{0,1:T(8,128)} reshape(f32[16,64,12,64]{1,0,3,2:T(8,128)} %bitcast.130) | data formatting | bytes 6291456 | tf_op jit(solution)/shard_map/reshape;reshape | solution.py:90
  607.4 5.4 add.160
  612.8 3.5 copy.129
  (152 shorter events, 50.3 us)
Async XLA Ops:
  0.0 39.9 %copy-start = (bf16[512,512]{1,0:T(8,128)(2,1)S(1)}, bf16[512,512]{1,0:T(8,128)(2,1)}, u32[]{:S(2)}) copy-start(bf16[512,512]{1,0:T(8,128)(2,1)} %param.14) | copy-start | bytes 1572868
  2.1 6.5 %collective-permute-start = (bf16[32,768]{1,0:T(8,128)(2,1)S(1)}, bf16[32,768]{1,0:T(8,128)(2,1)S(1)}, u32[]{:S(2)}, u32[]{:S(2)}) collective-permute-start(bf16[32,768]{1,0:T(8,128)(2,1)S(1)} %get-tuple-element.19), channel_id=1, source_target_pairs={{0,32},{32,64},{64,96},{96,128},{128,160},{160,192},{192,224},{1,3... | collective-permute-start | bytes 147464 | tf_op jit(solution)/shard_map/ppermute | solution.py:19
  6.6 5.4 collective-permute-start.1
  12.2 7.9 %collective-permute-start.2 = (bf16[1088,32]{1,0:T(8,128)(2,1)S(1)}, bf16[1088,32]{1,0:T(8,128)(2,1)S(1)}, u32[]{:S(2)}, u32[]{:S(2)}) collective-permute-start(bf16[1088,32]{1,0:T(8,128)(2,1)S(1)} %get-tuple-element.11), channel_id=1, source_target_pairs={{0,1},{1,2},{2,3},{3,4},{4,5},{5,6},{6,7},{7,8},{8,9},{9,10},{10,1... | collective-permute-start | bytes 208904 | tf_op jit(solution)/shard_map/ppermute | solution.py:19
  15.4 8.7 %collective-permute-start.3 = (bf16[1088,32]{1,0:T(8,128)(2,1)S(1)}, bf16[1088,32]{1,0:T(8,128)(2,1)S(1)}, u32[]{:S(2)}, u32[]{:S(2)}) collective-permute-start(bf16[1088,32]{1,0:T(8,128)(2,1)S(1)} %get-tuple-element.12), channel_id=1, source_target_pairs={{1,0},{2,1},{3,2},{4,3},{5,4},{6,5},{7,6},{8,7},{9,8},{10,9},{11,1... | collective-permute-start | bytes 208904 | tf_op jit(solution)/shard_map/ppermute | solution.py:21
  30.5 8.9 %copy-start.3 = (bf16[512,512]{1,0:T(8,128)(2,1)S(1)}, bf16[512,512]{1,0:T(8,128)(2,1)}, u32[]{:S(2)}) copy-start(bf16[512,512]{1,0:T(8,128)(2,1)} %param.12) | copy-start | bytes 1572868
  30.5 8.9 %copy-start.4 = (bf16[512,512]{1,0:T(8,128)(2,1)S(1)}, bf16[512,512]{1,0:T(8,128)(2,1)}, u32[]{:S(2)}) copy-start(bf16[512,512]{1,0:T(8,128)(2,1)} %param.10) | copy-start | bytes 1572868
  30.5 8.9 %copy-start.5 = (f32[512]{0:T(512)S(1)}, f32[512]{0:T(512)}, u32[]{:S(2)}) copy-start(f32[512]{0:T(512)} %param.13) | copy-start | bytes 6148
  30.5 8.9 %copy-start.6 = (f32[512]{0:T(512)S(1)}, f32[512]{0:T(512)}, u32[]{:S(2)}) copy-start(f32[512]{0:T(512)} %param.11) | copy-start | bytes 6148
  37.9 2.1 copy-start.2
  58.0 86.9 %copy-start.1 = (f32[12,3072]{1,0:T(8,128)S(1)}, f32[12,3072]{1,0:T(8,128)}, u32[]{:S(2)}) copy-start(f32[12,3072]{1,0:T(8,128)} %param.17) | copy-start | bytes 442372
  158.2 5.9 collective-permute-start.4
  161.4 7.0 %collective-permute-start.5 = (bf16[32,768]{0,1:T(8,128)(2,1)S(1)}, bf16[32,768]{0,1:T(8,128)(2,1)S(1)}, u32[]{:S(2)}, u32[]{:S(2)}) collective-permute-start(bf16[32,768]{0,1:T(8,128)(2,1)S(1)} %get-tuple-element.17), channel_id=1, source_target_pairs={{32,0},{64,32},{96,64},{128,96},{160,128},{192,160},{224,192},{33,... | collective-permute-start | bytes 147464 | tf_op jit(solution)/shard_map/ppermute | solution.py:21
  172.2 2.8 collective-permute-start.6
  173.5 5.3 collective-permute-start.7
  309.0 5.6 collective-permute-start.8
  312.0 7.0 %collective-permute-start.9 = (bf16[32,768]{0,1:T(8,128)(2,1)S(1)}, bf16[32,768]{0,1:T(8,128)(2,1)S(1)}, u32[]{:S(2)}, u32[]{:S(2)}) collective-permute-start(bf16[32,768]{0,1:T(8,128)(2,1)S(1)} %get-tuple-element.15), channel_id=1, source_target_pairs={{32,0},{64,32},{96,64},{128,96},{160,128},{192,160},{224,192},{33,... | collective-permute-start | bytes 147464 | tf_op jit(solution)/shard_map/ppermute | solution.py:21
  322.8 2.8 collective-permute-start.10
  324.1 5.3 collective-permute-start.11
  459.9 5.4 collective-permute-start.12
  462.7 7.0 %collective-permute-start.13 = (bf16[32,768]{0,1:T(8,128)(2,1)S(1)}, bf16[32,768]{0,1:T(8,128)(2,1)S(1)}, u32[]{:S(2)}, u32[]{:S(2)}) collective-permute-start(bf16[32,768]{0,1:T(8,128)(2,1)S(1)} %get-tuple-element.13), channel_id=1, source_target_pairs={{32,0},{64,32},{96,64},{128,96},{160,128},{192,160},{224,192},{33,... | collective-permute-start | bytes 147464 | tf_op jit(solution)/shard_map/ppermute | solution.py:21
  473.4 3.1 collective-permute-start.14
  474.9 5.1 collective-permute-start.15
where the time goes:
time: 627 us; the launch traced here: 617 us
  blocking collectives  323 us (52%)
  local copies, waits for them, and re-layouts  152 us (24%)
  other arithmetic  43.1 us (7%)
  waiting for transfers between devices  37.2 us (6%)
  starting transfers between devices  34.4 us (5%)
  matrix products  26.3 us (4%)
    unnamed x4, blocking collectives  323 us
    reshape x8, local copies, waits for them, and re-layouts, body(): values.reshape(count_x, count_y, tile, tile).transpose(0, 2, 1, 3)  52.2 us
    ppermute x8, waiting for transfers between devices, padded_2(): lax.ppermute(head, axis, [((i + 1) % count, i) for i in range(ends)])  31.9 us
    another operation x4, local copies, waits for them, and re-layouts, body(): blocks = prediction.reshape(coarse_x, CELL, coarse_y, CELL)  25.2 us
    ppermute x8, starting transfers between devices, padded_2(): lax.ppermute(tail, axis, [(i, (i + 1) % count) for i in range(ends)])  20.9 us
    dot_general x4, matrix products, body(): values = jnp.dot(coeffs, trunk_basis, preferred_element_type=jnp.float32)  20.2 us
    reduce_sum x8, other arithmetic, body(): means = jnp.mean(blocks, axis=(1, 3)).reshape(coarse_x * coarse_y)  13.6 us
    ppermute x8, starting transfers between devices, padded_2(): lax.ppermute(head, axis, [((i + 1) % count, i) for i in range(ends)])  13.5 us
  transfers between devices with their start and end apart: 16, of which 12 were waited for; matrix products, arithmetic and copies ran while one was open for 0% of the time, Pallas kernels for 0%

commit v1 on v0

v1 whole, which is shorter than its diff:
```python
import functools

import jax
import jax.numpy as jnp
import numpy as np
from jax import lax
from jax.experimental import pallas as pl
from jax.experimental.pallas import tpu as pltpu
from jax.sharding import PartitionSpec as P

TILE = 64
ITERS = 4
CELL = 256
PER_CELL = CELL // TILE
HALO = ITERS
LANES = 128
F32 = jnp.float32
BF16 = jnp.bfloat16
VMEM_LIMIT = 48 * 1024 * 1024


def dot(a, b, **kw):
    return jnp.dot(a, b, preferred_element_type=F32, **kw)


def nt_dot(a, b):
    return lax.dot_general(a, b, (((1,), (1,)), ((), ())), preferred_element_type=F32)


def low_lanes(shape):
    return lax.broadcasted_iota(jnp.int32, shape, 1) < TILE


def call(kernel, out_shape, *args, grid=(), in_specs=None, out_specs=None, scratch=(), flops=0):
    whole = pl.BlockSpec(memory_space=pltpu.VMEM)
    specs = {}
    if grid:
        specs["grid"] = grid
    return pl.pallas_call(
        kernel,
        out_shape=out_shape,
        in_specs=in_specs or [whole] * len(args),
        out_specs=out_specs or jax.tree.map(lambda _: whole, out_shape),
        scratch_shapes=list(scratch),
        compiler_params=pltpu.CompilerParams(vmem_limit_bytes=VMEM_LIMIT),
        cost_estimate=pl.CostEstimate(flops=flops, bytes_accessed=1 << 20, transcendentals=0),
        **specs,
    )(*args)


def sensor_layout():
    half = TILE // 2
    row31, row32, col31, col32 = (np.arange(TILE) + TILE * i for i in range(4))
    top, bottom, left, right = (np.arange(2 * TILE) + 2 * TILE * i for i in range(4))
    mid = slice(half, half + TILE)
    groups = [
        (row32, top[mid]),
        (row31, bottom[mid]),
        (np.r_[row32[half:], col32[half:]], np.r_[top[:half], left[:half]]),
        (np.r_[row31[half:], col32[:half]], np.r_[bottom[:half], left[-half:]]),
        (np.r_[row32[:half], col31[half:]], np.r_[top[-half:], right[:half]]),
        (np.r_[row31[:half], col31[:half]], np.r_[bottom[-half:], right[-half:]]),
        (col32, left[mid]),
        (col31, right[mid]),
    ]
    source = np.concatenate([g[0] for g in groups])
    order = np.concatenate([g[1] for g in groups])
    spread = np.zeros((4 * TILE, 8 * TILE), np.float32)
    spread[source, np.arange(8 * TILE)] = 1.0
    return spread, order


def extract_kernel(na, nb, field, own, up, down, row_part, col_part):
    step = pl.program_id(0)
    here, _, cols = field.shape
    sel_row = lax.broadcasted_iota(jnp.int32, (2 * 16, cols), 0)
    sel_col = lax.broadcasted_iota(jnp.int32, (2 * 16, cols), 1)
    side, b_of = sel_row // 16, sel_row % 16
    pick = jnp.where(sel_col == b_of * TILE + (TILE // 2 - 1) + side, 1.0, 0.0).astype(BF16)
    picked = nt_dot(pick, field[...].reshape(here * TILE, cols).astype(BF16))
    r31 = field[:, TILE // 2 - 1, :].astype(BF16).astype(F32)
    r32 = field[:, TILE // 2, :].astype(BF16).astype(F32)
    low = low_lanes((here, LANES))
    base = step * here
    for pair in range(nb // 2):
        lanes = slice(pair * LANES, (pair + 1) * LANES)
        x, y = r31[:, lanes], r32[:, lanes]
        row_part[pl.ds(pl.multiple_of(2 * pair * na + base, 8), here), :] = jnp.where(
            low, x, pltpu.roll(y, TILE, 1)
        )
        row_part[pl.ds(pl.multiple_of((2 * pair + 1) * na + base, 8), here), :] = jnp.where(
            low, pltpu.roll(x, TILE, 1), y
        )
    low = low_lanes((16, LANES))
    for pair in range(here // 2):
        lanes = slice(pair * LANES, (pair + 1) * LANES)
        x, y = picked[0:16, lanes], picked[16:32, lanes]
        even = jnp.where(low, x, pltpu.roll(y, TILE, 1))
        odd = jnp.where(low, pltpu.roll(x, TILE, 1), y)
        col_part[pl.ds(base + 2 * pair, nb, stride=na), :] = even[0:nb]
        col_part[pl.ds(base + 2 * pair + 1, nb, stride=na), :] = odd[0:nb]

    @pl.when(step == pl.num_programs(0) - 1)
    def _():
        all_tiles = jnp.concatenate([row_part[...], col_part[...]], axis=1)
        own[...] = all_tiles.astype(BF16)
        by_b = all_tiles.reshape(nb, na, 4 * TILE)
        up[...] = by_b[:, 0:HALO, :].reshape(nb * HALO, 4 * TILE).astype(BF16)
        down[...] = by_b[:, na - HALO :, :].reshape(nb * HALO, 4 * TILE).astype(BF16)


def columns_kernel(na, nb, own, above, below, c_own, c_above, c_below, both, left, right, c_left, c_right):
    tall = jnp.concatenate(
        [
            above[...].astype(F32).reshape(nb, HALO, 4 * TILE),
            own[...].astype(F32).reshape(nb, na, 4 * TILE),
            below[...].astype(F32).reshape(nb, HALO, 4 * TILE),
        ],
        axis=1,
    )
    height = na + 2 * HALO
    both[...] = tall.reshape(nb * height, 4 * TILE).astype(BF16)
    left[...] = tall[0:HALO].reshape(HALO * height, 4 * TILE).astype(BF16)
    right[...] = tall[nb - HALO :].reshape(HALO * height, 4 * TILE).astype(BF16)
    kx, ky = na // PER_CELL, nb // PER_CELL
    for target, j in ((c_left, 0), (c_right, ky - 1)):
        target[0:1, :] = c_above[j : j + 1, :]
        for i in range(kx):
            target[i + 1 : i + 2, :] = c_own[i * ky + j : i * ky + j + 1, :]
        target[kx + 1 : kx + 2, :] = c_below[j : j + 1, :]


def trunk_kernel(trunk, w_sensor, spread, blocks, sensor_trunk, mean_trunk, w_out, total, rows):
    step = pl.program_id(0)
    width = trunk.shape[1]
    per = width // TILE
    point = lax.broadcasted_iota(jnp.int32, (width, LANES), 0)
    lane = lax.broadcasted_iota(jnp.int32, (width, LANES), 1)
    row = step * per + point // TILE
    side = lane // TILE
    hit = (row == lane % TILE) & (point % TILE == TILE // 2 - 1 + side)
    pick = jnp.concatenate(
        [
            jnp.where(hit, 1.0, 0.0).astype(BF16),
            jnp.full((width, LANES), 1.0 / (TILE * TILE), BF16),
        ],
        axis=1,
    )
    part = dot(trunk[...], pick)

    @pl.when(step == 0)
    def _():
        total[...] = part

    @pl.when(step > 0)
    def _():
        total[...] += part

    half = pl.num_programs(0) // 2

    @pl.when(step == half - 1)
    def _():
        last = trunk[:, width - LANES : width].astype(F32)
        rows[:, 0:LANES] = pltpu.roll(last, TILE, 1)

    @pl.when(step == half)
    def _():
        first = trunk[:, 0:LANES].astype(F32)
        rows[:, LANES : 2 * LANES] = pltpu.roll(first, TILE, 1)

    @pl.when(step == pl.num_programs(0) - 1)
    def _():
        low = low_lanes((trunk.shape[0], LANES))
        row_part = jnp.where(low, rows[:, 0:LANES], rows[:, LANES : 2 * LANES])
        unique = jnp.concatenate([row_part, total[:, 0:LANES]], axis=1).astype(BF16)
        sensor_trunk[...] = dot(unique, spread[...]).astype(BF16)
        mean_trunk[...] = total[:, LANES : 2 * LANES]
        at = 0
        for start, size in blocks:
            w_out[at : at + size, :] = w_sensor[start : start + size, :]
            at += size


def sensor_vectors(sensors, base, count):
    height = HALO * 2 + 16
    low = low_lanes((count, LANES))

    def part(shift, group):
        return sensors[base + shift : base + shift + count, group * LANES : (group + 1) * LANES]

    parts = [
        jnp.where(low, part(-1, 0), part(1, 0)),
        jnp.where(low, part(-height - 1, 1), part(-height + 1, 1)),
        jnp.where(low, part(height - 1, 2), part(height + 1, 2)),
        jnp.where(low, part(-height, 3), part(height, 3)),
    ]
    return jnp.concatenate([p.astype(BF16) for p in parts], axis=1)


def branch(vectors, w1, b1, w2, b2, w3, b3):
    hidden = jnp.tanh(dot(vectors, w1[...]) + b1[...]).astype(BF16)
    hidden = jnp.tanh(dot(hidden, w2[...]) + b2[...]).astype(BF16)
    return (dot(hidden, w3[...]) + b3[...]).astype(BF16)


def send_means(coeffs, pool, mean_trunk, col, cells, payload):
    pooled = dot(pool[...], coeffs)
    means = dot(pooled, mean_trunk[...], precision=lax.Precision.HIGHEST)
    lane = lax.broadcasted_iota(jnp.int32, means.shape, 1)
    cell = lax.broadcasted_iota(jnp.int32, means.shape, 0)
    mine = ((lane - cells * col) & (LANES - 1)) == cell
    line = jnp.sum(jnp.where(mine, means, 0.0), axis=0, keepdims=True)
    payload[...] = jnp.broadcast_to(line, payload.shape)


def corrections(gathered, coarse, n_row, n_col, cells):
    blocks = n_col * cells // LANES
    lane = lax.broadcasted_iota(jnp.int32, (n_col, LANES), 1)
    source = cells * lax.broadcasted_iota(jnp.int32, (n_col, LANES), 0)
    block = (source + ((lane - source) & (LANES - 1))) // LANES
    total = None
    for r in range(n_row):
        values = gathered[r * n_col : (r + 1) * n_col, :]
        for k in range(blocks):
            line = jnp.sum(jnp.where(block == k, values, 0.0), axis=0, keepdims=True)
            at = (r * blocks + k) * LANES
            term = coarse[:, at : at + LANES] * line
            total = term if total is None else total + term
    return jnp.sum(total, axis=1, keepdims=True)


def first_kernel(
    na, nb, cells, mid, left, right, c_own, c_above, c_below, c_left, c_right, spread, w1, b1, w2, b2, w3, b3,
    pool, mean_trunk, coeffs, payload, coarse, sensors,
):
    height = na + 2 * HALO
    side = HALO * height
    wide = nb * height
    sensors[0:8, :] = jnp.zeros((8, 8 * TILE), F32)
    sensors[8 : 8 + side, :] = dot(left[...], spread[...])
    sensors[8 + side : 8 + side + wide, :] = dot(mid[...], spread[...])
    sensors[8 + side + wide : 8 + 2 * side + wide, :] = dot(right[...], spread[...])
    sensors[8 + 2 * side + wide : 16 + 2 * side + wide, :] = jnp.zeros((8, 8 * TILE), F32)
    count = (nb + 2 * HALO - 2) * height
    vectors = sensor_vectors(sensors, 8 + height, count)
    result = branch(vectors, w1, b1, w2, b2, w3, b3)
    coeffs[...] = result
    send_means(result, pool, mean_trunk, lax.axis_index("col"), cells, payload)
    kx, ky = na // PER_CELL, nb // PER_CELL
    for j in range(ky + 2):
        for i in range(kx + 2):
            if j == 0:
                line = c_left[i : i + 1, :]
            elif j == ky + 1:
                line = c_right[i : i + 1, :]
            elif i == 0:
                line = c_above[j - 1 : j, :]
            elif i == kx + 1:
                line = c_below[j - 1 : j, :]
            else:
                at = (i - 1) * ky + j - 1
                line = c_own[at : at + 1, :]
            at = j * height + i * PER_CELL
            coarse[at : at + PER_CELL, :] = jnp.broadcast_to(line, (PER_CELL, line.shape[1]))


def next_kernel(
    k, na, nb, n_row, n_col, cells, gathered, before, sensor_trunk, coarse, w1, b1, w2, b2, w3, b3,
    pool, mean_trunk, coeffs, payload, sensors,
):
    height = na + 2 * HALO
    first = k - 1
    have = nb + 2 * HALO - 2 * first
    rows = have * height
    predicted = dot(before[...], sensor_trunk[...])
    correction = corrections(gathered, coarse, n_row, n_col, cells)
    row, col = lax.axis_index("row"), lax.axis_index("col")
    a_at = row * na - HALO + lax.broadcasted_iota(jnp.int32, (height, 1), 0)
    a_ok = (a_at >= 0) & (a_at < n_row * na)
    sensors[0:8, :] = jnp.zeros((8, 8 * TILE), F32)
    sensors[8 + rows : 16 + rows, :] = jnp.zeros((8, 8 * TILE), F32)
    for b in range(have):
        b_at = col * nb - HALO + first + b
        inside = jnp.where(a_ok & (b_at >= 0) & (b_at < n_col * nb), 1.0, 0.0)
        cell = (first + b) // PER_CELL
        value = predicted[b * height : (b + 1) * height, :] + correction[cell * height : (cell + 1) * height, :]
        sensors[8 + b * height : 8 + (b + 1) * height, :] = jnp.where(inside > 0.5, value, 0.0)
    if k < ITERS:
        vectors = sensor_vectors(sensors, 8 + height, (have - 2) * height)
    else:
        vectors = jnp.concatenate(
            [sensor_vectors(sensors, 8 + (b + 1) * height + HALO, na) for b in range(nb)], axis=0
        )
    result = branch(vectors, w1, b1, w2, b2, w3, b3)
    coeffs[...] = result
    send_means(result, pool, mean_trunk, col, cells, payload)


def field_kernel(na, nb, n_row, n_col, cells, gathered, coarse, coeffs, trunk, out, correction, strip):
    step = pl.program_id(0)
    height = na + 2 * HALO

    @pl.when(step == 0)
    def _():
        found = corrections(gathered, coarse, n_row, n_col, cells)
        correction[...] = jnp.broadcast_to(found, correction.shape)

    values = dot(coeffs[...], trunk[...])
    per = trunk.shape[1] // TILE
    low = low_lanes((8, LANES))
    for pair in range(nb // 2):
        for a in range(0, na, 8):
            cell = 1 + 2 * pair // PER_CELL
            at = cell * height + HALO + a
            add = correction[at : at + 8, :]
            even, odd = (2 * pair * na + a, (2 * pair + 1) * na + a)
            for r in range(0, per, 2):
                lanes = slice(r * TILE, r * TILE + LANES)
                x, y = values[even : even + 8, lanes], values[odd : odd + 8, lanes]
                both = jnp.where(low, x, pltpu.roll(y, TILE, 1)) + add
                strip[pl.ds((pair * na + a) * per + r, 8, stride=per), :] = both
                both = jnp.where(low, pltpu.roll(x, TILE, 1), y) + add
                strip[pl.ds((pair * na + a) * per + r + 1, 8, stride=per), :] = both
        done = strip[pair * na * per : (pair + 1) * na * per, :]
        out[:, :, pair * LANES : (pair + 1) * LANES] = done.reshape(na, per, LANES)


def pool_matrix(na, nb, first, trimmed):
    kx, ky = na // PER_CELL, nb // PER_CELL
    height = na if trimmed else na + 2 * HALO
    skip_a = 0 if trimmed else HALO
    skip_b = HALO - first
    wide = nb + 2 * skip_b
    pool = np.zeros((16, wide * height), np.float32)
    for a in range(na):
        for b in range(nb):
            cell = (a // PER_CELL) * ky + b // PER_CELL
            pool[cell, (b + skip_b) * height + a + skip_a] = 1.0 / PER_CELL**2
    return jnp.asarray(pool, BF16)


def body(
    field_start,
    w_sensor,
    bias_sensor,
    w_middle,
    bias_middle,
    w_latent,
    bias_latent,
    trunk_basis,
    coarse_matrix,
):
    rows_here, cols_here = field_start.shape
    n_row, n_col = lax.axis_size("row"), lax.axis_size("col")
    na, nb = rows_here // TILE, cols_here // TILE
    height = na + 2 * HALO
    kx, ky = na // PER_CELL, nb // PER_CELL
    cells = kx * ky
    devices = n_row * n_col
    latent, points = trunk_basis.shape
    hid = w_sensor.shape[1]
    tile_values, places = 4 * TILE, 8 * TILE
    whole = pl.BlockSpec(memory_space=pltpu.VMEM)
    shape = jax.ShapeDtypeStruct

    def shift(x, axis, forward):
        count = lax.axis_size(axis)
        pairs = [(i, i + 1) if forward else (i + 1, i) for i in range(count - 1)]
        return lax.ppermute(x, axis, pairs)

    spread_np, order = sensor_layout()
    spread = jnp.asarray(spread_np, BF16)
    half = TILE // 2
    blocks = tuple((int(order[i]), half) for i in range(0, places, half))

    steps = 2
    own, up, down = call(
        functools.partial(extract_kernel, na, nb),
        (
            shape((nb * na, tile_values), BF16),
            shape((nb * HALO, tile_values), BF16),
            shape((nb * HALO, tile_values), BF16),
        ),
        field_start.reshape(na, TILE, cols_here),
        grid=(steps,),
        in_specs=[pl.BlockSpec((na // steps, TILE, cols_here), lambda i: (i, 0, 0))],
        out_specs=(
            pl.BlockSpec((nb * na, tile_values), lambda i: (0, 0)),
            pl.BlockSpec((nb * HALO, tile_values), lambda i: (0, 0)),
            pl.BlockSpec((nb * HALO, tile_values), lambda i: (0, 0)),
        ),
        scratch=[pltpu.VMEM((nb * na, LANES), F32)] * 2,
    )
    above, below = shift(down, "row", True), shift(up, "row", False)
    c_above = shift(coarse_matrix[cells - ky :], "row", True)
    c_below = shift(coarse_matrix[:ky], "row", False)

    steps = 4
    width = points // steps
    fixed = lambda i: (0, 0)
    sensor_trunk, mean_trunk, w_first = call(
        lambda t, w, s, *rest: trunk_kernel(t, w, s, blocks, *rest),
        (shape((latent, places), BF16), shape((latent, LANES), F32), shape(w_sensor.shape, BF16)),
        trunk_basis,
        w_sensor,
        spread,
        grid=(steps,),
        in_specs=[
            pl.BlockSpec((latent, width), lambda i: (0, i)),
            pl.BlockSpec(w_sensor.shape, fixed),
            pl.BlockSpec(spread.shape, fixed),
        ],
        out_specs=(
            pl.BlockSpec((latent, places), fixed),
            pl.BlockSpec((latent, LANES), fixed),
            pl.BlockSpec(w_sensor.shape, fixed),
        ),
        scratch=[pltpu.VMEM((latent, 2 * LANES), F32), pltpu.VMEM((latent, 2 * LANES), F32)],
    )

    c_shape = shape((kx + 2, coarse_matrix.shape[1]), F32)
    mid, to_left, to_right, c_to_left, c_to_right = call(
        functools.partial(columns_kernel, na, nb),
        (
            shape((nb * height, tile_values), BF16),
            shape((HALO * height, tile_values), BF16),
            shape((HALO * height, tile_values), BF16),
            c_shape,
            c_shape,
        ),
        own,
        above,
        below,
        coarse_matrix,
        c_above,
        c_below,
    )
    left, right = shift(to_right, "col", True), shift(to_left, "col", False)
    c_left, c_right = shift(c_to_right, "col", True), shift(c_to_left, "col", False)

    net = (
        w_first,
        bias_sensor.reshape(1, hid),
        w_middle,
        bias_middle.reshape(1, hid),
        w_latent,
        bias_latent.reshape(1, latent),
    )
    payload_shape = shape((devices, LANES), F32)
    coarse_shape = shape(((ky + 2) * height, coarse_matrix.shape[1]), F32)
    count = (nb + 2 * HALO - 2) * height
    coeffs, payload, coarse = call(
        functools.partial(first_kernel, na, nb, cells),
        (shape((count, latent), BF16), payload_shape, coarse_shape),
        mid,
        left,
        right,
        coarse_matrix,
        c_above,
        c_below,
        c_left,
        c_right,
        spread,
        *net,
        pool_matrix(na, nb, 1, False),
        mean_trunk,
        scratch=[pltpu.VMEM(((nb + 2 * HALO) * height + 16, places), F32)],
    )
    for k in range(2, ITERS + 1):
        gathered = lax.all_to_all(payload, ("row", "col"), 0, 0, tiled=True)
        have = nb + 2 * HALO - 2 * (k - 1)
        count = nb * na if k == ITERS else (have - 2) * height
        coeffs, payload = call(
            functools.partial(next_kernel, k, na, nb, n_row, n_col, cells),
            (shape((count, latent), BF16), payload_shape),
            gathered,
            coeffs,
            sensor_trunk,
            coarse,
            *net,
            pool_matrix(na, nb, k, k == ITERS),
            mean_trunk,
            scratch=[pltpu.VMEM((have * height + 16, places), F32)],
        )
    gathered = lax.all_to_all(payload, ("row", "col"), 0, 0, tiled=True)
    steps = 8
    out = call(
        functools.partial(field_kernel, na, nb, n_row, n_col, cells),
        shape((na, TILE, cols_here), F32),
        gathered,
        coarse,
        coeffs,
        trunk_basis,
        grid=(steps,),
        in_specs=[
            pl.BlockSpec(payload_shape.shape, fixed),
            pl.BlockSpec(coarse_shape.shape, fixed),
            pl.BlockSpec(coeffs.shape, fixed),
            pl.BlockSpec((latent, points // steps), lambda i: (0, i)),
        ],
        out_specs=pl.BlockSpec((na, TILE // steps, cols_here), lambda i: (0, i, 0)),
        scratch=[
            pltpu.VMEM(((ky + 2) * height, LANES), F32),
            pltpu.VMEM((rows_here * cols_here // steps // LANES, LANES), F32),
        ],
    )
    return out.reshape(rows_here, cols_here)


def solution(mesh):
    placed = (P("row", "col"), P(), P(), P(), P(), P(), P(), P(), P(("row", "col"), None))
    return jax.shard_map(
        body, mesh=mesh, in_specs=placed, out_specs=P("row", "col"), check_vma=False
    )
```

time: 627 us -> 132 us (0.21); the launches traced: 617 us -> 131 us
  blocking collectives: 323 us -> 86.6 us
  local copies, waits for them, and re-layouts: 152 us -> 2.96 us
  other arithmetic: 43.1 us -> 0 us
  waiting for transfers between devices: 37.2 us -> 2.74 us
  matrix products: 26.3 us -> 0 us
  Pallas kernels: 0 us -> 17.2 us
  starting transfers between devices: 34.4 us -> 21.1 us
    unnamed x4 -> x0, blocking collectives: 323 us -> none
    all_to_all x0 -> x4, blocking collectives: none -> 86.6 us  [body(): gathered = lax.all_to_all(payload, ('row', 'col'), 0, 0, tiled=True)]
    reshape x20 -> x0, local copies, waits for them, and re-layouts: 53.3 us -> none  [the longest x8 52.2 us: body(): values.reshape(count_x, count_y, tile, tile).transpose(0, 2, 1, 3)]
    slice x50 -> x1, local copies, waits for them, and re-layouts: 45.1 us -> 1 us  [body(): c_below = shift(coarse_matrix[:ky], 'row', False)]
    ppermute x16 -> x8, waiting for transfers between devices: 37.2 us -> 2.74 us  [shift(): return lax.ppermute(x, axis, pairs)]
    dot_general x12 -> x0, matrix products: 26.3 us -> none  [the longest x4 20.2 us: body(): values = jnp.dot(coeffs, trunk_basis, preferred_element_type=jnp.float32)]
    another operation x4 -> x0, local copies, waits for them, and re-layouts: 25.2 us -> none  [body(): blocks = prediction.reshape(coarse_x, CELL, coarse_y, CELL)]
    pallas_call x0 -> x8, Pallas kernels: none -> 17.2 us  [call(): pl.pallas_call(kernel, out_shape=out_shape, in_specs=in_specs or [whole]...]
  transfers between devices with their start and end apart: 16 -> 8, of which waited for: 12 -> 1; matrix products, arithmetic and copies ran while one was open for 0% -> 0% of each run, Pallas kernels for 0% -> 4%
where the time goes in v1:
time: 132 us; the launch traced here: 131 us
  blocking collectives  86.6 us (66%)
  starting transfers between devices  21.1 us (16%)
  Pallas kernels  17.2 us (13%)
  local copies, waits for them, and re-layouts  2.96 us (2%)
  waiting for transfers between devices  2.74 us (2%)
    all_to_all x4, blocking collectives, body(): gathered = lax.all_to_all(payload, ('row', 'col'), 0, 0, tiled=True)  86.6 us
    ppermute x8, starting transfers between devices, shift(): return lax.ppermute(x, axis, pairs)  21.1 us
    pallas_call x8, Pallas kernels, call(): pl.pallas_call(kernel, out_shape=out_shape, in_specs=in_specs or [whole]...  17.2 us
    ppermute x8, waiting for transfers between devices, shift(): return lax.ppermute(x, axis, pairs)  2.74 us
  transfers between devices with their start and end apart: 8, of which 1 were waited for; matrix products, arithmetic and copies ran while one was open for 0% of the time, Pallas kernels for 4%

profile of v1, /device:TPU:1, one launch (start us, length us, event | category | flops | bytes accessed | tf_op | source)
XLA Modules:
  0.0 131.0 jit_solution(7870119455458848019)
XLA Ops:
  0.0 0.0 copy-start.4
  0.0 1.0 fusion
  1.0 5.1 %collective-permute-start.3 = (f32[3,3072]{1,0:T(4,128)S(1)}, f32[3,3072]{1,0:T(4,128)S(1)}, u32[]{:S(2)}, u32[]{:S(2)}) collective-permute-start(f32[3,3072]{1,0:T(4,128)S(1)} %get-tuple-element.45), channel_id=1, source_target_pairs={{32,0},{64,32},{96,64},{128,96},{160,128},{192,160},{224,192},{33,... | collective-permute-start | bytes 110600 | tf_op jit(solution)/shard_map/ppermute | solution.py:369
  6.2 1.9 %collective-permute-start.2 = (f32[3,3072]{1,0:T(4,128)S(1)}, f32[3,3072]{1,0:T(4,128)S(1)}, u32[]{:S(2)}, u32[]{:S(2)}) collective-permute-start(f32[3,3072]{1,0:T(4,128)S(1)} %get-tuple-element.46), channel_id=1, source_target_pairs={{0,32},{32,64},{64,96},{96,128},{128,160},{160,192},{192,224},{1,3... | collective-permute-start | bytes 110600 | tf_op jit(solution)/shard_map/ppermute | solution.py:369
  8.1 0.0 copy-start.3
  8.1 1.9 %copy-done.3 = f32[1024,768]{1,0:T(8,128)S(1)} copy-done((f32[1024,768]{1,0:T(8,128)S(1)}, f32[1024,768]{1,0:T(8,128)}, u32[]{:S(2)}) %copy-start.3) | copy-done | bytes 3145752
  10.0 0.0 copy-start.5
  10.0 0.0 copy-start.6
  10.0 0.9 shard_map.136
  10.9 0.0 copy-start.1
  10.9 0.0 copy-start.2
  10.9 0.0 copy-start.7
  10.9 0.0 copy-start.8
  10.9 0.0 copy-start.9
  11.0 0.0 copy-start.10
  11.0 2.1 %collective-permute-start = (bf16[48,256]{1,0:T(8,128)(2,1)S(1)}, bf16[48,256]{1,0:T(8,128)(2,1)S(1)}, u32[]{:S(2)}, u32[]{:S(2)}) collective-permute-start(bf16[48,256]{1,0:T(8,128)(2,1)S(1)} %get-tuple-element.26), channel_id=1, source_target_pairs={{0,32},{32,64},{64,96},{96,128},{128,160},{160,192},{192,224},{1,3... | collective-permute-start | bytes 73736 | tf_op jit(solution)/shard_map/ppermute | solution.py:369
  13.0 2.4 %collective-permute-start.1 = (bf16[48,256]{1,0:T(8,128)(2,1)S(1)}, bf16[48,256]{1,0:T(8,128)(2,1)S(1)}, u32[]{:S(2)}, u32[]{:S(2)}) collective-permute-start(bf16[48,256]{1,0:T(8,128)(2,1)S(1)} %get-tuple-element.27), channel_id=1, source_target_pairs={{32,0},{64,32},{96,64},{128,96},{160,128},{192,160},{224,192},{33,... | collective-permute-start | bytes 73736 | tf_op jit(solution)/shard_map/ppermute | solution.py:369
  15.4 0.0 collective-permute-done.above
  15.4 2.7 %collective-permute-done.1.below = bf16[48,256]{1,0:T(8,128)(2,1)S(1)} collective-permute-done((bf16[48,256]{1,0:T(8,128)(2,1)S(1)}, bf16[48,256]{1,0:T(8,128)(2,1)S(1)}, u32[]{:S(2)}, u32[]{:S(2)}) %collective-permute-start.1) | collective-permute-done | bytes 24608 | tf_op jit(solution)/shard_map/ppermute | solution.py:369
  18.2 0.0 collective-permute-done.3.c_below
  18.2 0.0 collective-permute-done.2.c_above
  18.2 0.0 copy-done.4
  18.2 0.1 shard_map.137
  18.3 3.1 %collective-permute-start.6 = (f32[6,3072]{1,0:T(8,128)S(1)}, f32[6,3072]{1,0:T(8,128)S(1)}, u32[]{:S(2)}, u32[]{:S(2)}) collective-permute-start(f32[6,3072]{1,0:T(8,128)S(1)} %get-tuple-element.31), channel_id=1, source_target_pairs={{0,1},{1,2},{2,3},{3,4},{4,5},{5,6},{6,7},{7,8},{8,9},{9,10},{10,1... | collective-permute-start | bytes 221192 | tf_op jit(solution)/shard_map/ppermute | solution.py:369
  21.3 1.3 collective-permute-start.7
  22.6 4.0 %collective-permute-start.4 = (bf16[96,256]{1,0:T(8,128)(2,1)S(1)}, bf16[96,256]{1,0:T(8,128)(2,1)S(1)}, u32[]{:S(2)}, u32[]{:S(2)}) collective-permute-start(bf16[96,256]{1,0:T(8,128)(2,1)S(1)} %get-tuple-element.29), channel_id=1, source_target_pairs={{0,1},{1,2},{2,3},{3,4},{4,5},{5,6},{6,7},{7,8},{8,9},{9,10},{10,1... | collective-permute-start | bytes 147464 | tf_op jit(solution)/shard_map/ppermute | solution.py:369
  26.6 0.0 copy-start.12
  26.6 1.3 collective-permute-start.5
  27.9 0.0 copy-done.5
  27.9 0.0 copy-done.6
  27.9 4.5 %shard_map.138 = (bf16[512,512]{1,0:T(8,128)(2,1)S(1)}, f32[512,128]{1,0:T(8,128)S(1)}, bf16[512,512]{1,0:T(8,128)(2,1)S(1)}) custom-call(bf16[512,4096]{1,0:T(8,128)(2,1)} %trunk.1, bf16[512,512]{1,0:T(8,128)(2,1)S(1)} %copy-done.6, bf16[256,512]{1,0:T(8,128)(2,1)S(1)} %copy-done.5), custom_call_target="tpu_custom_call" | custom-call | bytes 1048576 | tf_op jit(solution)/shard_map/pallas_call | solution.py:39
  32.5 0.0 collective-permute-done.4.left
  32.5 0.0 collective-permute-done.5.right
  32.5 0.0 collective-permute-done.6.c_left
  32.5 0.0 collective-permute-done.7.c_right
  32.5 0.0 copy-done.1
  32.6 0.0 copy-done.2
  32.6 0.0 copy-done.7
  32.6 0.0 copy-done.8
  32.6 0.0 copy-done.9
  32.6 0.0 copy-done.10
  32.6 1.7 %shard_map.139 = (bf16[432,512]{1,0:T(8,128)(2,1)S(1)}, f32[256,128]{1,0:T(8,128)S(1)}, f32[120,3072]{1,0:T(8,128)S(1)}) custom-call(bf16[288,256]{1,0:T(8,128)(2,1)S(1)} %get-tuple-element.28.mid, bf16[96,256]{1,0:T(8,128)(2,1)S(1)} %collective-permute-done.4.left, bf16[96,256]{1,0:T(8,128)(2,1)S(1)} %collective-permute-done.5.right, ...), custom_call_target="tpu_custom_call" | custom-call | bytes 1048576 | tf_op jit(solution)/shard_map/pallas_call | solution.py:39
  34.3 0.0 copy-start.11
  34.3 31.5 %all_to_all.44 = f32[256,1,128]{2,1,0:T(1,128)S(1)} all-to-all(f32[256,1,128]{2,1,0:T(1,128)S(1)} %bitcast.26), channel_id=1, replica_groups=mesh['row'=8,'col'=32] {'row','col'}, dimensions={0} | all-to-all | bytes 262144 | tf_op jit(solution)/shard_map/all_to_all | solution.py:470
  65.8 0.0 copy-done.12
  65.8 1.6 %shard_map.140 = (bf16[384,512]{1,0:T(8,128)(2,1)S(1)}, f32[256,128]{1,0:T(8,128)S(1)}) custom-call(f32[256,128]{1,0:T(8,128)S(1)} %bitcast.24, bf16[432,512]{1,0:T(8,128)(2,1)S(1)} %get-tuple-element.36.before, bf16[512,512]{1,0:T(8,128)(2,1)S(1)} %get-tuple-element.37.sensor_trunk, f32[120,3072]{1,0:T(8,128)S(1)} %get-tuple-element.38.coarse, ...), custom_call_target="tpu_custom_call" | custom-call | bytes 1048576 | tf_op jit(solution)/shard_map/pallas_call | solution.py:39
  67.4 0.0 copy-start.13
  67.4 18.3 %all_to_all.45 = f32[256,1,128]{2,1,0:T(1,128)S(1)} all-to-all(f32[256,1,128]{2,1,0:T(1,128)S(1)} %bitcast.28), channel_id=1, replica_groups=mesh['row'=8,'col'=32] {'row','col'}, dimensions={0} | all-to-all | bytes 262144 | tf_op jit(solution)/shard_map/all_to_all | solution.py:470
  85.7 0.0 copy-done.11
  85.7 1.5 %shard_map.141 = (bf16[336,512]{1,0:T(8,128)(2,1)S(1)}, f32[256,128]{1,0:T(8,128)S(1)}) custom-call(f32[256,128]{1,0:T(8,128)S(1)} %bitcast.25, bf16[384,512]{1,0:T(8,128)(2,1)S(1)} %get-tuple-element.40.before, bf16[512,512]{1,0:T(8,128)(2,1)S(1)} %get-tuple-element.37.sensor_trunk, f32[120,3072]{1,0:T(8,128)S(1)} %get-tuple-element.38.coarse, ...), custom_call_target="tpu_custom_call" | custom-call | bytes 1048576 | tf_op jit(solution)/shard_map/pallas_call | solution.py:39
  87.2 0.0 copy-start
  87.2 18.6 %all_to_all.46 = f32[256,1,128]{2,1,0:T(1,128)S(1)} all-to-all(f32[256,1,128]{2,1,0:T(1,128)S(1)} %bitcast.29), channel_id=1, replica_groups=mesh['row'=8,'col'=32] {'row','col'}, dimensions={0} | all-to-all | bytes 262144 | tf_op jit(solution)/shard_map/all_to_all | solution.py:470
  105.8 0.0 copy-done.13
  105.8 1.3 %shard_map.142 = (bf16[192,512]{1,0:T(8,128)(2,1)S(1)}, f32[256,128]{1,0:T(8,128)S(1)}) custom-call(f32[256,128]{1,0:T(8,128)S(1)} %bitcast.23, bf16[336,512]{1,0:T(8,128)(2,1)S(1)} %get-tuple-element.42.before, bf16[512,512]{1,0:T(8,128)(2,1)S(1)} %get-tuple-element.37.sensor_trunk, f32[120,3072]{1,0:T(8,128)S(1)} %get-tuple-element.38.coarse, ...), custom_call_target="tpu_custom_call" | custom-call | bytes 1048576 | tf_op jit(solution)/shard_map/pallas_call | solution.py:39
  107.2 18.3 %all_to_all.47 = f32[256,1,128]{2,1,0:T(1,128)S(1)} all-to-all(f32[256,1,128]{2,1,0:T(1,128)S(1)} %bitcast.27), channel_id=1, replica_groups=mesh['row'=8,'col'=32] {'row','col'}, dimensions={0} | all-to-all | bytes 262144 | tf_op jit(solution)/shard_map/all_to_all | solution.py:485
  125.5 0.0 copy-done
  125.5 5.5 %shard_map.143 = f32[16,64,768]{2,1,0:T(8,128)} custom-call(f32[256,128]{1,0:T(8,128)S(1)} %bitcast.22, f32[120,3072]{1,0:T(8,128)S(1)} %get-tuple-element.38.coarse, bf16[192,512]{1,0:T(8,128)(2,1)S(1)} %get-tuple-element.44.coeffs, bf16[512,4096]{1,0:T(8,128)(2,1)S(1)} %copy-done), custom_call_target="tpu_custom_call" | custom-call | bytes 1048576 | tf_op jit(solution)/shard_map/pallas_call | solution.py:39
Async XLA Ops:
  0.0 18.2 %copy-start.4 = (f32[12,3072]{1,0:T(8,128)S(1)}, f32[12,3072]{1,0:T(8,128)}, u32[]{:S(2)}) copy-start(f32[12,3072]{1,0:T(8,128)} %c_own.3) | copy-start | bytes 442372
  1.0 17.2 %collective-permute-start.3 = (f32[3,3072]{1,0:T(4,128)S(1)}, f32[3,3072]{1,0:T(4,128)S(1)}, u32[]{:S(2)}, u32[]{:S(2)}) collective-permute-start(f32[3,3072]{1,0:T(4,128)S(1)} %get-tuple-element.45), channel_id=1, source_target_pairs={{32,0},{64,32},{96,64},{128,96},{160,128},{192,160},{224,192},{33,... | collective-permute-start | bytes 110600 | tf_op jit(solution)/shard_map/ppermute | solution.py:369
  6.2 12.0 %collective-permute-start.2 = (f32[3,3072]{1,0:T(4,128)S(1)}, f32[3,3072]{1,0:T(4,128)S(1)}, u32[]{:S(2)}, u32[]{:S(2)}) collective-permute-start(f32[3,3072]{1,0:T(4,128)S(1)} %get-tuple-element.46), channel_id=1, source_target_pairs={{0,32},{32,64},{64,96},{96,128},{128,160},{160,192},{192,224},{1,3... | collective-permute-start | bytes 110600 | tf_op jit(solution)/shard_map/ppermute | solution.py:369
  8.1 1.9 %copy-start.3 = (f32[1024,768]{1,0:T(8,128)S(1)}, f32[1024,768]{1,0:T(8,128)}, u32[]{:S(2)}) copy-start(f32[1024,768]{1,0:T(8,128)} %param.14) | copy-start | bytes 9437188
  10.0 17.9 %copy-start.5 = (bf16[256,512]{1,0:T(8,128)(2,1)S(1)}, bf16[256,512]{1,0:T(8,128)(2,1)}, u32[]{:S(2)}) copy-start(bf16[256,512]{1,0:T(8,128)(2,1)} %constant.10.clone.s.spread) | copy-start | bytes 786436
  10.0 18.0 %copy-start.6 = (bf16[512,512]{1,0:T(8,128)(2,1)S(1)}, bf16[512,512]{1,0:T(8,128)(2,1)}, u32[]{:S(2)}) copy-start(bf16[512,512]{1,0:T(8,128)(2,1)} %w.1) | copy-start | bytes 1572868
  10.9 21.7 %copy-start.1 = (bf16[512,512]{1,0:T(8,128)(2,1)S(1)}, bf16[512,512]{1,0:T(8,128)(2,1)}, u32[]{:S(2)}) copy-start(bf16[512,512]{1,0:T(8,128)(2,1)} %w2.7) | copy-start | bytes 1572868
  10.9 21.6 %copy-start.2 = (bf16[512,512]{1,0:T(8,128)(2,1)S(1)}, bf16[512,512]{1,0:T(8,128)(2,1)}, u32[]{:S(2)}) copy-start(bf16[512,512]{1,0:T(8,128)(2,1)} %w3.7) | copy-start | bytes 1572868
  10.9 21.6 %copy-start.7 = (f32[512]{0:T(512)S(1)}, f32[512]{0:T(512)}, u32[]{:S(2)}) copy-start(f32[512]{0:T(512)} %param.16) | copy-start | bytes 6148
  10.9 21.6 %copy-start.8 = (f32[512]{0:T(512)S(1)}, f32[512]{0:T(512)}, u32[]{:S(2)}) copy-start(f32[512]{0:T(512)} %param.18) | copy-start | bytes 6148
  10.9 21.6 %copy-start.9 = (f32[512]{0:T(512)S(1)}, f32[512]{0:T(512)}, u32[]{:S(2)}) copy-start(f32[512]{0:T(512)} %param.20) | copy-start | bytes 6148
  11.0 21.6 %copy-start.10 = (bf16[16,432]{1,0:T(8,128)(2,1)S(1)}, bf16[16,432]{1,0:T(8,128)(2,1)}, u32[]{:S(2)}) copy-start(bf16[16,432]{1,0:T(8,128)(2,1)} %constant.11.clone.pool) | copy-start | bytes 41476
  11.0 4.5 %collective-permute-start = (bf16[48,256]{1,0:T(8,128)(2,1)S(1)}, bf16[48,256]{1,0:T(8,128)(2,1)S(1)}, u32[]{:S(2)}, u32[]{:S(2)}) collective-permute-start(bf16[48,256]{1,0:T(8,128)(2,1)S(1)} %get-tuple-element.26), channel_id=1, source_target_pairs={{0,32},{32,64},{64,96},{96,128},{128,160},{160,192},{192,224},{1,3... | collective-permute-start | bytes 73736 | tf_op jit(solution)/shard_map/ppermute | solution.py:369
  13.0 5.1 %collective-permute-start.1 = (bf16[48,256]{1,0:T(8,128)(2,1)S(1)}, bf16[48,256]{1,0:T(8,128)(2,1)S(1)}, u32[]{:S(2)}, u32[]{:S(2)}) collective-permute-start(bf16[48,256]{1,0:T(8,128)(2,1)S(1)} %get-tuple-element.27), channel_id=1, source_target_pairs={{32,0},{64,32},{96,64},{128,96},{160,128},{192,160},{224,192},{33,... | collective-permute-start | bytes 73736 | tf_op jit(solution)/shard_map/ppermute | solution.py:369
  18.3 14.3 %collective-permute-start.6 = (f32[6,3072]{1,0:T(8,128)S(1)}, f32[6,3072]{1,0:T(8,128)S(1)}, u32[]{:S(2)}, u32[]{:S(2)}) collective-permute-start(f32[6,3072]{1,0:T(8,128)S(1)} %get-tuple-element.31), channel_id=1, source_target_pairs={{0,1},{1,2},{2,3},{3,4},{4,5},{5,6},{6,7},{7,8},{8,9},{9,10},{10,1... | collective-permute-start | bytes 221192 | tf_op jit(solution)/shard_map/ppermute | solution.py:369
  21.3 11.2 %collective-permute-start.7 = (f32[6,3072]{1,0:T(8,128)S(1)}, f32[6,3072]{1,0:T(8,128)S(1)}, u32[]{:S(2)}, u32[]{:S(2)}) collective-permute-start(f32[6,3072]{1,0:T(8,128)S(1)} %get-tuple-element.32), channel_id=1, source_target_pairs={{1,0},{2,1},{3,2},{4,3},{5,4},{6,5},{7,6},{8,7},{9,8},{10,9},{11,1... | collective-permute-start | bytes 221192 | tf_op jit(solution)/shard_map/ppermute | solution.py:369
  22.6 9.9 %collective-permute-start.4 = (bf16[96,256]{1,0:T(8,128)(2,1)S(1)}, bf16[96,256]{1,0:T(8,128)(2,1)S(1)}, u32[]{:S(2)}, u32[]{:S(2)}) collective-permute-start(bf16[96,256]{1,0:T(8,128)(2,1)S(1)} %get-tuple-element.29), channel_id=1, source_target_pairs={{0,1},{1,2},{2,3},{3,4},{4,5},{5,6},{6,7},{7,8},{8,9},{9,10},{10,1... | collective-permute-start | bytes 147464 | tf_op jit(solution)/shard_map/ppermute | solution.py:369
  26.6 39.2 %copy-start.12 = (bf16[16,384]{1,0:T(8,128)(2,1)S(1)}, bf16[16,384]{1,0:T(8,128)(2,1)}, u32[]{:S(2)}) copy-start(bf16[16,384]{1,0:T(8,128)(2,1)} %constant.12.clone.pool) | copy-start | bytes 36868
  26.6 5.9 %collective-permute-start.5 = (bf16[96,256]{1,0:T(8,128)(2,1)S(1)}, bf16[96,256]{1,0:T(8,128)(2,1)S(1)}, u32[]{:S(2)}, u32[]{:S(2)}) collective-permute-start(bf16[96,256]{1,0:T(8,128)(2,1)S(1)} %get-tuple-element.30), channel_id=1, source_target_pairs={{1,0},{2,1},{3,2},{4,3},{5,4},{6,5},{7,6},{8,7},{9,8},{10,9},{11,1... | collective-permute-start | bytes 147464 | tf_op jit(solution)/shard_map/ppermute | solution.py:369
  34.3 51.4 %copy-start.11 = (bf16[16,336]{1,0:T(8,128)(2,1)S(1)}, bf16[16,336]{1,0:T(8,128)(2,1)}, u32[]{:S(2)}) copy-start(bf16[16,336]{1,0:T(8,128)(2,1)} %constant.13.clone.pool) | copy-start | bytes 32260
  67.4 38.4 %copy-start.13 = (bf16[16,192]{1,0:T(8,128)(2,1)S(1)}, bf16[16,192]{1,0:T(8,128)(2,1)}, u32[]{:S(2)}) copy-start(bf16[16,192]{1,0:T(8,128)(2,1)} %constant.14.clone.pool) | copy-start | bytes 18436
  87.2 38.2 %copy-start = (bf16[512,4096]{1,0:T(8,128)(2,1)S(1)}, bf16[512,4096]{1,0:T(8,128)(2,1)}, u32[]{:S(2)}) copy-start(bf16[512,4096]{1,0:T(8,128)(2,1)} %trunk.1) | copy-start | bytes 12582916

commit v2 on v0

v2 whole, which is shorter than its diff:
```python
import functools

import jax
import jax.numpy as jnp
import numpy as np
from jax import lax
from jax.experimental import pallas as pl
from jax.experimental.pallas import tpu as pltpu
from jax.sharding import PartitionSpec as P

TILE = 64
ITERS = 4
CELL = 256
PER_CELL = CELL // TILE
HALO = ITERS
LANES = 128
F32 = jnp.float32
BF16 = jnp.bfloat16
VMEM_LIMIT = 48 * 1024 * 1024


def dot(a, b, **kw):
    return jnp.dot(a, b, preferred_element_type=F32, **kw)


def nt_dot(a, b):
    return lax.dot_general(a, b, (((1,), (1,)), ((), ())), preferred_element_type=F32)


def low_lanes(shape):
    return lax.broadcasted_iota(jnp.int32, shape, 1) < TILE


def call(kernel, out_shape, *args, grid=(), in_specs=None, out_specs=None, scratch=(), flops=0):
    whole = pl.BlockSpec(memory_space=pltpu.VMEM)
    specs = {}
    if grid:
        specs["grid"] = grid
    return pl.pallas_call(
        kernel,
        out_shape=out_shape,
        in_specs=in_specs or [whole] * len(args),
        out_specs=out_specs or jax.tree.map(lambda _: whole, out_shape),
        scratch_shapes=list(scratch),
        compiler_params=pltpu.CompilerParams(vmem_limit_bytes=VMEM_LIMIT),
        cost_estimate=pl.CostEstimate(flops=flops, bytes_accessed=1 << 20, transcendentals=0),
        **specs,
    )(*args)


def sensor_layout():
    half = TILE // 2
    row31, row32, col31, col32 = (np.arange(TILE) + TILE * i for i in range(4))
    top, bottom, left, right = (np.arange(2 * TILE) + 2 * TILE * i for i in range(4))
    mid = slice(half, half + TILE)
    groups = [
        (row32, top[mid]),
        (row31, bottom[mid]),
        (np.r_[row32[half:], col32[half:]], np.r_[top[:half], left[:half]]),
        (np.r_[row31[half:], col32[:half]], np.r_[bottom[:half], left[-half:]]),
        (np.r_[row32[:half], col31[half:]], np.r_[top[-half:], right[:half]]),
        (np.r_[row31[:half], col31[:half]], np.r_[bottom[-half:], right[-half:]]),
        (col32, left[mid]),
        (col31, right[mid]),
    ]
    source = np.concatenate([g[0] for g in groups])
    order = np.concatenate([g[1] for g in groups])
    spread = np.zeros((4 * TILE, 8 * TILE), np.float32)
    spread[source, np.arange(8 * TILE)] = 1.0
    return spread, order


def extract_kernel(na, nb, ky, field, coarse, own, up, down, cells, arrived, row_part, col_part, packed):
    cols = field.shape[2]
    here = na // arrived.shape[0]
    copies = [
        pltpu.make_async_copy(field.at[pl.ds(i * here, here)], cells.at[pl.ds(i * here, here)], arrived.at[i])
        for i in range(arrived.shape[0])
    ]
    for copy in copies:
        copy.start()
    sel_row = lax.broadcasted_iota(jnp.int32, (2 * 16, cols), 0)
    sel_col = lax.broadcasted_iota(jnp.int32, (2 * 16, cols), 1)
    side, b_of = sel_row // 16, sel_row % 16
    pick = jnp.where(sel_col == b_of * TILE + (TILE // 2 - 1) + side, 1.0, 0.0).astype(BF16)
    low_row, low_col = low_lanes((here, LANES)), low_lanes((16, LANES))
    for i, copy in enumerate(copies):
        copy.wait()
        base = i * here
        chunk = cells[base : base + here]
        picked = nt_dot(pick, chunk.reshape(here * TILE, cols).astype(BF16))
        r31 = cells[base : base + here, TILE // 2 - 1, :]
        r32 = cells[base : base + here, TILE // 2, :]
        for pair in range(nb // 2):
            lanes = slice(pair * LANES, (pair + 1) * LANES)
            x, y = r31[:, lanes], r32[:, lanes]
            even, odd = 2 * pair * na + base, (2 * pair + 1) * na + base
            row_part[even : even + here, :] = jnp.where(low_row, x, pltpu.roll(y, TILE, 1))
            row_part[odd : odd + here, :] = jnp.where(low_row, pltpu.roll(x, TILE, 1), y)
        for pair in range(here // 2):
            lanes = slice(pair * LANES, (pair + 1) * LANES)
            x, y = picked[0:16, lanes], picked[16:32, lanes]
            even = jnp.where(low_col, x, pltpu.roll(y, TILE, 1))
            odd = jnp.where(low_col, pltpu.roll(x, TILE, 1), y)
            col_part[pl.ds(base + 2 * pair, nb, stride=na), :] = even[0:nb]
            col_part[pl.ds(base + 2 * pair + 1, nb, stride=na), :] = odd[0:nb]
    own[:, 0:LANES] = row_part[...].astype(BF16)
    own[:, LANES : 2 * LANES] = col_part[...].astype(BF16)
    for target, first, line in ((up, 0, 0), (down, na - HALO, coarse.shape[0] - ky)):
        packed[...] = jnp.zeros(packed.shape, F32)
        for b in range(nb):
            rows = slice(b * na + first, b * na + first + HALO)
            packed[0:HALO, 2 * b * LANES : (2 * b + 1) * LANES] = row_part[rows, :]
            packed[0:HALO, (2 * b + 1) * LANES : (2 * b + 2) * LANES] = col_part[rows, :]
        packed[HALO : HALO + ky, :] = coarse[line : line + ky, :]
        target[...] = packed[...].astype(BF16)


def columns_kernel(na, nb, own, above, below, coarse, both, left, right, tall, packed):
    height, values = na + 2 * HALO, 4 * TILE
    kx, ky = na // PER_CELL, nb // PER_CELL
    over, under = above[...].astype(F32), below[...].astype(F32)
    for b in range(nb):
        at = b * height
        tall[at : at + HALO, :] = over[0:HALO, b * values : (b + 1) * values]
        tall[at + HALO : at + HALO + na, :] = own[b * na : (b + 1) * na, :].astype(F32)
        tall[at + HALO + na : at + height, :] = under[0:HALO, b * values : (b + 1) * values]
    both[...] = tall[...].astype(BF16)
    packed[...] = jnp.zeros(packed.shape, F32)
    for target, first, j in ((left, 0, 0), (right, nb - HALO, ky - 1)):
        for b in range(HALO):
            for g in range(height // 8):
                lanes = slice((b * (height // 8) + g) * values, (b * (height // 8) + g + 1) * values)
                at = (first + b) * height + 8 * g
                packed[0:8, lanes] = tall[at : at + 8, :]
        packed[8:9, :] = over[HALO + j : HALO + j + 1, :]
        for i in range(kx):
            packed[9 + i : 10 + i, :] = coarse[i * ky + j : i * ky + j + 1, :]
        packed[9 + kx : 10 + kx, :] = under[HALO + j : HALO + j + 1, :]
        target[...] = packed[...].astype(BF16)


def mean_kernel(trunk, mean_trunk):
    share = jnp.full((trunk.shape[1], LANES), 1.0 / (TILE * TILE), BF16)
    mean_trunk[...] = dot(trunk[...], share)


def trunk_sensors(trunk, spread):
    width = 1024
    per = width // TILE
    point = lax.broadcasted_iota(jnp.int32, (width, LANES), 0)
    lane = lax.broadcasted_iota(jnp.int32, (width, LANES), 1)
    column = point % TILE == TILE // 2 - 1 + lane // TILE
    total = None
    for step in range(trunk.shape[1] // width):
        hit = column & (step * per + point // TILE == lane % TILE)
        part = dot(trunk[:, step * width : (step + 1) * width], jnp.where(hit, 1.0, 0.0).astype(BF16))
        total = part if total is None else total + part
    middle = trunk.shape[1] // 2
    row31 = pltpu.roll(trunk[:, middle - LANES : middle].astype(F32), TILE, 1)
    row32 = pltpu.roll(trunk[:, middle : middle + LANES].astype(F32), TILE, 1)
    rows = jnp.where(low_lanes(row31.shape), row31, row32)
    unique = jnp.concatenate([rows, total], axis=1).astype(BF16)
    return dot(unique, spread[...]).astype(BF16)


def sensor_vectors(sensors, base, count):
    height = HALO * 2 + 16
    low = low_lanes((count, LANES))

    def part(shift, group):
        return sensors[base + shift : base + shift + count, group * LANES : (group + 1) * LANES]

    parts = [
        jnp.where(low, part(-1, 0), part(1, 0)),
        jnp.where(low, part(-height - 1, 1), part(-height + 1, 1)),
        jnp.where(low, part(height - 1, 2), part(height + 1, 2)),
        jnp.where(low, part(-height, 3), part(height, 3)),
    ]
    return jnp.concatenate([p.astype(BF16) for p in parts], axis=1)


def branch(vectors, w1, b1, w2, b2, w3, b3):
    hidden = jnp.tanh(dot(vectors, w1[...]) + b1[...]).astype(BF16)
    hidden = jnp.tanh(dot(hidden, w2[...]) + b2[...]).astype(BF16)
    return (dot(hidden, w3[...]) + b3[...]).astype(BF16)


def send_means(coeffs, pool, mean_trunk, col, cells, payload):
    pooled = dot(pool[...], coeffs)
    means = dot(pooled, mean_trunk[...], precision=lax.Precision.HIGHEST)
    lane = lax.broadcasted_iota(jnp.int32, means.shape, 1)
    cell = lax.broadcasted_iota(jnp.int32, means.shape, 0)
    mine = ((lane - cells * col) & (LANES - 1)) == cell
    line = jnp.sum(jnp.where(mine, means, 0.0), axis=0, keepdims=True)
    payload[...] = jnp.broadcast_to(line, payload.shape)


def corrections(gathered, coarse, n_row, n_col, cells):
    blocks = n_col * cells // LANES
    lane = lax.broadcasted_iota(jnp.int32, (n_col, LANES), 1)
    source = cells * lax.broadcasted_iota(jnp.int32, (n_col, LANES), 0)
    block = (source + ((lane - source) & (LANES - 1))) // LANES
    total = None
    for r in range(n_row):
        values = gathered[r * n_col : (r + 1) * n_col, :]
        for k in range(blocks):
            line = jnp.sum(jnp.where(block == k, values, 0.0), axis=0, keepdims=True)
            at = (r * blocks + k) * LANES
            term = coarse[:, at : at + LANES] * line
            total = term if total is None else total + term
    return jnp.sum(total, axis=1, keepdims=True)


def own_vectors(na, nb, sensors, base):
    height = na + 2 * HALO
    return jnp.concatenate(
        [sensor_vectors(sensors, base + b * height + HALO, na) for b in range(nb)], axis=0
    )


def zero_ends(sensors):
    rows = sensors.shape[0]
    sensors[0:8, :] = jnp.zeros((8, sensors.shape[1]), F32)
    sensors[rows - 8 : rows, :] = jnp.zeros((8, sensors.shape[1]), F32)


def first_kernel(
    na, nb, cells, mid, left, right, spread, w1, b1, w2, b2, w3, b3, pool, mean_trunk, payload, sensors, tiles
):
    height, values = na + 2 * HALO, 4 * TILE
    side = HALO * height
    wide = nb * height
    tiles[side : side + wide, :] = mid[...].astype(F32)
    for source, first in ((left, 0), (right, side + wide)):
        lines = source[...].astype(F32)
        for g in range(side // 8):
            tiles[first + 8 * g : first + 8 * (g + 1), :] = lines[0:8, g * values : (g + 1) * values]
    zero_ends(sensors)
    sensors[8 : 8 + 2 * side + wide, :] = dot(tiles[...].astype(BF16), spread[...])
    result = branch(own_vectors(na, nb, sensors, 8 + side), w1, b1, w2, b2, w3, b3)
    send_means(result, pool, mean_trunk, lax.axis_index("col"), cells, payload)


def first_halo_kernel(
    na, nb, sensors, trunk, spread, c_own, above, below, left, right, w1, b1, w2, b2, w3, b3,
    predicted, sensor_trunk, coarse,
):
    height = na + 2 * HALO
    columns = trunk_sensors(trunk, spread)
    sensor_trunk[...] = columns
    vectors = sensor_vectors(sensors, 8 + height, predicted.shape[0])
    predicted[...] = dot(branch(vectors, w1, b1, w2, b2, w3, b3), columns)
    kx, ky = na // PER_CELL, nb // PER_CELL
    edge = [x[...].astype(F32) for x in (above, below, left, right)]
    for j in range(ky + 2):
        for i in range(kx + 2):
            if j == 0:
                line = edge[2][8 + i : 9 + i, :]
            elif j == ky + 1:
                line = edge[3][8 + i : 9 + i, :]
            elif i == 0:
                line = edge[0][HALO + j - 1 : HALO + j, :]
            elif i == kx + 1:
                line = edge[1][HALO + j - 1 : HALO + j, :]
            else:
                at = (i - 1) * ky + j - 1
                line = c_own[at : at + 1, :]
            at = j * height + i * PER_CELL
            coarse[at : at + PER_CELL, :] = jnp.broadcast_to(line, (PER_CELL, line.shape[1]))


def fill_sensors(na, nb, n_row, n_col, first, columns, predicted, correction, sensors):
    height = na + 2 * HALO
    row, col = lax.axis_index("row"), lax.axis_index("col")
    a_at = row * na - HALO + lax.broadcasted_iota(jnp.int32, (height, 1), 0)
    a_ok = (a_at >= 0) & (a_at < n_row * na)
    zero_ends(sensors)
    for i, b in enumerate(columns):
        b_at = col * nb - HALO + b
        inside = jnp.where(a_ok & (b_at >= 0) & (b_at < n_col * nb), 1.0, 0.0)
        cell = b // PER_CELL
        at = (b - first) * height
        value = predicted[at : at + height, :] + correction[cell * height : (cell + 1) * height, 0:1]
        sensors[8 + i * height : 8 + (i + 1) * height, :] = jnp.where(inside > 0.5, value, 0.0)


def next_kernel(
    k, na, nb, n_row, n_col, cells, gathered, predicted, coarse, w1, b1, w2, b2, w3, b3,
    pool, mean_trunk, payload, extra, sensors,
):
    height = na + 2 * HALO
    found = corrections(gathered, coarse, n_row, n_col, cells)
    columns = range(HALO - 1, HALO + nb + 1)
    fill_sensors(na, nb, n_row, n_col, k - 1, columns, predicted, found, sensors)
    result = branch(own_vectors(na, nb, sensors, 8 + height), w1, b1, w2, b2, w3, b3)
    send_means(result, pool, mean_trunk, lax.axis_index("col"), cells, payload)
    if k < ITERS:
        extra[...] = jnp.broadcast_to(found, extra.shape)
    else:
        extra[...] = result


def halo_kernel(
    k, na, nb, n_row, n_col, before, correction, sensor_trunk, w1, b1, w2, b2, w3, b3, predicted, sensors
):
    columns = range(k - 1, nb + 2 * HALO - (k - 1))
    fill_sensors(na, nb, n_row, n_col, k - 1, columns, before, correction, sensors)
    vectors = sensor_vectors(sensors, 8 + na + 2 * HALO, predicted.shape[0])
    predicted[...] = dot(branch(vectors, w1, b1, w2, b2, w3, b3), sensor_trunk[...])


def predict_kernel(na, nb, steps, coeffs, trunk, out, strip):
    width = trunk.shape[1] // steps
    per = width // TILE
    low = low_lanes((8, LANES))
    for step in range(steps):
        values = dot(coeffs[...], trunk[:, step * width : (step + 1) * width])
        for pair in range(nb // 2):
            for a in range(0, na, 8):
                even, odd = (2 * pair * na + a, (2 * pair + 1) * na + a)
                for r in range(0, per, 2):
                    lanes = slice(r * TILE, r * TILE + LANES)
                    x, y = values[even : even + 8, lanes], values[odd : odd + 8, lanes]
                    at = (pair * na + a) * per + r
                    strip[pl.ds(at, 8, stride=per), :] = jnp.where(low, x, pltpu.roll(y, TILE, 1))
                    strip[pl.ds(at + 1, 8, stride=per), :] = jnp.where(low, pltpu.roll(x, TILE, 1), y)
            done = strip[pair * na * per : (pair + 1) * na * per, :].reshape(na, per, LANES)
            out[:, step * per : (step + 1) * per, pair * LANES : (pair + 1) * LANES] = done


def field_kernel(ky, n_row, n_col, cells, gathered, coarse, prediction, out, correction):
    step = pl.program_id(0)

    @pl.when(step == 0)
    def _():
        found = corrections(gathered, coarse, n_row, n_col, cells)
        correction[...] = jnp.broadcast_to(found, correction.shape)

    here = out.shape[0]
    for j in range(ky):
        add = correction[pl.ds(step * ky + j, 1), :].reshape(1, 1, LANES)
        for lane in range(j * CELL, (j + 1) * CELL, LANES):
            lanes = slice(lane, lane + LANES)
            out[:, :, lanes] = prediction[pl.ds(step * here, here), :, lanes] + add


def pool_matrix(na, nb):
    ky = nb // PER_CELL
    pool = np.zeros((16, nb * na), np.float32)
    for a in range(na):
        for b in range(nb):
            pool[(a // PER_CELL) * ky + b // PER_CELL, b * na + a] = 1.0 / PER_CELL**2
    return jnp.asarray(pool, BF16)


def body(
    field_start,
    w_sensor,
    bias_sensor,
    w_middle,
    bias_middle,
    w_latent,
    bias_latent,
    trunk_basis,
    coarse_matrix,
):
    rows_here, cols_here = field_start.shape
    n_row, n_col = lax.axis_size("row"), lax.axis_size("col")
    na, nb = rows_here // TILE, cols_here // TILE
    height = na + 2 * HALO
    kx, ky = na // PER_CELL, nb // PER_CELL
    cells = kx * ky
    devices = n_row * n_col
    latent = trunk_basis.shape[0]
    hid = w_sensor.shape[1]
    tile_values, places = 4 * TILE, 8 * TILE
    total = coarse_matrix.shape[1]
    whole = pl.BlockSpec(memory_space=pltpu.VMEM)
    shape = jax.ShapeDtypeStruct
    part = functools.partial

    def shift(x, axis, forward):
        count = lax.axis_size(axis)
        pairs = [(i, i + 1) if forward else (i + 1, i) for i in range(count - 1)]
        return lax.ppermute(x, axis, pairs)

    def exchange(x):
        return lax.all_to_all(x, ("row", "col"), 0, 0, tiled=True)

    spread_np, order = sensor_layout()
    spread = jnp.asarray(spread_np, BF16)
    half = TILE // 2
    w_first = jnp.concatenate([w_sensor[at : at + half] for at in order[::half].tolist()], axis=0)
    net = (
        w_first,
        bias_sensor.reshape(1, hid),
        w_middle,
        bias_middle.reshape(1, hid),
        w_latent,
        bias_latent.reshape(1, latent),
    )
    pool = pool_matrix(na, nb)

    own, up, down = call(
        part(extract_kernel, na, nb, ky),
        (shape((nb * na, tile_values), BF16), shape((8, total), BF16), shape((8, total), BF16)),
        field_start.reshape(na, TILE, cols_here),
        coarse_matrix,
        in_specs=[pl.BlockSpec(memory_space=pltpu.HBM), whole],
        scratch=[
            pltpu.VMEM((na, TILE, cols_here), F32),
            pltpu.SemaphoreType.DMA((4,)),
            pltpu.VMEM((nb * na, LANES), F32),
            pltpu.VMEM((nb * na, LANES), F32),
            pltpu.VMEM((8, total), F32),
        ],
    )
    above, below = shift(down, "row", True), shift(up, "row", False)
    mean_trunk = call(mean_kernel, shape((latent, LANES), F32), trunk_basis, flops=1 << 28)
    mid, to_left, to_right = call(
        part(columns_kernel, na, nb),
        (shape((nb * height, tile_values), BF16), shape((16, total), BF16), shape((16, total), BF16)),
        own,
        above,
        below,
        coarse_matrix,
        scratch=[pltpu.VMEM((nb * height, tile_values), F32), pltpu.VMEM((16, total), F32)],
    )
    left, right = shift(to_right, "col", True), shift(to_left, "col", False)

    def region(k):
        return (nb + 2 * HALO - 2 * k) * height

    payload_shape = shape((devices, LANES), F32)
    payload, sensors = call(
        part(first_kernel, na, nb, cells),
        (payload_shape, shape((region(0) + 16, places), F32)),
        mid,
        left,
        right,
        spread,
        *net,
        pool,
        mean_trunk,
        scratch=[pltpu.VMEM((region(0), tile_values), F32)],
    )
    gathered = exchange(payload)
    predicted, sensor_trunk, coarse = call(
        part(first_halo_kernel, na, nb),
        (
            shape((region(1), places), F32),
            shape((latent, places), BF16),
            shape(((ky + 2) * height, total), F32),
        ),
        sensors,
        trunk_basis,
        spread,
        coarse_matrix,
        above,
        below,
        left,
        right,
        *net,
        flops=1 << 32,
    )
    for k in range(2, ITERS + 1):
        extra = shape((coarse.shape[0], LANES), F32) if k < ITERS else shape((nb * na, latent), BF16)
        payload, extra = call(
            part(next_kernel, k, na, nb, n_row, n_col, cells),
            (payload_shape, extra),
            gathered,
            predicted,
            coarse,
            *net,
            pool,
            mean_trunk,
            scratch=[pltpu.VMEM(((nb + 2) * height + 16, places), F32)],
        )
        gathered = exchange(payload)
        if k < ITERS:
            predicted = call(
                part(halo_kernel, k, na, nb, n_row, n_col),
                shape((region(k), places), F32),
                predicted,
                extra,
                sensor_trunk,
                *net,
                scratch=[pltpu.VMEM((region(k - 1) + 16, places), F32)],
                flops=1 << 31,
            )
    steps = 8
    prediction = call(
        part(predict_kernel, na, nb, steps),
        shape((na, TILE, cols_here), F32),
        extra,
        trunk_basis,
        scratch=[pltpu.VMEM((rows_here * cols_here // steps // LANES, LANES), F32)],
        flops=1 << 32,
    )
    out = call(
        part(field_kernel, ky, n_row, n_col, cells),
        shape((na, TILE, cols_here), F32),
        gathered,
        coarse_matrix,
        prediction,
        grid=(kx,),
        out_specs=pl.BlockSpec((PER_CELL, TILE, cols_here), lambda i: (i, 0, 0)),
        scratch=[pltpu.VMEM((cells, LANES), F32)],
    )
    return out.reshape(rows_here, cols_here)


def solution(mesh):
    placed = (P("row", "col"), P(), P(), P(), P(), P(), P(), P(), P(("row", "col"), None))
    return jax.shard_map(
        body, mesh=mesh, in_specs=placed, out_specs=P("row", "col"), check_vma=False
    )
```

time: 627 us -> 145 us (0.23); the launches traced: 617 us -> 143 us
  blocking collectives: 323 us -> 0 us
  local copies, waits for them, and re-layouts: 152 us -> 32.7 us
  other arithmetic: 43.1 us -> 0 us
  Pallas kernels: 0 us -> 27.7 us
  matrix products: 26.3 us -> 0 us
  starting transfers between devices: 34.4 us -> 58.1 us
  waiting for transfers between devices: 37.2 us -> 24.4 us
    unnamed x4 -> x0, blocking collectives: 323 us -> none
    reshape x20 -> x0, local copies, waits for them, and re-layouts: 53.3 us -> none  [the longest x8 52.2 us: body(): values.reshape(count_x, count_y, tile, tile).transpose(0, 2, 1, 3)]
    all_to_all x0 -> x4, starting transfers between devices: none -> 47 us  [exchange(): return lax.all_to_all(x, ('row', 'col'), 0, 0, tiled=True)]
    slice x50 -> x0, local copies, waits for them, and re-layouts: 45.1 us -> none  [the longest x4 11.3 us: cycle_values(): bottom_rows = padded[side - 1:side - 1 + count_x * tile:tile, :]]
    ppermute x16 -> x4, waiting for transfers between devices: 37.2 us -> 1.96 us  [shift(): return lax.ppermute(x, axis, pairs)]
    pallas_call x0 -> x12, Pallas kernels: none -> 27.7 us  [call(): pl.pallas_call(kernel, out_shape=out_shape, in_specs=in_specs or [whole]...]
    dot_general x12 -> x0, matrix products: 26.3 us -> none  [the longest x4 20.2 us: body(): values = jnp.dot(coeffs, trunk_basis, preferred_element_type=jnp.float32)]
    another operation x4 -> x0, local copies, waits for them, and re-layouts: 25.2 us -> none  [body(): blocks = prediction.reshape(coarse_x, CELL, coarse_y, CELL)]
  transfers between devices with their start and end apart: 16 -> 8, of which waited for: 12 -> 5; matrix products, arithmetic and copies ran while one was open for 0% -> 7% of each run, Pallas kernels for 0% -> 11%
where the time goes in v2:
time: 145 us; the launch traced here: 143 us
  starting transfers between devices  58.1 us (40%)
  local copies, waits for them, and re-layouts  32.7 us (23%)
  Pallas kernels  27.7 us (19%)
  waiting for transfers between devices  24.4 us (17%)
    all_to_all x4, starting transfers between devices, exchange(): return lax.all_to_all(x, ('row', 'col'), 0, 0, tiled=True)  47 us
    unnamed x85, local copies, waits for them, and re-layouts  31.9 us
    pallas_call x12, Pallas kernels, call(): pl.pallas_call(kernel, out_shape=out_shape, in_specs=in_specs or [whole]...  27.7 us
    all_to_all x4, waiting for transfers between devices, exchange(): return lax.all_to_all(x, ('row', 'col'), 0, 0, tiled=True)  22.4 us
    ppermute x4, starting transfers between devices, shift(): return lax.ppermute(x, axis, pairs)  11.1 us
  transfers between devices with their start and end apart: 8, of which 5 were waited for; matrix products, arithmetic and copies ran while one was open for 7% of the time, Pallas kernels for 11%

profile of v2, /device:TPU:1, one launch (start us, length us, event | category | flops | bytes accessed | tf_op | source)
XLA Modules:
  0.0 143.2 jit_solution(735200726451266882)
XLA Ops:
  0.0 2.0 %copy-done.5 = f32[1024,768]{1,0:T(8,128)S(1)} copy-done((f32[1024,768]{1,0:T(8,128)S(1)}, f32[1024,768]{1,0:T(8,128)}, u32[]{:S(2)}) %copy-start.5) | copy-done | bytes 3145752
  2.0 1.1 copy-done.6
  3.1 1.9 %shard_map.109 = (bf16[192,256]{1,0:T(8,128)(2,1)S(1)}, bf16[8,3072]{1,0:T(8,128)(2,1)S(1)}, bf16[8,3072]{1,0:T(8,128)(2,1)S(1)}) custom-call(f32[16,64,768]{2,1,0:T(8,128)S(1)} %bitcast.21, f32[12,3072]{1,0:T(8,128)S(1)} %copy-done.6), custom_call_target="tpu_custom_call" | custom-call | bytes 1048576 | tf_op jit(solution)/shard_map/pallas_call | solution.py:39
  5.0 0.0 copy-start.2
  5.0 0.0 copy-start.15
  5.0 0.0 copy-start.16
  5.1 4.6 %collective-permute-start = (bf16[8,3072]{1,0:T(8,128)(2,1)S(1)}, bf16[8,3072]{1,0:T(8,128)(2,1)S(1)}, u32[]{:S(2)}, u32[]{:S(2)}) collective-permute-start(bf16[8,3072]{1,0:T(8,128)(2,1)S(1)} %get-tuple-element.23), channel_id=1, source_target_pairs={{0,32},{32,64},{64,96},{96,128},{128,160},{160,192},{192,224},{1,3... | collective-permute-start | bytes 147464 | tf_op jit(solution)/shard_map/ppermute | solution.py:386
  9.7 1.9 %collective-permute-start.1 = (bf16[8,3072]{1,0:T(8,128)(2,1)S(1)}, bf16[8,3072]{1,0:T(8,128)(2,1)S(1)}, u32[]{:S(2)}, u32[]{:S(2)}) collective-permute-start(bf16[8,3072]{1,0:T(8,128)(2,1)S(1)} %get-tuple-element.24), channel_id=1, source_target_pairs={{32,0},{64,32},{96,64},{128,96},{160,128},{192,160},{224,192},{33,... | collective-permute-start | bytes 147464 | tf_op jit(solution)/shard_map/ppermute | solution.py:386
  11.7 0.8 slice_dynamic-update-slice_fusion.3
  12.5 0.8 slice_dynamic-update-slice_fusion.2
  13.4 0.8 slice_dynamic-update-slice_fusion.11
  14.1 0.8 slice_dynamic-update-slice_fusion.10
  14.9 0.8 slice_dynamic-update-slice_fusion.9
  15.7 0.8 slice_dynamic-update-slice_fusion.8
  16.4 0.8 slice_dynamic-update-slice_fusion.7
  17.2 0.8 slice_dynamic-update-slice_fusion.6
  17.9 0.8 slice_dynamic-update-slice_fusion.5
  18.7 0.8 slice_dynamic-update-slice_fusion.4
  19.5 0.8 slice_dynamic-update-slice_fusion.1
  20.3 0.1 shard_map.110
  20.4 3.2 %collective-permute-start.2 = (bf16[16,3072]{1,0:T(8,128)(2,1)S(1)}, bf16[16,3072]{1,0:T(8,128)(2,1)S(1)}, u32[]{:S(2)}, u32[]{:S(2)}) collective-permute-start(bf16[16,3072]{1,0:T(8,128)(2,1)S(1)} %get-tuple-element.26), channel_id=1, source_target_pairs={{0,1},{1,2},{2,3},{3,4},{4,5},{5,6},{6,7},{7,8},{8,9},{9,10},{10,1... | collective-permute-start | bytes 294920 | tf_op jit(solution)/shard_map/ppermute | solution.py:386
  23.7 1.3 collective-permute-start.3
  25.0 0.8 slice_dynamic-update-slice_fusion.w1
  25.8 1.2 shard_map.111.mean_trunk
  27.1 1.9 %collective-permute-done.3.right = bf16[16,3072]{1,0:T(8,128)(2,1)S(1)} collective-permute-done((bf16[16,3072]{1,0:T(8,128)(2,1)S(1)}, bf16[16,3072]{1,0:T(8,128)(2,1)S(1)}, u32[]{:S(2)}, u32[]{:S(2)}) %collective-permute-start.3) | collective-permute-done | bytes 98336 | tf_op jit(solution)/shard_map/ppermute | solution.py:386
  29.1 1.9 %shard_map.112 = (f32[256,128]{1,0:T(8,128)}, f32[496,512]{1,0:T(8,128)S(1)}) custom-call(bf16[288,256]{1,0:T(8,128)(2,1)S(1)} %get-tuple-element.25.mid, bf16[16,3072]{1,0:T(8,128)(2,1)S(1)} %collective-permute-done.2.left, bf16[16,3072]{1,0:T(8,128)(2,1)S(1)} %collective-permute-done.3.right, bf16[256,512]{1,0:T(8,128)(2,1)S(1)} %copy-done.15, ...), custom_call_target="tpu_custom_call" | custom-call | bytes 1048576 | tf_op jit(solution)/shard_map/pallas_call | solution.py:39
  31.0 1.0 copy-done.26
  31.9 18.0 %all-to-all-start = ((f32[256,1,128]{2,1,0:T(1,128)}), f32[256,1,128]{2,1,0:T(1,128)S(1)}, u32[]{:S(2)}, u32[]{:S(2)}) async-start(f32[256,1,128]{2,1,0:T(1,128)} %bitcast.5), calls=%async_computation | async-start | bytes 262144 | tf_op jit(solution)/shard_map/all_to_all | solution.py:389
  49.9 0.8 copy-done.20
  50.7 0.8 copy-done.22
  51.5 1.2 copy-done.27
  52.7 7.9 %shard_map.113 = (f32[432,512]{1,0:T(8,128)S(1)}, bf16[512,512]{1,0:T(8,128)(2,1)S(1)}, f32[120,3072]{1,0:T(8,128)}) custom-call(f32[496,512]{1,0:T(8,128)S(1)} %copy-done.27, bf16[512,4096]{1,0:T(8,128)(2,1)} %trunk.5, bf16[256,512]{1,0:T(8,128)(2,1)S(1)} %copy-done.15, f32[12,3072]{1,0:T(8,128)S(1)} %copy-done.7, bf16[8,3072]{1,0:T(8,128)(2,1)S(1)} %copy-done.20, ...), custom_call_target="tpu_custom_call" | custom-call | flops 4294967296 | bytes 1048576 | tf_op jit(solution)/shard_map/pallas_call | solution.py:39
  60.6 0.8 copy-done.34
  61.4 1.1 all-to-all-done
  62.5 1.4 copy-done
  63.9 1.9 %shard_map.114 = (f32[256,128]{1,0:T(8,128)}, f32[120,128]{1,0:T(8,128)S(1)}) custom-call(f32[256,128]{1,0:T(8,128)S(1)} %bitcast.22, f32[432,512]{1,0:T(8,128)S(1)} %get-tuple-element.30.predicted.before, f32[120,3072]{1,0:T(8,128)S(1)} %copy-done, bf16[512,512]{1,0:T(8,128)(2,1)S(1)} %slice_dynamic-update-slice_fusion.w1, f32[1,512]{1,0:T(1,128)S(1)} %bitcast.28, ...), custom_call_target="tpu_custom_call" | custom-call | bytes 1048576 | tf_op jit(solution)/shard_map/pallas_call | solution.py:39
  65.8 0.6 copy-done.30
  66.5 14.0 %all-to-all-start.1 = ((f32[256,1,128]{2,1,0:T(1,128)}), f32[256,1,128]{2,1,0:T(1,128)}, u32[]{:S(2)}, u32[]{:S(2)}) async-start(f32[256,1,128]{2,1,0:T(1,128)} %bitcast.8), calls=%async_computation.1 | async-start | bytes 262144 | tf_op jit(solution)/shard_map/all_to_all | solution.py:389
  80.4 1.2 copy-done.9
  81.6 0.8 copy-done.31
  82.4 1.0 copy-done.35
  83.5 1.2 shard_map.115.predicted.before
  84.7 0.9 copy-done.10
  85.6 6.6 %all-to-all-done.1 = f32[256,1,128]{2,1,0:T(1,128)} async-done(((f32[256,1,128]{2,1,0:T(1,128)}), f32[256,1,128]{2,1,0:T(1,128)}, u32[]{:S(2)}, u32[]{:S(2)}) %all-to-all-start.1) | async-done | bytes 131104 | tf_op jit(solution)/shard_map/all_to_all | solution.py:389
  92.2 1.1 copy-done.11
  93.4 2.2 %shard_map.116 = (f32[256,128]{1,0:T(8,128)S(1)}, f32[120,128]{1,0:T(8,128)S(1)}) custom-call(f32[256,128]{1,0:T(8,128)} %bitcast.9.gathered, f32[384,512]{1,0:T(8,128)S(1)} %copy-done.11, f32[120,3072]{1,0:T(8,128)S(1)} %copy-done.1, bf16[512,512]{1,0:T(8,128)(2,1)S(1)} %slice_dynamic-update-slice_fusion.w1, f32[1,512]{1,0:T(1,128)S(1)} %bitcast.30, ...), custom_call_target="tpu_custom_call" | custom-call | bytes 1048576 | tf_op jit(solution)/shard_map/pallas_call | solution.py:39
  95.6 0.6 copy-done.32
  96.2 0.6 copy-done.18
  96.8 8.1 %all-to-all-start.2 = ((f32[256,1,128]{2,1,0:T(1,128)}), f32[256,1,128]{2,1,0:T(1,128)}, u32[]{:S(2)}, u32[]{:S(2)}) async-start(f32[256,1,128]{2,1,0:T(1,128)} %bitcast.25), calls=%async_computation.2 | async-start | bytes 262144 | tf_op jit(solution)/shard_map/all_to_all | solution.py:389
  105.0 1.1 copy-done.12
  106.1 0.8 copy-done.33
  106.9 1.0 copy-done.36
  108.0 1.2 shard_map.117.predicted
  109.2 0.8 copy-done.13
  110.0 6.8 %all-to-all-done.2 = f32[256,1,128]{2,1,0:T(1,128)} async-done(((f32[256,1,128]{2,1,0:T(1,128)}), f32[256,1,128]{2,1,0:T(1,128)}, u32[]{:S(2)}, u32[]{:S(2)}) %all-to-all-start.2) | async-done | bytes 131104 | tf_op jit(solution)/shard_map/all_to_all | solution.py:389
  116.8 1.1 copy-done.14
  117.9 2.2 %shard_map.118 = (f32[256,128]{1,0:T(8,128)S(1)}, bf16[192,512]{1,0:T(8,128)(2,1)S(1)}) custom-call(f32[256,128]{1,0:T(8,128)} %bitcast.12.gathered, f32[336,512]{1,0:T(8,128)S(1)} %copy-done.14, f32[120,3072]{1,0:T(8,128)S(1)} %copy-done.1, bf16[512,512]{1,0:T(8,128)(2,1)S(1)} %slice_dynamic-update-slice_fusion.w1, f32[1,512]{1,0:T(1,128)S(1)} %bitcast.32, ...), custom_call_target="tpu_custom_call" | custom-call | bytes 1048576 | tf_op jit(solution)/shard_map/pallas_call | solution.py:39
  120.1 0.7 copy-done.28
  120.7 0.7 copy-done.17
  121.4 6.9 %all-to-all-start.3 = ((f32[256,1,128]{2,1,0:T(1,128)}), f32[256,1,128]{2,1,0:T(1,128)S(1)}, u32[]{:S(2)}, u32[]{:S(2)}) async-start(f32[256,1,128]{2,1,0:T(1,128)} %bitcast.24), calls=%async_computation.3 | async-start | bytes 262144 | tf_op jit(solution)/shard_map/all_to_all | solution.py:389
  128.3 0.9 copy-done.29
  129.3 3.7 %shard_map.119.prediction = f32[16,64,768]{2,1,0:T(8,128)S(1)} custom-call(bf16[192,512]{1,0:T(8,128)(2,1)S(1)} %copy-done.29, bf16[512,4096]{1,0:T(8,128)(2,1)} %trunk.5), custom_call_target="tpu_custom_call" | custom-call | flops 4294967296 | bytes 1048576 | tf_op jit(solution)/shard_map/pallas_call | solution.py:39
  133.0 7.9 %all-to-all-done.3 = f32[256,1,128]{2,1,0:T(1,128)S(1)} async-done(((f32[256,1,128]{2,1,0:T(1,128)}), f32[256,1,128]{2,1,0:T(1,128)S(1)}, u32[]{:S(2)}, u32[]{:S(2)}) %all-to-all-start.3) | async-done | bytes 131104 | tf_op jit(solution)/shard_map/all_to_all | solution.py:389
  140.9 2.3 %shard_map.120 = f32[16,64,768]{2,1,0:T(8,128)} custom-call(f32[256,128]{1,0:T(8,128)S(1)} %bitcast.23, f32[12,3072]{1,0:T(8,128)S(1)} %copy-done.7, f32[16,64,768]{2,1,0:T(8,128)S(1)} %shard_map.119.prediction), custom_call_target="tpu_custom_call" | custom-call | bytes 1048576 | tf_op jit(solution)/shard_map/pallas_call | solution.py:39
  (50 shorter events, 0.1 us)
Async XLA Ops:
  0.0 25.8 %copy-start.4 = (bf16[512,4096]{1,0:T(8,128)(2,1)S(1)}, bf16[512,4096]{1,0:T(8,128)(2,1)}, u32[]{:S(2)}) copy-start(bf16[512,4096]{1,0:T(8,128)(2,1)} %trunk.5) | copy-start | bytes 12582916
  0.0 2.0 %copy-start.5 = (f32[1024,768]{1,0:T(8,128)S(1)}, f32[1024,768]{1,0:T(8,128)}, u32[]{:S(2)}) copy-start(f32[1024,768]{1,0:T(8,128)} %param.11) | copy-start | bytes 9437188
  2.0 1.1 copy-start.6
  5.0 24.0 %copy-start.2 = (bf16[512,512]{1,0:T(8,128)(2,1)S(1)}, bf16[512,512]{1,0:T(8,128)(2,1)}, u32[]{:S(2)}) copy-start(bf16[512,512]{1,0:T(8,128)(2,1)} %w2.13) | copy-start | bytes 1572868
  5.0 24.0 %copy-start.3 = (bf16[512,512]{1,0:T(8,128)(2,1)S(1)}, bf16[512,512]{1,0:T(8,128)(2,1)}, u32[]{:S(2)}) copy-start(bf16[512,512]{1,0:T(8,128)(2,1)} %w3.13) | copy-start | bytes 1572868
  5.0 24.0 %copy-start.15 = (bf16[256,512]{1,0:T(8,128)(2,1)S(1)}, bf16[256,512]{1,0:T(8,128)(2,1)}, u32[]{:S(2)}) copy-start(bf16[256,512]{1,0:T(8,128)(2,1)} %constant.4.clone.spread) | copy-start | bytes 786436
  5.0 24.0 %copy-start.16 = (bf16[16,192]{1,0:T(8,128)(2,1)S(1)}, bf16[16,192]{1,0:T(8,128)(2,1)}, u32[]{:S(2)}) copy-start(bf16[16,192]{1,0:T(8,128)(2,1)} %constant.5.clone.pool) | copy-start | bytes 18436
  5.1 24.0 %copy-start.23 = (f32[512]{0:T(512)S(1)}, f32[512]{0:T(512)}, u32[]{:S(2)}) copy-start(f32[512]{0:T(512)} %param.13) | copy-start | bytes 6148
  5.1 24.0 %copy-start.24 = (f32[512]{0:T(512)S(1)}, f32[512]{0:T(512)}, u32[]{:S(2)}) copy-start(f32[512]{0:T(512)} %param.15) | copy-start | bytes 6148
  5.1 24.0 %copy-start.25 = (f32[512]{0:T(512)S(1)}, f32[512]{0:T(512)}, u32[]{:S(2)}) copy-start(f32[512]{0:T(512)} %param.17) | copy-start | bytes 6148
  5.1 15.2 %collective-permute-start = (bf16[8,3072]{1,0:T(8,128)(2,1)S(1)}, bf16[8,3072]{1,0:T(8,128)(2,1)S(1)}, u32[]{:S(2)}, u32[]{:S(2)}) collective-permute-start(bf16[8,3072]{1,0:T(8,128)(2,1)S(1)} %get-tuple-element.23), channel_id=1, source_target_pairs={{0,32},{32,64},{64,96},{96,128},{128,160},{160,192},{192,224},{1,3... | collective-permute-start | bytes 147464 | tf_op jit(solution)/shard_map/ppermute | solution.py:386
  9.7 10.6 %collective-permute-start.1 = (bf16[8,3072]{1,0:T(8,128)(2,1)S(1)}, bf16[8,3072]{1,0:T(8,128)(2,1)S(1)}, u32[]{:S(2)}, u32[]{:S(2)}) collective-permute-start(bf16[8,3072]{1,0:T(8,128)(2,1)S(1)} %get-tuple-element.24), channel_id=1, source_target_pairs={{32,0},{64,32},{96,64},{128,96},{160,128},{192,160},{224,192},{33,... | collective-permute-start | bytes 147464 | tf_op jit(solution)/shard_map/ppermute | solution.py:386
  20.3 8.7 %copy-start.19 = (bf16[8,3072]{1,0:T(8,128)(2,1)}, bf16[8,3072]{1,0:T(8,128)(2,1)S(1)}, u32[]{:S(2)}) copy-start(bf16[8,3072]{1,0:T(8,128)(2,1)S(1)} %collective-permute-done.above) | copy-start | bytes 147460
  20.3 8.7 %copy-start.21 = (bf16[8,3072]{1,0:T(8,128)(2,1)}, bf16[8,3072]{1,0:T(8,128)(2,1)S(1)}, u32[]{:S(2)}) copy-start(bf16[8,3072]{1,0:T(8,128)(2,1)S(1)} %collective-permute-done.1.below) | copy-start | bytes 147460
  20.4 6.6 %collective-permute-start.2 = (bf16[16,3072]{1,0:T(8,128)(2,1)S(1)}, bf16[16,3072]{1,0:T(8,128)(2,1)S(1)}, u32[]{:S(2)}, u32[]{:S(2)}) collective-permute-start(bf16[16,3072]{1,0:T(8,128)(2,1)S(1)} %get-tuple-element.26), channel_id=1, source_target_pairs={{0,1},{1,2},{2,3},{3,4},{4,5},{5,6},{6,7},{7,8},{8,9},{9,10},{10,1... | collective-permute-start | bytes 294920 | tf_op jit(solution)/shard_map/ppermute | solution.py:386
  23.7 5.4 %collective-permute-start.3 = (bf16[16,3072]{1,0:T(8,128)(2,1)S(1)}, bf16[16,3072]{1,0:T(8,128)(2,1)S(1)}, u32[]{:S(2)}, u32[]{:S(2)}) collective-permute-start(bf16[16,3072]{1,0:T(8,128)(2,1)S(1)} %get-tuple-element.27), channel_id=1, source_target_pairs={{1,0},{2,1},{3,2},{4,3},{5,4},{6,5},{7,6},{8,7},{9,8},{10,9},{11,1... | collective-permute-start | bytes 294920 | tf_op jit(solution)/shard_map/ppermute | solution.py:386
  25.8 24.1 %copy-start.7 = (f32[12,3072]{1,0:T(8,128)S(1)}, f32[12,3072]{1,0:T(8,128)}, u32[]{:S(2)}) copy-start(f32[12,3072]{1,0:T(8,128)} %coarse.5) | copy-start | bytes 442372
  31.0 1.0 copy-start.26
  31.9 30.6 %all-to-all-start = ((f32[256,1,128]{2,1,0:T(1,128)}), f32[256,1,128]{2,1,0:T(1,128)S(1)}, u32[]{:S(2)}, u32[]{:S(2)}) async-start(f32[256,1,128]{2,1,0:T(1,128)} %bitcast.5), calls=%async_computation | async-start | bytes 262144 | tf_op jit(solution)/shard_map/all_to_all | solution.py:389
  49.9 0.8 copy-start.20
  50.7 0.8 copy-start.22
  51.5 1.2 copy-start.27
  60.6 0.8 copy-start.34
  61.4 19.0 %copy-start.8 = (f32[432,512]{1,0:T(8,128)}, f32[432,512]{1,0:T(8,128)S(1)}, u32[]{:S(2)}) copy-start(f32[432,512]{1,0:T(8,128)S(1)} %get-tuple-element.30.predicted.before) | copy-start | bytes 2654212
  62.5 1.4 copy-start
  65.8 0.6 copy-start.30
  66.5 25.8 %all-to-all-start.1 = ((f32[256,1,128]{2,1,0:T(1,128)}), f32[256,1,128]{2,1,0:T(1,128)}, u32[]{:S(2)}, u32[]{:S(2)}) async-start(f32[256,1,128]{2,1,0:T(1,128)} %bitcast.8), calls=%async_computation.1 | async-start | bytes 262144 | tf_op jit(solution)/shard_map/all_to_all | solution.py:389
  80.4 1.2 copy-start.9
  81.6 0.8 copy-start.31
  82.4 1.0 copy-start.35
  83.5 8.8 %copy-start.1 = (f32[120,3072]{1,0:T(8,128)S(1)}, f32[120,3072]{1,0:T(8,128)}, u32[]{:S(2)}) copy-start(f32[120,3072]{1,0:T(8,128)} %get-tuple-element.31.coarse) | copy-start | bytes 4423684
  84.7 0.9 copy-start.10
  92.2 1.1 copy-start.11
  95.5 0.6 copy-start.32
  96.2 0.6 copy-start.18
  96.8 20.0 %all-to-all-start.2 = ((f32[256,1,128]{2,1,0:T(1,128)}), f32[256,1,128]{2,1,0:T(1,128)}, u32[]{:S(2)}, u32[]{:S(2)}) async-start(f32[256,1,128]{2,1,0:T(1,128)} %bitcast.25), calls=%async_computation.2 | async-start | bytes 262144 | tf_op jit(solution)/shard_map/all_to_all | solution.py:389
  105.0 1.1 copy-start.12
  106.1 0.8 copy-start.33
  106.9 1.0 copy-start.36
  109.1 0.8 copy-start.13
  116.8 1.1 copy-start.14
  120.1 0.7 copy-start.28
  120.7 0.7 copy-start.17
  121.4 19.5 %all-to-all-start.3 = ((f32[256,1,128]{2,1,0:T(1,128)}), f32[256,1,128]{2,1,0:T(1,128)S(1)}, u32[]{:S(2)}, u32[]{:S(2)}) async-start(f32[256,1,128]{2,1,0:T(1,128)} %bitcast.24), calls=%async_computation.3 | async-start | bytes 262144 | tf_op jit(solution)/shard_map/all_to_all | solution.py:389
  128.3 0.9 copy-start.29

commit v3 on v2

--- a/solution.py
+++ b/solution.py
@@ -17,6 +17,7 @@
 F32 = jnp.float32
 BF16 = jnp.bfloat16
 VMEM_LIMIT = 48 * 1024 * 1024
+VMEM_LIMIT_FIRST = 52 * 1024 * 1024
 
 
 def dot(a, b, **kw):
@@ -31,7 +32,7 @@
     return lax.broadcasted_iota(jnp.int32, shape, 1) < TILE
 
 
-def call(kernel, out_shape, *args, grid=(), in_specs=None, out_specs=None, scratch=(), flops=0):
+def call(kernel, out_shape, *args, grid=(), in_specs=None, out_specs=None, scratch=(), flops=0, vmem=VMEM_LIMIT):
     whole = pl.BlockSpec(memory_space=pltpu.VMEM)
     specs = {}
     if grid:
@@ -42,7 +43,7 @@
         in_specs=in_specs or [whole] * len(args),
         out_specs=out_specs or jax.tree.map(lambda _: whole, out_shape),
         scratch_shapes=list(scratch),
-        compiler_params=pltpu.CompilerParams(vmem_limit_bytes=VMEM_LIMIT),
+        compiler_params=pltpu.CompilerParams(vmem_limit_bytes=vmem),
         cost_estimate=pl.CostEstimate(flops=flops, bytes_accessed=1 << 20, transcendentals=0),
         **specs,
     )(*args)
@@ -70,7 +71,9 @@
     return spread, order
 
 
-def extract_kernel(na, nb, ky, field, coarse, own, up, down, cells, arrived, row_part, col_part, packed):
+def extract_kernel(
+    na, nb, ky, field, coarse_hbm, own, up, down, cells, coarse, arrived, coarse_arrived, row_part, col_part, packed
+):
     cols = field.shape[2]
     here = na // arrived.shape[0]
     copies = [
@@ -79,6 +82,8 @@
     ]
     for copy in copies:
         copy.start()
+    coarse_copy = pltpu.make_async_copy(coarse_hbm, coarse, coarse_arrived)
+    coarse_copy.start()
     sel_row = lax.broadcasted_iota(jnp.int32, (2 * 16, cols), 0)
     sel_col = lax.broadcasted_iota(jnp.int32, (2 * 16, cols), 1)
     side, b_of = sel_row // 16, sel_row % 16
@@ -106,6 +111,7 @@
             col_part[pl.ds(base + 2 * pair + 1, nb, stride=na), :] = odd[0:nb]
     own[:, 0:LANES] = row_part[...].astype(BF16)
     own[:, LANES : 2 * LANES] = col_part[...].astype(BF16)
+    coarse_copy.wait()
     for target, first, line in ((up, 0, 0), (down, na - HALO, coarse.shape[0] - ky)):
         packed[...] = jnp.zeros(packed.shape, F32)
         for b in range(nb):
@@ -140,28 +146,40 @@
         target[...] = packed[...].astype(BF16)
 
 
-def mean_kernel(trunk, mean_trunk):
-    share = jnp.full((trunk.shape[1], LANES), 1.0 / (TILE * TILE), BF16)
-    mean_trunk[...] = dot(trunk[...], share)
-
-
-def trunk_sensors(trunk, spread):
-    width = 1024
+def trunk_kernel(blocks, trunk_hbm, w_sensor, spread, sensor_trunk, mean_trunk, w_out, trunk, arrived):
+    steps = arrived.shape[0]
+    width = trunk.shape[1] // steps
     per = width // TILE
+    copies = [
+        pltpu.make_async_copy(
+            trunk_hbm.at[:, pl.ds(i * width, width)], trunk.at[:, pl.ds(i * width, width)], arrived.at[i]
+        )
+        for i in range(steps)
+    ]
+    for copy in copies:
+        copy.start()
+    at = 0
+    for start, size in blocks:
+        w_out[at : at + size, :] = w_sensor[start : start + size, :]
+        at += size
     point = lax.broadcasted_iota(jnp.int32, (width, LANES), 0)
     lane = lax.broadcasted_iota(jnp.int32, (width, LANES), 1)
     column = point % TILE == TILE // 2 - 1 + lane // TILE
+    away = jnp.where(column, lane % TILE - point // TILE, -1)
+    share = jnp.full((width, LANES), 1.0 / (TILE * TILE), BF16)
     total = None
-    for step in range(trunk.shape[1] // width):
-        hit = column & (step * per + point // TILE == lane % TILE)
-        part = dot(trunk[:, step * width : (step + 1) * width], jnp.where(hit, 1.0, 0.0).astype(BF16))
+    for step, copy in enumerate(copies):
+        copy.wait()
+        pick = jnp.where(away == step * per, 1.0, 0.0).astype(BF16)
+        part = dot(trunk[:, step * width : (step + 1) * width], jnp.concatenate([pick, share], axis=1))
         total = part if total is None else total + part
     middle = trunk.shape[1] // 2
     row31 = pltpu.roll(trunk[:, middle - LANES : middle].astype(F32), TILE, 1)
     row32 = pltpu.roll(trunk[:, middle : middle + LANES].astype(F32), TILE, 1)
     rows = jnp.where(low_lanes(row31.shape), row31, row32)
-    unique = jnp.concatenate([rows, total], axis=1).astype(BF16)
-    return dot(unique, spread[...]).astype(BF16)
+    unique = jnp.concatenate([rows, total[:, 0:LANES]], axis=1).astype(BF16)
+    sensor_trunk[...] = dot(unique, spread[...]).astype(BF16)
+    mean_trunk[...] = total[:, LANES : 2 * LANES]
 
 
 def sensor_vectors(sensors, base, count):
@@ -226,131 +244,121 @@
 
 
 def first_kernel(
-    na, nb, cells, mid, left, right, spread, w1, b1, w2, b2, w3, b3, pool, mean_trunk, payload, sensors, tiles
+    na, nb, cells, mid, left, right, above, below, c_own, spread, w1, b1, w2, b2, w3, b3, pool, mean_trunk,
+    coeffs, payload, coarse, sensors, tiles,
 ):
     height, values = na + 2 * HALO, 4 * TILE
     side = HALO * height
     wide = nb * height
     tiles[side : side + wide, :] = mid[...].astype(F32)
-    for source, first in ((left, 0), (right, side + wide)):
-        lines = source[...].astype(F32)
+    edge = [x[...].astype(F32) for x in (above, below, left, right)]
+    for lines, first in ((edge[2], 0), (edge[3], side + wide)):
         for g in range(side // 8):
             tiles[first + 8 * g : first + 8 * (g + 1), :] = lines[0:8, g * values : (g + 1) * values]
     zero_ends(sensors)
     sensors[8 : 8 + 2 * side + wide, :] = dot(tiles[...].astype(BF16), spread[...])
-    result = branch(own_vectors(na, nb, sensors, 8 + side), w1, b1, w2, b2, w3, b3)
+    vectors = sensor_vectors(sensors, 8 + height, coeffs.shape[0])
+    result = branch(vectors, w1, b1, w2, b2, w3, b3)
+    coeffs[...] = result
     send_means(result, pool, mean_trunk, lax.axis_index("col"), cells, payload)
-
-
-def first_halo_kernel(
-    na, nb, sensors, trunk, spread, c_own, above, below, left, right, w1, b1, w2, b2, w3, b3,
-    predicted, sensor_trunk, coarse,
+    kx, ky = na // PER_CELL, nb // PER_CELL
+    coarse[0 : kx + 2, :] = edge[2][8 : 10 + kx, :]
+    coarse[8 * (ky + 1) : 8 * (ky + 1) + kx + 2, :] = edge[3][8 : 10 + kx, :]
+    for j in range(ky):
+        at = 8 * (j + 1)
+        coarse[at : at + 1, :] = edge[0][HALO + j : HALO + j + 1, :]
+        for i in range(kx):
+            coarse[at + 1 + i : at + 2 + i, :] = c_own[i * ky + j : i * ky + j + 1, :]
+        coarse[at + 1 + kx : at + 2 + kx, :] = edge[1][HALO + j : HALO + j + 1, :]
+    for j in range(ky + 2):
+        at = 8 * j + kx + 2
+        coarse[at : 8 * (j + 1), :] = jnp.zeros((6 - kx, coarse.shape[1]), F32)
+
+
+def next_kernel(
+    k, na, nb, n_row, n_col, cells, gathered, before, sensor_trunk, coarse, w1, b1, w2, b2, w3, b3,
+    pool, mean_trunk, coeffs, payload, sensors, lines,
 ):
     height = na + 2 * HALO
-    columns = trunk_sensors(trunk, spread)
-    sensor_trunk[...] = columns
-    vectors = sensor_vectors(sensors, 8 + height, predicted.shape[0])
-    predicted[...] = dot(branch(vectors, w1, b1, w2, b2, w3, b3), columns)
-    kx, ky = na // PER_CELL, nb // PER_CELL
-    edge = [x[...].astype(F32) for x in (above, below, left, right)]
-    for j in range(ky + 2):
-        for i in range(kx + 2):
-            if j == 0:
-                line = edge[2][8 + i : 9 + i, :]
-            elif j == ky + 1:
-                line = edge[3][8 + i : 9 + i, :]
-            elif i == 0:
-                line = edge[0][HALO + j - 1 : HALO + j, :]
-            elif i == kx + 1:
-                line = edge[1][HALO + j - 1 : HALO + j, :]
-            else:
-                at = (i - 1) * ky + j - 1
-                line = c_own[at : at + 1, :]
-            at = j * height + i * PER_CELL
-            coarse[at : at + PER_CELL, :] = jnp.broadcast_to(line, (PER_CELL, line.shape[1]))
-
-
-def fill_sensors(na, nb, n_row, n_col, first, columns, predicted, correction, sensors):
-    height = na + 2 * HALO
+    predicted = dot(before[...], sensor_trunk[...])
+    found = corrections(gathered, coarse, n_row, n_col, cells)
+    found = jnp.broadcast_to(found, (found.shape[0], sensors.shape[1]))
     row, col = lax.axis_index("row"), lax.axis_index("col")
     a_at = row * na - HALO + lax.broadcasted_iota(jnp.int32, (height, 1), 0)
     a_ok = (a_at >= 0) & (a_at < n_row * na)
+    for j in range(nb // PER_CELL + 2):
+        for i in range(height // PER_CELL):
+            at = j * height + i * PER_CELL
+            lines[at : at + PER_CELL, :] = jnp.broadcast_to(
+                found[8 * j + i : 8 * j + i + 1, :], (PER_CELL, found.shape[1])
+            )
     zero_ends(sensors)
-    for i, b in enumerate(columns):
+    first = k - 1
+    have = nb + 2 * HALO - 2 * first
+    for i in range(have):
+        b = first + i
         b_at = col * nb - HALO + b
         inside = jnp.where(a_ok & (b_at >= 0) & (b_at < n_col * nb), 1.0, 0.0)
         cell = b // PER_CELL
-        at = (b - first) * height
-        value = predicted[at : at + height, :] + correction[cell * height : (cell + 1) * height, 0:1]
+        value = predicted[i * height : (i + 1) * height, :] + lines[cell * height : (cell + 1) * height, :]
         sensors[8 + i * height : 8 + (i + 1) * height, :] = jnp.where(inside > 0.5, value, 0.0)
-
-
-def next_kernel(
-    k, na, nb, n_row, n_col, cells, gathered, predicted, coarse, w1, b1, w2, b2, w3, b3,
-    pool, mean_trunk, payload, extra, sensors,
-):
-    height = na + 2 * HALO
-    found = corrections(gathered, coarse, n_row, n_col, cells)
-    columns = range(HALO - 1, HALO + nb + 1)
-    fill_sensors(na, nb, n_row, n_col, k - 1, columns, predicted, found, sensors)
-    result = branch(own_vectors(na, nb, sensors, 8 + height), w1, b1, w2, b2, w3, b3)
-    send_means(result, pool, mean_trunk, lax.axis_index("col"), cells, payload)
     if k < ITERS:
-        extra[...] = jnp.broadcast_to(found, extra.shape)
+        vectors = sensor_vectors(sensors, 8 + height, coeffs.shape[0])
     else:
-        extra[...] = result
-
-
-def halo_kernel(
-    k, na, nb, n_row, n_col, before, correction, sensor_trunk, w1, b1, w2, b2, w3, b3, predicted, sensors
-):
-    columns = range(k - 1, nb + 2 * HALO - (k - 1))
-    fill_sensors(na, nb, n_row, n_col, k - 1, columns, before, correction, sensors)
-    vectors = sensor_vectors(sensors, 8 + na + 2 * HALO, predicted.shape[0])
-    predicted[...] = dot(branch(vectors, w1, b1, w2, b2, w3, b3), sensor_trunk[...])
-
-
-def predict_kernel(na, nb, steps, coeffs, trunk, out, strip):
+        vectors = own_vectors(na, nb, sensors, 8 + height)
+    result = branch(vectors, w1, b1, w2, b2, w3, b3)
+    coeffs[...] = result
+    send_means(result, pool, mean_trunk, col, cells, payload)
+
+
+def field_kernel(na, nb, n_row, n_col, cells, gathered, coarse, coeffs, trunk, out, correction, strip, ready, sent):
+    steps = ready.shape[0]
     width = trunk.shape[1] // steps
     per = width // TILE
+    ky = nb // PER_CELL
+    found = corrections(gathered, coarse, n_row, n_col, cells)
+    correction[...] = jnp.broadcast_to(found, correction.shape)
+    upper = lax.broadcasted_iota(jnp.int32, (8, LANES), 0) < PER_CELL
+    adds = {}
+    for a in range(0, na, 8):
+        for j in range(ky):
+            at = a // PER_CELL * ky + j
+            adds[a, j] = jnp.where(upper, correction[at : at + 1, :], correction[at + ky : at + ky + 1, :])
     low = low_lanes((8, LANES))
+    copies = []
     for step in range(steps):
         values = dot(coeffs[...], trunk[:, step * width : (step + 1) * width])
         for pair in range(nb // 2):
             for a in range(0, na, 8):
+                add = adds[a, 2 * pair // PER_CELL]
                 even, odd = (2 * pair * na + a, (2 * pair + 1) * na + a)
                 for r in range(0, per, 2):
                     lanes = slice(r * TILE, r * TILE + LANES)
                     x, y = values[even : even + 8, lanes], values[odd : odd + 8, lanes]
                     at = (pair * na + a) * per + r
-                    strip[pl.ds(at, 8, stride=per), :] = jnp.where(low, x, pltpu.roll(y, TILE, 1))
-                    strip[pl.ds(at + 1, 8, stride=per), :] = jnp.where(low, pltpu.roll(x, TILE, 1), y)
+                    strip[pl.ds(at, 8, stride=per), :] = jnp.where(low, x, pltpu.roll(y, TILE, 1)) + add
+                    strip[pl.ds(at + 1, 8, stride=per), :] = jnp.where(low, pltpu.roll(x, TILE, 1), y) + add
             done = strip[pair * na * per : (pair + 1) * na * per, :].reshape(na, per, LANES)
-            out[:, step * per : (step + 1) * per, pair * LANES : (pair + 1) * LANES] = done
-
-
-def field_kernel(ky, n_row, n_col, cells, gathered, coarse, prediction, out, correction):
-    step = pl.program_id(0)
-
-    @pl.when(step == 0)
-    def _():
-        found = corrections(gathered, coarse, n_row, n_col, cells)
-        correction[...] = jnp.broadcast_to(found, correction.shape)
-
-    here = out.shape[0]
-    for j in range(ky):
-        add = correction[pl.ds(step * ky + j, 1), :].reshape(1, 1, LANES)
-        for lane in range(j * CELL, (j + 1) * CELL, LANES):
-            lanes = slice(lane, lane + LANES)
-            out[:, :, lanes] = prediction[pl.ds(step * here, here), :, lanes] + add
-
-
-def pool_matrix(na, nb):
-    ky = nb // PER_CELL
-    pool = np.zeros((16, nb * na), np.float32)
+            ready[step, :, :, pair * LANES : (pair + 1) * LANES] = done
+        copies.append(
+            pltpu.make_async_copy(ready.at[step], out.at[:, pl.ds(step * per, per), :], sent.at[step])
+        )
+        copies[-1].start()
+    for copy in copies:
+        copy.wait()
+
+
+def pool_matrix(na, nb, first, trimmed):
+    kx, ky = na // PER_CELL, nb // PER_CELL
+    height = na if trimmed else na + 2 * HALO
+    skip_a = 0 if trimmed else HALO
+    skip_b = HALO - first
+    wide = nb + 2 * skip_b
+    pool = np.zeros((16, wide * height), np.float32)
     for a in range(na):
         for b in range(nb):
-            pool[(a // PER_CELL) * ky + b // PER_CELL, b * na + a] = 1.0 / PER_CELL**2
+            cell = (a // PER_CELL) * ky + b // PER_CELL
+            pool[cell, (b + skip_b) * height + a + skip_a] = 1.0 / PER_CELL**2
     return jnp.asarray(pool, BF16)
 
 
@@ -391,7 +399,38 @@
     spread_np, order = sensor_layout()
     spread = jnp.asarray(spread_np, BF16)
     half = TILE // 2
-    w_first = jnp.concatenate([w_sensor[at : at + half] for at in order[::half].tolist()], axis=0)
+    blocks = tuple((int(at), half) for at in order[::half])
+    hbm = pl.BlockSpec(memory_space=pltpu.HBM)
+
+    own, up, down = call(
+        part(extract_kernel, na, nb, ky),
+        (shape((nb * na, tile_values), BF16), shape((8, total), BF16), shape((8, total), BF16)),
+        field_start.reshape(na, TILE, cols_here),
+        coarse_matrix,
+        in_specs=[hbm, hbm],
+        scratch=[
+            pltpu.VMEM((na, TILE, cols_here), F32),
+            pltpu.VMEM(coarse_matrix.shape, F32),
+            pltpu.SemaphoreType.DMA((4,)),
+            pltpu.SemaphoreType.DMA,
+            pltpu.VMEM((nb * na, LANES), F32),
+            pltpu.VMEM((nb * na, LANES), F32),
+            pltpu.VMEM((8, total), F32),
+        ],
+        vmem=VMEM_LIMIT_FIRST,
+    )
+    above, below = shift(down, "row", True), shift(up, "row", False)
+    sensor_trunk, mean_trunk, w_first = call(
+        part(trunk_kernel, blocks),
+        (shape((latent, places), BF16), shape((latent, LANES), F32), shape(w_sensor.shape, BF16)),
+        trunk_basis,
+        w_sensor,
+        spread,
+        in_specs=[hbm, whole, whole],
+        scratch=[pltpu.VMEM(trunk_basis.shape, BF16), pltpu.SemaphoreType.DMA((4,))],
+        flops=1 << 30,
+    )
+    above, below, w_first = lax.optimization_barrier((above, below, w_first))
     net = (
         w_first,
         bias_sensor.reshape(1, hid),
@@ -400,24 +439,6 @@
         w_latent,
         bias_latent.reshape(1, latent),
     )
-    pool = pool_matrix(na, nb)
-
-    own, up, down = call(
-        part(extract_kernel, na, nb, ky),
-        (shape((nb * na, tile_values), BF16), shape((8, total), BF16), shape((8, total), BF16)),
-        field_start.reshape(na, TILE, cols_here),
-        coarse_matrix,
-        in_specs=[pl.BlockSpec(memory_space=pltpu.HBM), whole],
-        scratch=[
-            pltpu.VMEM((na, TILE, cols_here), F32),
-            pltpu.SemaphoreType.DMA((4,)),
-            pltpu.VMEM((nb * na, LANES), F32),
-            pltpu.VMEM((nb * na, LANES), F32),
-            pltpu.VMEM((8, total), F32),
-        ],
-    )
-    above, below = shift(down, "row", True), shift(up, "row", False)
-    mean_trunk = call(mean_kernel, shape((latent, LANES), F32), trunk_basis, flops=1 << 28)
     mid, to_left, to_right = call(
         part(columns_kernel, na, nb),
         (shape((nb * height, tile_values), BF16), shape((16, total), BF16), shape((16, total), BF16)),
@@ -433,80 +454,54 @@
         return (nb + 2 * HALO - 2 * k) * height
 
     payload_shape = shape((devices, LANES), F32)
-    payload, sensors = call(
+    coeffs, payload, coarse = call(
         part(first_kernel, na, nb, cells),
-        (payload_shape, shape((region(0) + 16, places), F32)),
+        (shape((region(1), latent), BF16), payload_shape, shape((8 * (ky + 2), total), F32)),
         mid,
         left,
         right,
+        above,
+        below,
+        coarse_matrix,
         spread,
         *net,
-        pool,
+        pool_matrix(na, nb, 1, False),
         mean_trunk,
-        scratch=[pltpu.VMEM((region(0), tile_values), F32)],
-    )
-    gathered = exchange(payload)
-    predicted, sensor_trunk, coarse = call(
-        part(first_halo_kernel, na, nb),
-        (
-            shape((region(1), places), F32),
-            shape((latent, places), BF16),
-            shape(((ky + 2) * height, total), F32),
-        ),
-        sensors,
-        trunk_basis,
-        spread,
-        coarse_matrix,
-        above,
-        below,
-        left,
-        right,
-        *net,
-        flops=1 << 32,
+        scratch=[pltpu.VMEM((region(0) + 16, places), F32), pltpu.VMEM((region(0), tile_values), F32)],
     )
     for k in range(2, ITERS + 1):
-        extra = shape((coarse.shape[0], LANES), F32) if k < ITERS else shape((nb * na, latent), BF16)
-        payload, extra = call(
+        gathered = exchange(payload)
+        coeffs, payload = call(
             part(next_kernel, k, na, nb, n_row, n_col, cells),
-            (payload_shape, extra),
+            (shape((region(k) if k < ITERS else nb * na, latent), BF16), payload_shape),
             gathered,
-            predicted,
+            coeffs,
+            sensor_trunk,
             coarse,
             *net,
-            pool,
+            pool_matrix(na, nb, k, k == ITERS),
             mean_trunk,
-            scratch=[pltpu.VMEM(((nb + 2) * height + 16, places), F32)],
+            scratch=[
+                pltpu.VMEM((region(k - 1) + 16, places), F32),
+                pltpu.VMEM(((ky + 2) * height, places), F32),
+            ],
         )
-        gathered = exchange(payload)
-        if k < ITERS:
-            predicted = call(
-                part(halo_kernel, k, na, nb, n_row, n_col),
-                shape((region(k), places), F32),
-                predicted,
-                extra,
-                sensor_trunk,
-                *net,
-                scratch=[pltpu.VMEM((region(k - 1) + 16, places), F32)],
-                flops=1 << 31,
-            )
+    gathered = exchange(payload)
     steps = 8
-    prediction = call(
-        part(predict_kernel, na, nb, steps),
-        shape((na, TILE, cols_here), F32),
-        extra,
-        trunk_basis,
-        scratch=[pltpu.VMEM((rows_here * cols_here // steps // LANES, LANES), F32)],
-        flops=1 << 32,
-    )
     out = call(
-        part(field_kernel, ky, n_row, n_col, cells),
+        part(field_kernel, na, nb, n_row, n_col, cells),
         shape((na, TILE, cols_here), F32),
         gathered,
         coarse_matrix,
-        prediction,
-        grid=(kx,),
-        out_specs=pl.BlockSpec((PER_CELL, TILE, cols_here), lambda i: (i, 0, 0)),
-        scratch=[pltpu.VMEM((cells, LANES), F32)],
+        coeffs,
+        trunk_basis,
+        out_specs=hbm,
+        scratch=[
+            pltpu.VMEM((cells, LANES), F32),
+            pltpu.VMEM((rows_here * cols_here // steps // LANES, LANES), F32),
+            pltpu.VMEM((steps, na, TILE // steps, cols_here), F32),
+            pltpu.SemaphoreType.DMA((steps,)),
+        ],
     )
     return out.reshape(rows_here, cols_here)
 

time: 145 us -> 118 us (0.81)
  blocking collectives: 0 us -> 85.5 us
  starting transfers between devices: 58.1 us -> 11.1 us
  local copies, waits for them, and re-layouts: 32.7 us -> 1 us
  waiting for transfers between devices: 24.4 us -> 4.07 us
  Pallas kernels: 27.7 us -> 15.4 us
    all_to_all x0 -> x4, blocking collectives: none -> 85.5 us  [exchange(): return lax.all_to_all(x, ('row', 'col'), 0, 0, tiled=True)]
    all_to_all x4 -> x0, starting transfers between devices: 47 us -> none  [exchange(): return lax.all_to_all(x, ('row', 'col'), 0, 0, tiled=True)]
    unnamed x85 -> x28, local copies, waits for them, and re-layouts: 31.9 us -> 1 us
    all_to_all x4 -> x0, waiting for transfers between devices: 22.4 us -> none  [exchange(): return lax.all_to_all(x, ('row', 'col'), 0, 0, tiled=True)]
    pallas_call x12 -> x8, Pallas kernels: 27.7 us -> 15.4 us  [call(): pl.pallas_call(kernel, out_shape=out_shape, in_specs=in_specs or [whole]...]
    ppermute x4, waiting for transfers between devices: 1.96 us -> 4.07 us  [shift(): return lax.ppermute(x, axis, pairs)]
  transfers between devices with their start and end apart: 8 -> 4, of which waited for: 5 -> 2; matrix products, arithmetic and copies ran while one was open for 7% -> 0% of each run, Pallas kernels for 11% -> 4%
where the time goes in v3:
time: 118 us; the launch traced here: 117 us
  blocking collectives  85.5 us (72%)
  Pallas kernels  15.4 us (13%)
  starting transfers between devices  11.1 us (9%)
  waiting for transfers between devices  4.07 us (3%)
    all_to_all x4, blocking collectives, exchange(): return lax.all_to_all(x, ('row', 'col'), 0, 0, tiled=True)  85.5 us
    pallas_call x8, Pallas kernels, call(): pl.pallas_call(kernel, out_shape=out_shape, in_specs=in_specs or [whole]...  15.4 us
    ppermute x4, starting transfers between devices, shift(): return lax.ppermute(x, axis, pairs)  11.1 us
    ppermute x4, waiting for transfers between devices, shift(): return lax.ppermute(x, axis, pairs)  4.07 us
  transfers between devices with their start and end apart: 4, of which 2 were waited for; matrix products, arithmetic and copies ran while one was open for 0% of the time, Pallas kernels for 4%

profile of v3, /device:TPU:1, one launch (start us, length us, event | category | flops | bytes accessed | tf_op | source)
XLA Modules:
  0.0 117.4 jit_solution(933899662385066611)
XLA Ops:
  0.0 0.0 copy-start.3
  0.0 0.9 copy-done.3
  0.9 0.0 copy-start.5
  0.9 0.0 copy-start.6
  0.9 2.9 %shard_map.136 = (bf16[192,256]{1,0:T(8,128)(2,1)S(1)}, bf16[8,3072]{1,0:T(8,128)(2,1)S(1)}, bf16[8,3072]{1,0:T(8,128)(2,1)S(1)}) custom-call(f32[16,64,768]{2,1,0:T(8,128)} %bitcast.41, f32[12,3072]{1,0:T(8,128)S(1)} %copy-done.3), custom_call_target="tpu_custom_call" | custom-call | bytes 1048576 | tf_op jit(solution)/shard_map/pallas_call | solution.py:40
  3.8 0.0 copy-start.4
  3.9 0.0 copy-start.1
  3.9 0.0 copy-start.2
  3.9 0.0 copy-start.7
  3.9 0.0 copy-start.8
  3.9 0.0 copy-start.9
  3.9 0.0 copy-start.10
  3.9 4.6 %collective-permute-start = (bf16[8,3072]{1,0:T(8,128)(2,1)S(1)}, bf16[8,3072]{1,0:T(8,128)(2,1)S(1)}, u32[]{:S(2)}, u32[]{:S(2)}) collective-permute-start(bf16[8,3072]{1,0:T(8,128)(2,1)S(1)} %get-tuple-element.27), channel_id=1, source_target_pairs={{0,32},{32,64},{64,96},{96,128},{128,160},{160,192},{192,224},{1,3... | collective-permute-start | bytes 147464 | tf_op jit(solution)/shard_map/ppermute | solution.py:394
  8.6 0.0 copy-start.12
  8.6 1.9 %collective-permute-start.1 = (bf16[8,3072]{1,0:T(8,128)(2,1)S(1)}, bf16[8,3072]{1,0:T(8,128)(2,1)S(1)}, u32[]{:S(2)}, u32[]{:S(2)}) collective-permute-start(bf16[8,3072]{1,0:T(8,128)(2,1)S(1)} %get-tuple-element.28), channel_id=1, source_target_pairs={{32,0},{64,32},{96,64},{128,96},{160,128},{192,160},{224,192},{33,... | collective-permute-start | bytes 147464 | tf_op jit(solution)/shard_map/ppermute | solution.py:394
  10.5 0.0 copy-done.5
  10.5 0.0 copy-done.6
  10.6 4.2 %shard_map.137 = (bf16[512,512]{1,0:T(8,128)(2,1)S(1)}, f32[512,128]{1,0:T(8,128)S(1)}, bf16[512,512]{1,0:T(8,128)(2,1)S(1)}) custom-call(bf16[512,4096]{1,0:T(8,128)(2,1)} %trunk.1, bf16[512,512]{1,0:T(8,128)(2,1)S(1)} %copy-done.6, bf16[256,512]{1,0:T(8,128)(2,1)S(1)} %copy-done.5), custom_call_target="tpu_custom_call" | custom-call | flops 1073741824 | bytes 1048576 | tf_op jit(solution)/shard_map/pallas_call | solution.py:40
  14.8 0.0 collective-permute-done.above
  14.8 0.0 collective-permute-done.1.below
  14.8 0.0 copy-done.4
  14.8 0.1 shard_map.138
  14.9 3.2 %collective-permute-start.2 = (bf16[16,3072]{1,0:T(8,128)(2,1)S(1)}, bf16[16,3072]{1,0:T(8,128)(2,1)S(1)}, u32[]{:S(2)}, u32[]{:S(2)}) collective-permute-start(bf16[16,3072]{1,0:T(8,128)(2,1)S(1)} %get-tuple-element.33), channel_id=1, source_target_pairs={{0,1},{1,2},{2,3},{3,4},{4,5},{5,6},{6,7},{7,8},{8,9},{9,10},{10,1... | collective-permute-start | bytes 294920 | tf_op jit(solution)/shard_map/ppermute | solution.py:394
  18.1 1.3 %collective-permute-start.3 = (bf16[16,3072]{1,0:T(8,128)(2,1)S(1)}, bf16[16,3072]{1,0:T(8,128)(2,1)S(1)}, u32[]{:S(2)}, u32[]{:S(2)}) collective-permute-start(bf16[16,3072]{1,0:T(8,128)(2,1)S(1)} %get-tuple-element.34), channel_id=1, source_target_pairs={{1,0},{2,1},{3,2},{4,3},{5,4},{6,5},{7,6},{8,7},{9,8},{10,9},{11,1... | collective-permute-start | bytes 294920 | tf_op jit(solution)/shard_map/ppermute | solution.py:394
  19.4 0.3 collective-permute-done.2.left
  19.7 3.7 %collective-permute-done.3.right = bf16[16,3072]{1,0:T(8,128)(2,1)S(1)} collective-permute-done((bf16[16,3072]{1,0:T(8,128)(2,1)S(1)}, bf16[16,3072]{1,0:T(8,128)(2,1)S(1)}, u32[]{:S(2)}, u32[]{:S(2)}) %collective-permute-start.3) | collective-permute-done | bytes 98336 | tf_op jit(solution)/shard_map/ppermute | solution.py:394
  23.5 0.0 copy-done.1
  23.5 0.0 copy-done.2
  23.5 0.0 copy-done.7
  23.5 0.0 copy-done.8
  23.5 0.0 copy-done.9
  23.5 0.0 copy-done.10
  23.5 0.0 copy-start.11
  23.5 1.4 %shard_map.139 = (bf16[432,512]{1,0:T(8,128)(2,1)S(1)}, f32[256,128]{1,0:T(8,128)S(1)}, f32[40,3072]{1,0:T(8,128)S(1)}) custom-call(bf16[288,256]{1,0:T(8,128)(2,1)S(1)} %get-tuple-element.32.mid, bf16[16,3072]{1,0:T(8,128)(2,1)S(1)} %collective-permute-done.2.left, bf16[16,3072]{1,0:T(8,128)(2,1)S(1)} %collective-permute-done.3.right, ...), custom_call_target="tpu_custom_call" | custom-call | bytes 1048576 | tf_op jit(solution)/shard_map/pallas_call | solution.py:40
  24.9 30.4 %all_to_all.44 = f32[256,1,128]{2,1,0:T(1,128)S(1)} all-to-all(f32[256,1,128]{2,1,0:T(1,128)S(1)} %bitcast.25), channel_id=1, replica_groups=mesh['row'=8,'col'=32] {'row','col'}, dimensions={0} | all-to-all | bytes 262144 | tf_op jit(solution)/shard_map/all_to_all | solution.py:397
  55.3 0.0 copy-done.12
  55.3 0.0 copy-start.13
  55.3 1.6 %shard_map.140 = (bf16[384,512]{1,0:T(8,128)(2,1)S(1)}, f32[256,128]{1,0:T(8,128)S(1)}) custom-call(f32[256,128]{1,0:T(8,128)S(1)} %bitcast.23, bf16[432,512]{1,0:T(8,128)(2,1)S(1)} %get-tuple-element.38.before, bf16[512,512]{1,0:T(8,128)(2,1)S(1)} %get-tuple-element.39.sensor_trunk, f32[40,3072]{1,0:T(8,128)S(1)} %get-tuple-element.40.coarse, ...), custom_call_target="tpu_custom_call" | custom-call | bytes 1048576 | tf_op jit(solution)/shard_map/pallas_call | solution.py:40
  56.9 18.3 %all_to_all.45 = f32[256,1,128]{2,1,0:T(1,128)S(1)} all-to-all(f32[256,1,128]{2,1,0:T(1,128)S(1)} %bitcast.27), channel_id=1, replica_groups=mesh['row'=8,'col'=32] {'row','col'}, dimensions={0} | all-to-all | bytes 262144 | tf_op jit(solution)/shard_map/all_to_all | solution.py:397
  75.2 0.0 copy-done.11
  75.2 0.0 copy-start
  75.2 1.5 %shard_map.141 = (bf16[336,512]{1,0:T(8,128)(2,1)S(1)}, f32[256,128]{1,0:T(8,128)S(1)}) custom-call(f32[256,128]{1,0:T(8,128)S(1)} %bitcast.24, bf16[384,512]{1,0:T(8,128)(2,1)S(1)} %get-tuple-element.42.before, bf16[512,512]{1,0:T(8,128)(2,1)S(1)} %get-tuple-element.39.sensor_trunk, f32[40,3072]{1,0:T(8,128)S(1)} %get-tuple-element.40.coarse, ...), custom_call_target="tpu_custom_call" | custom-call | bytes 1048576 | tf_op jit(solution)/shard_map/pallas_call | solution.py:40
  76.8 18.3 %all_to_all.46 = f32[256,1,128]{2,1,0:T(1,128)S(1)} all-to-all(f32[256,1,128]{2,1,0:T(1,128)S(1)} %bitcast.28), channel_id=1, replica_groups=mesh['row'=8,'col'=32] {'row','col'}, dimensions={0} | all-to-all | bytes 262144 | tf_op jit(solution)/shard_map/all_to_all | solution.py:397
  95.1 0.0 copy-done.13
  95.1 1.3 %shard_map.142 = (bf16[192,512]{1,0:T(8,128)(2,1)S(1)}, f32[256,128]{1,0:T(8,128)S(1)}) custom-call(f32[256,128]{1,0:T(8,128)S(1)} %bitcast.22, bf16[336,512]{1,0:T(8,128)(2,1)S(1)} %get-tuple-element.44.before, bf16[512,512]{1,0:T(8,128)(2,1)S(1)} %get-tuple-element.39.sensor_trunk, f32[40,3072]{1,0:T(8,128)S(1)} %get-tuple-element.40.coarse, ...), custom_call_target="tpu_custom_call" | custom-call | bytes 1048576 | tf_op jit(solution)/shard_map/pallas_call | solution.py:40
  96.4 18.5 %all_to_all.47 = f32[256,1,128]{2,1,0:T(1,128)S(1)} all-to-all(f32[256,1,128]{2,1,0:T(1,128)S(1)} %bitcast.26), channel_id=1, replica_groups=mesh['row'=8,'col'=32] {'row','col'}, dimensions={0} | all-to-all | bytes 262144 | tf_op jit(solution)/shard_map/all_to_all | solution.py:397
  114.9 0.0 copy-done
  114.9 2.3 %shard_map.143 = f32[16,64,768]{2,1,0:T(8,128)} custom-call(f32[256,128]{1,0:T(8,128)S(1)} %bitcast.21, f32[12,3072]{1,0:T(8,128)S(1)} %copy-done.4, bf16[192,512]{1,0:T(8,128)(2,1)S(1)} %get-tuple-element.46.coeffs, bf16[512,4096]{1,0:T(8,128)(2,1)S(1)} %copy-done), custom_call_target="tpu_custom_call" | custom-call | bytes 1048576 | tf_op jit(solution)/shard_map/pallas_call | solution.py:40
Async XLA Ops:
  0.0 0.9 copy-start.3
  0.9 9.6 %copy-start.5 = (bf16[256,512]{1,0:T(8,128)(2,1)S(1)}, bf16[256,512]{1,0:T(8,128)(2,1)}, u32[]{:S(2)}) copy-start(bf16[256,512]{1,0:T(8,128)(2,1)} %constant.10.clone.spread) | copy-start | bytes 786436
  0.9 9.6 %copy-start.6 = (bf16[512,512]{1,0:T(8,128)(2,1)S(1)}, bf16[512,512]{1,0:T(8,128)(2,1)}, u32[]{:S(2)}) copy-start(bf16[512,512]{1,0:T(8,128)(2,1)} %w_sensor.1) | copy-start | bytes 1572868
  3.8 10.9 %copy-start.4 = (f32[12,3072]{1,0:T(8,128)S(1)}, f32[12,3072]{1,0:T(8,128)}, u32[]{:S(2)}) copy-start(f32[12,3072]{1,0:T(8,128)} %coarse.3) | copy-start | bytes 442372
  3.9 19.6 %copy-start.1 = (bf16[512,512]{1,0:T(8,128)(2,1)S(1)}, bf16[512,512]{1,0:T(8,128)(2,1)}, u32[]{:S(2)}) copy-start(bf16[512,512]{1,0:T(8,128)(2,1)} %w2.7) | copy-start | bytes 1572868
  3.9 19.6 %copy-start.2 = (bf16[512,512]{1,0:T(8,128)(2,1)S(1)}, bf16[512,512]{1,0:T(8,128)(2,1)}, u32[]{:S(2)}) copy-start(bf16[512,512]{1,0:T(8,128)(2,1)} %w3.7) | copy-start | bytes 1572868
  3.9 19.6 %copy-start.7 = (f32[512]{0:T(512)S(1)}, f32[512]{0:T(512)}, u32[]{:S(2)}) copy-start(f32[512]{0:T(512)} %param.16) | copy-start | bytes 6148
  3.9 19.6 %copy-start.8 = (f32[512]{0:T(512)S(1)}, f32[512]{0:T(512)}, u32[]{:S(2)}) copy-start(f32[512]{0:T(512)} %param.18) | copy-start | bytes 6148
  3.9 19.6 %copy-start.9 = (f32[512]{0:T(512)S(1)}, f32[512]{0:T(512)}, u32[]{:S(2)}) copy-start(f32[512]{0:T(512)} %param.20) | copy-start | bytes 6148
  3.9 19.6 %copy-start.10 = (bf16[16,432]{1,0:T(8,128)(2,1)S(1)}, bf16[16,432]{1,0:T(8,128)(2,1)}, u32[]{:S(2)}) copy-start(bf16[16,432]{1,0:T(8,128)(2,1)} %constant.11.clone.pool) | copy-start | bytes 41476
  3.9 10.8 %collective-permute-start = (bf16[8,3072]{1,0:T(8,128)(2,1)S(1)}, bf16[8,3072]{1,0:T(8,128)(2,1)S(1)}, u32[]{:S(2)}, u32[]{:S(2)}) collective-permute-start(bf16[8,3072]{1,0:T(8,128)(2,1)S(1)} %get-tuple-element.27), channel_id=1, source_target_pairs={{0,32},{32,64},{64,96},{96,128},{128,160},{160,192},{192,224},{1,3... | collective-permute-start | bytes 147464 | tf_op jit(solution)/shard_map/ppermute | solution.py:394
  8.6 46.8 %copy-start.12 = (bf16[16,384]{1,0:T(8,128)(2,1)S(1)}, bf16[16,384]{1,0:T(8,128)(2,1)}, u32[]{:S(2)}) copy-start(bf16[16,384]{1,0:T(8,128)(2,1)} %constant.12.clone.pool) | copy-start | bytes 36868
  8.6 6.2 %collective-permute-start.1 = (bf16[8,3072]{1,0:T(8,128)(2,1)S(1)}, bf16[8,3072]{1,0:T(8,128)(2,1)S(1)}, u32[]{:S(2)}, u32[]{:S(2)}) collective-permute-start(bf16[8,3072]{1,0:T(8,128)(2,1)S(1)} %get-tuple-element.28), channel_id=1, source_target_pairs={{32,0},{64,32},{96,64},{128,96},{160,128},{192,160},{224,192},{33,... | collective-permute-start | bytes 147464 | tf_op jit(solution)/shard_map/ppermute | solution.py:394
  14.9 4.8 %collective-permute-start.2 = (bf16[16,3072]{1,0:T(8,128)(2,1)S(1)}, bf16[16,3072]{1,0:T(8,128)(2,1)S(1)}, u32[]{:S(2)}, u32[]{:S(2)}) collective-permute-start(bf16[16,3072]{1,0:T(8,128)(2,1)S(1)} %get-tuple-element.33), channel_id=1, source_target_pairs={{0,1},{1,2},{2,3},{3,4},{4,5},{5,6},{6,7},{7,8},{8,9},{9,10},{10,1... | collective-permute-start | bytes 294920 | tf_op jit(solution)/shard_map/ppermute | solution.py:394
  18.1 5.4 %collective-permute-start.3 = (bf16[16,3072]{1,0:T(8,128)(2,1)S(1)}, bf16[16,3072]{1,0:T(8,128)(2,1)S(1)}, u32[]{:S(2)}, u32[]{:S(2)}) collective-permute-start(bf16[16,3072]{1,0:T(8,128)(2,1)S(1)} %get-tuple-element.34), channel_id=1, source_target_pairs={{1,0},{2,1},{3,2},{4,3},{5,4},{6,5},{7,6},{8,7},{9,8},{10,9},{11,1... | collective-permute-start | bytes 294920 | tf_op jit(solution)/shard_map/ppermute | solution.py:394
  23.5 51.7 %copy-start.11 = (bf16[16,336]{1,0:T(8,128)(2,1)S(1)}, bf16[16,336]{1,0:T(8,128)(2,1)}, u32[]{:S(2)}) copy-start(bf16[16,336]{1,0:T(8,128)(2,1)} %constant.13.clone.pool) | copy-start | bytes 32260
  55.3 39.7 %copy-start.13 = (bf16[16,192]{1,0:T(8,128)(2,1)S(1)}, bf16[16,192]{1,0:T(8,128)(2,1)}, u32[]{:S(2)}) copy-start(bf16[16,192]{1,0:T(8,128)(2,1)} %constant.14.clone.pool) | copy-start | bytes 18436
  75.2 39.7 %copy-start = (bf16[512,4096]{1,0:T(8,128)(2,1)S(1)}, bf16[512,4096]{1,0:T(8,128)(2,1)}, u32[]{:S(2)}) copy-start(bf16[512,4096]{1,0:T(8,128)(2,1)} %trunk.1) | copy-start | bytes 12582916

commit v4 on v3

--- a/solution.py
+++ b/solution.py
@@ -17,7 +17,6 @@
 F32 = jnp.float32
 BF16 = jnp.bfloat16
 VMEM_LIMIT = 48 * 1024 * 1024
-VMEM_LIMIT_FIRST = 52 * 1024 * 1024
 
 
 def dot(a, b, **kw):
@@ -32,7 +31,7 @@
     return lax.broadcasted_iota(jnp.int32, shape, 1) < TILE
 
 
-def call(kernel, out_shape, *args, grid=(), in_specs=None, out_specs=None, scratch=(), flops=0, vmem=VMEM_LIMIT):
+def call(kernel, out_shape, *args, grid=(), in_specs=None, out_specs=None, scratch=(), flops=1 << 31, vmem=VMEM_LIMIT):
     whole = pl.BlockSpec(memory_space=pltpu.VMEM)
     specs = {}
     if grid:
@@ -71,27 +70,15 @@
     return spread, order
 
 
-def extract_kernel(
-    na, nb, ky, field, coarse_hbm, own, up, down, cells, coarse, arrived, coarse_arrived, row_part, col_part, packed
-):
-    cols = field.shape[2]
-    here = na // arrived.shape[0]
-    copies = [
-        pltpu.make_async_copy(field.at[pl.ds(i * here, here)], cells.at[pl.ds(i * here, here)], arrived.at[i])
-        for i in range(arrived.shape[0])
-    ]
-    for copy in copies:
-        copy.start()
-    coarse_copy = pltpu.make_async_copy(coarse_hbm, coarse, coarse_arrived)
-    coarse_copy.start()
+def extract_kernel(na, nb, cells, row_part, col_part):
+    cols = cells.shape[2]
+    here = 8
     sel_row = lax.broadcasted_iota(jnp.int32, (2 * 16, cols), 0)
     sel_col = lax.broadcasted_iota(jnp.int32, (2 * 16, cols), 1)
     side, b_of = sel_row // 16, sel_row % 16
     pick = jnp.where(sel_col == b_of * TILE + (TILE // 2 - 1) + side, 1.0, 0.0).astype(BF16)
     low_row, low_col = low_lanes((here, LANES)), low_lanes((16, LANES))
-    for i, copy in enumerate(copies):
-        copy.wait()
-        base = i * here
+    for base in range(0, na, here):
         chunk = cells[base : base + here]
         picked = nt_dot(pick, chunk.reshape(here * TILE, cols).astype(BF16))
         r31 = cells[base : base + here, TILE // 2 - 1, :]
@@ -109,11 +96,11 @@
             odd = jnp.where(low_col, pltpu.roll(x, TILE, 1), y)
             col_part[pl.ds(base + 2 * pair, nb, stride=na), :] = even[0:nb]
             col_part[pl.ds(base + 2 * pair + 1, nb, stride=na), :] = odd[0:nb]
-    own[:, 0:LANES] = row_part[...].astype(BF16)
-    own[:, LANES : 2 * LANES] = col_part[...].astype(BF16)
-    coarse_copy.wait()
+
+
+def pack_kernel(na, nb, ky, row_part, col_part, coarse, up, down, packed):
+    packed[...] = jnp.zeros(packed.shape, F32)
     for target, first, line in ((up, 0, 0), (down, na - HALO, coarse.shape[0] - ky)):
-        packed[...] = jnp.zeros(packed.shape, F32)
         for b in range(nb):
             rows = slice(b * na + first, b * na + first + HALO)
             packed[0:HALO, 2 * b * LANES : (2 * b + 1) * LANES] = row_part[rows, :]
@@ -122,14 +109,15 @@
         target[...] = packed[...].astype(BF16)
 
 
-def columns_kernel(na, nb, own, above, below, coarse, both, left, right, tall, packed):
+def columns_kernel(na, nb, row_part, col_part, above, below, coarse, both, left, right, tall, packed):
     height, values = na + 2 * HALO, 4 * TILE
     kx, ky = na // PER_CELL, nb // PER_CELL
     over, under = above[...].astype(F32), below[...].astype(F32)
     for b in range(nb):
         at = b * height
         tall[at : at + HALO, :] = over[0:HALO, b * values : (b + 1) * values]
-        tall[at + HALO : at + HALO + na, :] = own[b * na : (b + 1) * na, :].astype(F32)
+        tall[at + HALO : at + HALO + na, 0:LANES] = row_part[b * na : (b + 1) * na, :]
+        tall[at + HALO : at + HALO + na, LANES : 2 * LANES] = col_part[b * na : (b + 1) * na, :]
         tall[at + HALO + na : at + height, :] = under[0:HALO, b * values : (b + 1) * values]
     both[...] = tall[...].astype(BF16)
     packed[...] = jnp.zeros(packed.shape, F32)
@@ -146,14 +134,11 @@
         target[...] = packed[...].astype(BF16)
 
 
-def trunk_kernel(blocks, trunk_hbm, w_sensor, spread, sensor_trunk, mean_trunk, w_out, trunk, arrived):
+def trunk_kernel(blocks, trunk_hbm, w_sensor, trunk, mean_trunk, w_out, arrived):
     steps = arrived.shape[0]
-    width = trunk.shape[1] // steps
-    per = width // TILE
+    depth = trunk.shape[0] // steps
     copies = [
-        pltpu.make_async_copy(
-            trunk_hbm.at[:, pl.ds(i * width, width)], trunk.at[:, pl.ds(i * width, width)], arrived.at[i]
-        )
+        pltpu.make_async_copy(trunk_hbm.at[pl.ds(i * depth, depth)], trunk.at[pl.ds(i * depth, depth)], arrived.at[i])
         for i in range(steps)
     ]
     for copy in copies:
@@ -162,24 +147,31 @@
     for start, size in blocks:
         w_out[at : at + size, :] = w_sensor[start : start + size, :]
         at += size
+    share = jnp.full((trunk.shape[1], LANES), 1.0 / (TILE * TILE), BF16)
+    for i, copy in enumerate(copies):
+        copy.wait()
+        rows = slice(i * depth, (i + 1) * depth)
+        mean_trunk[rows, :] = dot(trunk[rows, :], share)
+
+
+def sensor_trunk_kernel(trunk, spread, sensor_trunk):
+    width = 1024
+    per = width // TILE
     point = lax.broadcasted_iota(jnp.int32, (width, LANES), 0)
     lane = lax.broadcasted_iota(jnp.int32, (width, LANES), 1)
-    column = point % TILE == TILE // 2 - 1 + lane // TILE
-    away = jnp.where(column, lane % TILE - point // TILE, -1)
-    share = jnp.full((width, LANES), 1.0 / (TILE * TILE), BF16)
+    column = (point & (TILE - 1)) == TILE // 2 - 1 + (lane >> 6)
+    away = jnp.where(column, (lane & (TILE - 1)) - (point >> 6), -1)
     total = None
-    for step, copy in enumerate(copies):
-        copy.wait()
+    for step in range(trunk.shape[1] // width):
         pick = jnp.where(away == step * per, 1.0, 0.0).astype(BF16)
-        part = dot(trunk[:, step * width : (step + 1) * width], jnp.concatenate([pick, share], axis=1))
+        part = dot(trunk[:, step * width : (step + 1) * width], pick)
         total = part if total is None else total + part
     middle = trunk.shape[1] // 2
     row31 = pltpu.roll(trunk[:, middle - LANES : middle].astype(F32), TILE, 1)
     row32 = pltpu.roll(trunk[:, middle : middle + LANES].astype(F32), TILE, 1)
     rows = jnp.where(low_lanes(row31.shape), row31, row32)
-    unique = jnp.concatenate([rows, total[:, 0:LANES]], axis=1).astype(BF16)
+    unique = jnp.concatenate([rows, total], axis=1).astype(BF16)
     sensor_trunk[...] = dot(unique, spread[...]).astype(BF16)
-    mean_trunk[...] = total[:, LANES : 2 * LANES]
 
 
 def sensor_vectors(sensors, base, count):
@@ -402,35 +394,43 @@
     blocks = tuple((int(at), half) for at in order[::half])
     hbm = pl.BlockSpec(memory_space=pltpu.HBM)
 
-    own, up, down = call(
-        part(extract_kernel, na, nb, ky),
-        (shape((nb * na, tile_values), BF16), shape((8, total), BF16), shape((8, total), BF16)),
+    row_part, col_part = call(
+        part(extract_kernel, na, nb),
+        (shape((nb * na, LANES), F32), shape((nb * na, LANES), F32)),
         field_start.reshape(na, TILE, cols_here),
+    )
+    up, down = call(
+        part(pack_kernel, na, nb, ky),
+        (shape((8, total), BF16), shape((8, total), BF16)),
+        row_part,
+        col_part,
         coarse_matrix,
-        in_specs=[hbm, hbm],
-        scratch=[
-            pltpu.VMEM((na, TILE, cols_here), F32),
-            pltpu.VMEM(coarse_matrix.shape, F32),
-            pltpu.SemaphoreType.DMA((4,)),
-            pltpu.SemaphoreType.DMA,
-            pltpu.VMEM((nb * na, LANES), F32),
-            pltpu.VMEM((nb * na, LANES), F32),
-            pltpu.VMEM((8, total), F32),
-        ],
-        vmem=VMEM_LIMIT_FIRST,
+        scratch=[pltpu.VMEM((8, total), F32)],
     )
     above, below = shift(down, "row", True), shift(up, "row", False)
-    sensor_trunk, mean_trunk, w_first = call(
+    trunk, mean_trunk, w_first = call(
         part(trunk_kernel, blocks),
-        (shape((latent, places), BF16), shape((latent, LANES), F32), shape(w_sensor.shape, BF16)),
+        (shape(trunk_basis.shape, BF16), shape((latent, LANES), F32), shape(w_sensor.shape, BF16)),
         trunk_basis,
         w_sensor,
-        spread,
-        in_specs=[hbm, whole, whole],
-        scratch=[pltpu.VMEM(trunk_basis.shape, BF16), pltpu.SemaphoreType.DMA((4,))],
-        flops=1 << 30,
+        in_specs=[hbm, whole],
+        scratch=[pltpu.SemaphoreType.DMA((4,))],
+        flops=1 << 32,
     )
     above, below, w_first = lax.optimization_barrier((above, below, w_first))
+    mid, to_left, to_right = call(
+        part(columns_kernel, na, nb),
+        (shape((nb * height, tile_values), BF16), shape((16, total), BF16), shape((16, total), BF16)),
+        row_part,
+        col_part,
+        above,
+        below,
+        coarse_matrix,
+        scratch=[pltpu.VMEM((nb * height, tile_values), F32), pltpu.VMEM((16, total), F32)],
+    )
+    to_left, to_right, mean_trunk = lax.optimization_barrier((to_left, to_right, mean_trunk))
+    left, right = shift(to_right, "col", True), shift(to_left, "col", False)
+
     net = (
         w_first,
         bias_sensor.reshape(1, hid),
@@ -439,16 +439,11 @@
         w_latent,
         bias_latent.reshape(1, latent),
     )
-    mid, to_left, to_right = call(
-        part(columns_kernel, na, nb),
-        (shape((nb * height, tile_values), BF16), shape((16, total), BF16), shape((16, total), BF16)),
-        own,
-        above,
-        below,
-        coarse_matrix,
-        scratch=[pltpu.VMEM((nb * height, tile_values), F32), pltpu.VMEM((16, total), F32)],
-    )
-    left, right = shift(to_right, "col", True), shift(to_left, "col", False)
+
+    sensor_trunk = call(
+        sensor_trunk_kernel, shape((latent, places), BF16), trunk, spread, flops=1 << 30
+    )
+    left, right, sensor_trunk = lax.optimization_barrier((left, right, sensor_trunk))
 
     def region(k):
         return (nb + 2 * HALO - 2 * k) * height
@@ -494,7 +489,7 @@
         gathered,
         coarse_matrix,
         coeffs,
-        trunk_basis,
+        trunk,
         out_specs=hbm,
         scratch=[
             pltpu.VMEM((cells, LANES), F32),

time: 118 us -> 115 us (0.975)
  Pallas kernels: 15.4 us -> 13.5 us
  waiting for transfers between devices: 4.07 us -> 2.83 us
  local copies, waits for them, and re-layouts: 1 us -> 2.22 us
    pallas_call x8 -> x10, Pallas kernels: 15.4 us -> 13.5 us  [call(): pl.pallas_call(kernel, out_shape=out_shape, in_specs=in_specs or [whole]...]
    ppermute x4, waiting for transfers between devices: 4.07 us -> 2.83 us  [shift(): return lax.ppermute(x, axis, pairs)]
    unnamed x28 -> x26, local copies, waits for them, and re-layouts: 1 us -> 2.22 us
where the time goes in v4:
time: 115 us
  blocking collectives  85 us (74%)
  Pallas kernels  13.5 us (12%)
  starting transfers between devices  11.1 us (10%)
  waiting for transfers between devices  2.83 us (2%)
  local copies, waits for them, and re-layouts  2.22 us (2%)
    all_to_all x4, blocking collectives, exchange(): return lax.all_to_all(x, ('row', 'col'), 0, 0, tiled=True)  85 us
    pallas_call x10, Pallas kernels, call(): pl.pallas_call(kernel, out_shape=out_shape, in_specs=in_specs or [whole]...  13.5 us
    ppermute x4, starting transfers between devices, shift(): return lax.ppermute(x, axis, pairs)  11.1 us
    ppermute x4, waiting for transfers between devices, shift(): return lax.ppermute(x, axis, pairs)  2.83 us
  transfers between devices with their start and end apart: 4, of which 2 were waited for; matrix products, arithmetic and copies ran while one was open for 0% of the time, Pallas kernels for 4%

profile of v4, /device:TPU:1, one launch (start us, length us, event | category | flops | bytes accessed | tf_op | source)
XLA Modules:
  0.0 115.0 jit_solution(2253349644273071271)
XLA Ops:
  0.0 0.0 copy-start.1
  0.0 1.9 %copy-done.1 = f32[1024,768]{1,0:T(8,128)S(1)} copy-done((f32[1024,768]{1,0:T(8,128)S(1)}, f32[1024,768]{1,0:T(8,128)}, u32[]{:S(2)}) %copy-start.1) | copy-done | bytes 3145752
  1.9 0.0 copy-start.5
  1.9 0.6 shard_map.136
  2.5 0.0 copy-start.2
  2.6 0.3 copy-done.5
  2.8 0.1 shard_map.137
  2.9 4.5 %collective-permute-start = (bf16[8,3072]{1,0:T(8,128)(2,1)S(1)}, bf16[8,3072]{1,0:T(8,128)(2,1)S(1)}, u32[]{:S(2)}, u32[]{:S(2)}) collective-permute-start(bf16[8,3072]{1,0:T(8,128)(2,1)S(1)} %get-tuple-element.35), channel_id=1, source_target_pairs={{0,32},{32,64},{64,96},{96,128},{128,160},{160,192},{192,224},{1,3... | collective-permute-start | bytes 147464 | tf_op jit(solution)/shard_map/ppermute | solution.py:386
  7.4 1.9 %collective-permute-start.1 = (bf16[8,3072]{1,0:T(8,128)(2,1)S(1)}, bf16[8,3072]{1,0:T(8,128)(2,1)S(1)}, u32[]{:S(2)}, u32[]{:S(2)}) collective-permute-start(bf16[8,3072]{1,0:T(8,128)(2,1)S(1)} %get-tuple-element.36), channel_id=1, source_target_pairs={{32,0},{64,32},{96,64},{128,96},{160,128},{192,160},{224,192},{33,... | collective-permute-start | bytes 147464 | tf_op jit(solution)/shard_map/ppermute | solution.py:386
  9.3 0.0 copy-done.2
  9.3 3.0 %shard_map.138 = (bf16[512,4096]{1,0:T(8,128)(2,1)S(1)}, f32[512,128]{1,0:T(8,128)S(1)}, bf16[512,512]{1,0:T(8,128)(2,1)S(1)}) custom-call(bf16[512,4096]{1,0:T(8,128)(2,1)} %trunk_hbm.1, bf16[512,512]{1,0:T(8,128)(2,1)S(1)} %copy-done.2), custom_call_target="tpu_custom_call" | custom-call | flops 4294967296 | bytes 1048576 | tf_op jit(solution)/shard_map/pallas_call | solution.py:39
  12.3 0.0 copy-start
  12.3 0.0 collective-permute-done.above
  12.3 0.5 collective-permute-done.1.below
  12.8 0.1 shard_map.139
  12.9 0.0 copy-start.3
  12.9 0.0 copy-start.4
  12.9 0.0 copy-start.6
  12.9 0.0 copy-start.7
  13.0 0.0 copy-start.8
  13.0 0.0 copy-start.9
  13.0 3.3 %collective-permute-start.2 = (bf16[16,3072]{1,0:T(8,128)(2,1)S(1)}, bf16[16,3072]{1,0:T(8,128)(2,1)S(1)}, u32[]{:S(2)}, u32[]{:S(2)}) collective-permute-start(bf16[16,3072]{1,0:T(8,128)(2,1)S(1)} %get-tuple-element.44), channel_id=1, source_target_pairs={{0,1},{1,2},{2,3},{3,4},{4,5},{5,6},{6,7},{7,8},{8,9},{9,10},{10,1... | collective-permute-start | bytes 294920 | tf_op jit(solution)/shard_map/ppermute | solution.py:386
  16.3 1.3 %collective-permute-start.3 = (bf16[16,3072]{1,0:T(8,128)(2,1)S(1)}, bf16[16,3072]{1,0:T(8,128)(2,1)S(1)}, u32[]{:S(2)}, u32[]{:S(2)}) collective-permute-start(bf16[16,3072]{1,0:T(8,128)(2,1)S(1)} %get-tuple-element.45), channel_id=1, source_target_pairs={{1,0},{2,1},{3,2},{4,3},{5,4},{6,5},{7,6},{8,7},{9,8},{10,9},{11,1... | collective-permute-start | bytes 294920 | tf_op jit(solution)/shard_map/ppermute | solution.py:386
  17.6 0.0 copy-done
  17.6 1.7 %shard_map.140.sensor_trunk = bf16[512,512]{1,0:T(8,128)(2,1)S(1)} custom-call(bf16[512,4096]{1,0:T(8,128)(2,1)S(1)} %get-tuple-element.46.trunk, bf16[256,512]{1,0:T(8,128)(2,1)S(1)} %copy-done), custom_call_target="tpu_custom_call" | custom-call | flops 1073741824 | bytes 1048576 | tf_op jit(solution)/shard_map/pallas_call | solution.py:39
  19.3 0.0 copy-start.11
  19.3 0.0 collective-permute-done.2.left
  19.3 2.3 %collective-permute-done.3.right = bf16[16,3072]{1,0:T(8,128)(2,1)S(1)} collective-permute-done((bf16[16,3072]{1,0:T(8,128)(2,1)S(1)}, bf16[16,3072]{1,0:T(8,128)(2,1)S(1)}, u32[]{:S(2)}, u32[]{:S(2)}) %collective-permute-start.3) | collective-permute-done | bytes 98336 | tf_op jit(solution)/shard_map/ppermute | solution.py:386
  21.7 0.0 copy-done.3
  21.7 0.0 copy-done.4
  21.7 0.0 copy-done.6
  21.7 0.0 copy-done.7
  21.7 0.0 copy-done.8
  21.7 0.0 copy-done.9
  21.7 1.4 %shard_map.141 = (bf16[432,512]{1,0:T(8,128)(2,1)S(1)}, f32[256,128]{1,0:T(8,128)S(1)}, f32[40,3072]{1,0:T(8,128)S(1)}) custom-call(bf16[288,256]{1,0:T(8,128)(2,1)S(1)} %get-tuple-element.40.mid, bf16[16,3072]{1,0:T(8,128)(2,1)S(1)} %collective-permute-done.2.left, bf16[16,3072]{1,0:T(8,128)(2,1)S(1)} %collective-permute-done.3.right, ...), custom_call_target="tpu_custom_call" | custom-call | flops 2147483648 | bytes 1048576 | tf_op jit(solution)/shard_map/pallas_call | solution.py:39
  23.1 0.0 copy-start.10
  23.1 29.9 %all_to_all.44 = f32[256,1,128]{2,1,0:T(1,128)S(1)} all-to-all(f32[256,1,128]{2,1,0:T(1,128)S(1)} %bitcast.21), channel_id=1, replica_groups=mesh['row'=8,'col'=32] {'row','col'}, dimensions={0} | all-to-all | bytes 262144 | tf_op jit(solution)/shard_map/all_to_all | solution.py:389
  53.1 0.0 copy-done.11
  53.1 1.6 %shard_map.142 = (bf16[384,512]{1,0:T(8,128)(2,1)S(1)}, f32[256,128]{1,0:T(8,128)S(1)}) custom-call(f32[256,128]{1,0:T(8,128)S(1)} %bitcast.24, bf16[432,512]{1,0:T(8,128)(2,1)S(1)} %get-tuple-element.52.before, bf16[512,512]{1,0:T(8,128)(2,1)S(1)} %shard_map.140.sensor_trunk, f32[40,3072]{1,0:T(8,128)S(1)} %get-tuple-element.54.coarse, ...), custom_call_target="tpu_custom_call" | custom-call | flops 2147483648 | bytes 1048576 | tf_op jit(solution)/shard_map/pallas_call | solution.py:39
  54.6 0.0 copy-start.12
  54.7 18.3 %all_to_all.45 = f32[256,1,128]{2,1,0:T(1,128)S(1)} all-to-all(f32[256,1,128]{2,1,0:T(1,128)S(1)} %bitcast.26), channel_id=1, replica_groups=mesh['row'=8,'col'=32] {'row','col'}, dimensions={0} | all-to-all | bytes 262144 | tf_op jit(solution)/shard_map/all_to_all | solution.py:389
  73.0 0.0 copy-done.10
  73.0 1.5 %shard_map.143 = (bf16[336,512]{1,0:T(8,128)(2,1)S(1)}, f32[256,128]{1,0:T(8,128)S(1)}) custom-call(f32[256,128]{1,0:T(8,128)S(1)} %bitcast.25, bf16[384,512]{1,0:T(8,128)(2,1)S(1)} %get-tuple-element.56.before, bf16[512,512]{1,0:T(8,128)(2,1)S(1)} %shard_map.140.sensor_trunk, f32[40,3072]{1,0:T(8,128)S(1)} %get-tuple-element.54.coarse, ...), custom_call_target="tpu_custom_call" | custom-call | flops 2147483648 | bytes 1048576 | tf_op jit(solution)/shard_map/pallas_call | solution.py:39
  74.4 18.3 %all_to_all.46 = f32[256,1,128]{2,1,0:T(1,128)S(1)} all-to-all(f32[256,1,128]{2,1,0:T(1,128)S(1)} %bitcast.27), channel_id=1, replica_groups=mesh['row'=8,'col'=32] {'row','col'}, dimensions={0} | all-to-all | bytes 262144 | tf_op jit(solution)/shard_map/all_to_all | solution.py:389
  92.8 0.0 copy-done.12
  92.8 1.3 %shard_map.144 = (bf16[192,512]{1,0:T(8,128)(2,1)S(1)}, f32[256,128]{1,0:T(8,128)S(1)}) custom-call(f32[256,128]{1,0:T(8,128)S(1)} %bitcast.22, bf16[336,512]{1,0:T(8,128)(2,1)S(1)} %get-tuple-element.58.before, bf16[512,512]{1,0:T(8,128)(2,1)S(1)} %shard_map.140.sensor_trunk, f32[40,3072]{1,0:T(8,128)S(1)} %get-tuple-element.54.coarse, ...), custom_call_target="tpu_custom_call" | custom-call | flops 2147483648 | bytes 1048576 | tf_op jit(solution)/shard_map/pallas_call | solution.py:39
  94.1 18.5 %all_to_all.47 = f32[256,1,128]{2,1,0:T(1,128)S(1)} all-to-all(f32[256,1,128]{2,1,0:T(1,128)S(1)} %bitcast.23), channel_id=1, replica_groups=mesh['row'=8,'col'=32] {'row','col'}, dimensions={0} | all-to-all | bytes 262144 | tf_op jit(solution)/shard_map/all_to_all | solution.py:389
  112.6 2.3 %shard_map.145 = f32[16,64,768]{2,1,0:T(8,128)} custom-call(f32[256,128]{1,0:T(8,128)S(1)} %bitcast.28, f32[12,3072]{1,0:T(8,128)S(1)} %copy-done.5, bf16[192,512]{1,0:T(8,128)(2,1)S(1)} %get-tuple-element.60.coeffs, bf16[512,4096]{1,0:T(8,128)(2,1)S(1)} %get-tuple-element.46.trunk), custom_call_target="tpu_custom_call" | custom-call | flops 2147483648 | bytes 1048576 | tf_op jit(solution)/shard_map/pallas_call | solution.py:39
Async XLA Ops:
  0.0 1.9 %copy-start.1 = (f32[1024,768]{1,0:T(8,128)S(1)}, f32[1024,768]{1,0:T(8,128)}, u32[]{:S(2)}) copy-start(f32[1024,768]{1,0:T(8,128)} %param.14) | copy-start | bytes 9437188
  1.9 0.9 copy-start.5
  2.5 6.8 %copy-start.2 = (bf16[512,512]{1,0:T(8,128)(2,1)S(1)}, bf16[512,512]{1,0:T(8,128)(2,1)}, u32[]{:S(2)}) copy-start(bf16[512,512]{1,0:T(8,128)(2,1)} %w_sensor.1) | copy-start | bytes 1572868
  2.9 9.4 %collective-permute-start = (bf16[8,3072]{1,0:T(8,128)(2,1)S(1)}, bf16[8,3072]{1,0:T(8,128)(2,1)S(1)}, u32[]{:S(2)}, u32[]{:S(2)}) collective-permute-start(bf16[8,3072]{1,0:T(8,128)(2,1)S(1)} %get-tuple-element.35), channel_id=1, source_target_pairs={{0,32},{32,64},{64,96},{96,128},{128,160},{160,192},{192,224},{1,3... | collective-permute-start | bytes 147464 | tf_op jit(solution)/shard_map/ppermute | solution.py:386
  7.4 5.4 %collective-permute-start.1 = (bf16[8,3072]{1,0:T(8,128)(2,1)S(1)}, bf16[8,3072]{1,0:T(8,128)(2,1)S(1)}, u32[]{:S(2)}, u32[]{:S(2)}) collective-permute-start(bf16[8,3072]{1,0:T(8,128)(2,1)S(1)} %get-tuple-element.36), channel_id=1, source_target_pairs={{32,0},{64,32},{96,64},{128,96},{160,128},{192,160},{224,192},{33,... | collective-permute-start | bytes 147464 | tf_op jit(solution)/shard_map/ppermute | solution.py:386
  12.3 5.3 %copy-start = (bf16[256,512]{1,0:T(8,128)(2,1)S(1)}, bf16[256,512]{1,0:T(8,128)(2,1)}, u32[]{:S(2)}) copy-start(bf16[256,512]{1,0:T(8,128)(2,1)} %constant.10.clone.spread) | copy-start | bytes 786436
  12.9 8.8 %copy-start.3 = (bf16[512,512]{1,0:T(8,128)(2,1)S(1)}, bf16[512,512]{1,0:T(8,128)(2,1)}, u32[]{:S(2)}) copy-start(bf16[512,512]{1,0:T(8,128)(2,1)} %w2.7) | copy-start | bytes 1572868
  12.9 8.8 %copy-start.4 = (bf16[512,512]{1,0:T(8,128)(2,1)S(1)}, bf16[512,512]{1,0:T(8,128)(2,1)}, u32[]{:S(2)}) copy-start(bf16[512,512]{1,0:T(8,128)(2,1)} %w3.7) | copy-start | bytes 1572868
  12.9 8.8 %copy-start.6 = (f32[512]{0:T(512)S(1)}, f32[512]{0:T(512)}, u32[]{:S(2)}) copy-start(f32[512]{0:T(512)} %param.16) | copy-start | bytes 6148
  12.9 8.8 %copy-start.7 = (f32[512]{0:T(512)S(1)}, f32[512]{0:T(512)}, u32[]{:S(2)}) copy-start(f32[512]{0:T(512)} %param.18) | copy-start | bytes 6148
  13.0 8.8 %copy-start.8 = (f32[512]{0:T(512)S(1)}, f32[512]{0:T(512)}, u32[]{:S(2)}) copy-start(f32[512]{0:T(512)} %param.20) | copy-start | bytes 6148
  13.0 8.8 %copy-start.9 = (bf16[16,432]{1,0:T(8,128)(2,1)S(1)}, bf16[16,432]{1,0:T(8,128)(2,1)}, u32[]{:S(2)}) copy-start(bf16[16,432]{1,0:T(8,128)(2,1)} %constant.11.clone.pool) | copy-start | bytes 41476
  13.0 6.4 %collective-permute-start.2 = (bf16[16,3072]{1,0:T(8,128)(2,1)S(1)}, bf16[16,3072]{1,0:T(8,128)(2,1)S(1)}, u32[]{:S(2)}, u32[]{:S(2)}) collective-permute-start(bf16[16,3072]{1,0:T(8,128)(2,1)S(1)} %get-tuple-element.44), channel_id=1, source_target_pairs={{0,1},{1,2},{2,3},{3,4},{4,5},{5,6},{6,7},{7,8},{8,9},{9,10},{10,1... | collective-permute-start | bytes 294920 | tf_op jit(solution)/shard_map/ppermute | solution.py:386
  16.3 5.4 %collective-permute-start.3 = (bf16[16,3072]{1,0:T(8,128)(2,1)S(1)}, bf16[16,3072]{1,0:T(8,128)(2,1)S(1)}, u32[]{:S(2)}, u32[]{:S(2)}) collective-permute-start(bf16[16,3072]{1,0:T(8,128)(2,1)S(1)} %get-tuple-element.45), channel_id=1, source_target_pairs={{1,0},{2,1},{3,2},{4,3},{5,4},{6,5},{7,6},{8,7},{9,8},{10,9},{11,1... | collective-permute-start | bytes 294920 | tf_op jit(solution)/shard_map/ppermute | solution.py:386
  19.3 33.8 %copy-start.11 = (bf16[16,384]{1,0:T(8,128)(2,1)S(1)}, bf16[16,384]{1,0:T(8,128)(2,1)}, u32[]{:S(2)}) copy-start(bf16[16,384]{1,0:T(8,128)(2,1)} %constant.12.clone.pool) | copy-start | bytes 36868
  23.1 49.8 %copy-start.10 = (bf16[16,336]{1,0:T(8,128)(2,1)S(1)}, bf16[16,336]{1,0:T(8,128)(2,1)}, u32[]{:S(2)}) copy-start(bf16[16,336]{1,0:T(8,128)(2,1)} %constant.13.clone.pool) | copy-start | bytes 32260
  54.6 38.1 %copy-start.12 = (bf16[16,192]{1,0:T(8,128)(2,1)S(1)}, bf16[16,192]{1,0:T(8,128)(2,1)}, u32[]{:S(2)}) copy-start(bf16[16,192]{1,0:T(8,128)(2,1)} %constant.14.clone.pool) | copy-start | bytes 18436

commit v5 on v4

--- a/solution.py
+++ b/solution.py
@@ -109,9 +109,8 @@
         target[...] = packed[...].astype(BF16)
 
 
-def columns_kernel(na, nb, row_part, col_part, above, below, coarse, both, left, right, tall, packed):
+def columns_kernel(na, nb, row_part, col_part, above, below, both, left, right, tall, packed):
     height, values = na + 2 * HALO, 4 * TILE
-    kx, ky = na // PER_CELL, nb // PER_CELL
     over, under = above[...].astype(F32), below[...].astype(F32)
     for b in range(nb):
         at = b * height
@@ -120,17 +119,12 @@
         tall[at + HALO : at + HALO + na, LANES : 2 * LANES] = col_part[b * na : (b + 1) * na, :]
         tall[at + HALO + na : at + height, :] = under[0:HALO, b * values : (b + 1) * values]
     both[...] = tall[...].astype(BF16)
-    packed[...] = jnp.zeros(packed.shape, F32)
-    for target, first, j in ((left, 0, 0), (right, nb - HALO, ky - 1)):
+    for target, first in ((left, 0), (right, nb - HALO)):
         for b in range(HALO):
             for g in range(height // 8):
                 lanes = slice((b * (height // 8) + g) * values, (b * (height // 8) + g + 1) * values)
                 at = (first + b) * height + 8 * g
-                packed[0:8, lanes] = tall[at : at + 8, :]
-        packed[8:9, :] = over[HALO + j : HALO + j + 1, :]
-        for i in range(kx):
-            packed[9 + i : 10 + i, :] = coarse[i * ky + j : i * ky + j + 1, :]
-        packed[9 + kx : 10 + kx, :] = under[HALO + j : HALO + j + 1, :]
+                packed[:, lanes] = tall[at : at + 8, :]
         target[...] = packed[...].astype(BF16)
 
 
@@ -154,7 +148,15 @@
         mean_trunk[rows, :] = dot(trunk[rows, :], share)
 
 
-def sensor_trunk_kernel(trunk, spread, sensor_trunk):
+def sensor_trunk_kernel(kx, ky, trunk, spread, above, below, coarse, sensor_trunk, left, right, packed):
+    over, under = above[...].astype(F32), below[...].astype(F32)
+    packed[...] = jnp.zeros(packed.shape, F32)
+    for target, j in ((left, 0), (right, ky - 1)):
+        packed[0:1, :] = over[HALO + j : HALO + j + 1, :]
+        for i in range(kx):
+            packed[1 + i : 2 + i, :] = coarse[i * ky + j : i * ky + j + 1, :]
+        packed[1 + kx : 2 + kx, :] = under[HALO + j : HALO + j + 1, :]
+        target[...] = packed[...].astype(BF16)
     width = 1024
     per = width // TILE
     point = lax.broadcasted_iota(jnp.int32, (width, LANES), 0)
@@ -236,35 +238,46 @@
 
 
 def first_kernel(
-    na, nb, cells, mid, left, right, above, below, c_own, spread, w1, b1, w2, b2, w3, b3, pool, mean_trunk,
-    coeffs, payload, coarse, sensors, tiles,
+    na, nb, cells, mid, left, right, spread, w1, b1, w2, b2, w3, b3, pool, mean_trunk,
+    coeffs, payload, sensors, tiles,
 ):
     height, values = na + 2 * HALO, 4 * TILE
     side = HALO * height
     wide = nb * height
     tiles[side : side + wide, :] = mid[...].astype(F32)
-    edge = [x[...].astype(F32) for x in (above, below, left, right)]
-    for lines, first in ((edge[2], 0), (edge[3], side + wide)):
+    for source, first in ((left, 0), (right, side + wide)):
+        lines = source[...].astype(F32)
         for g in range(side // 8):
-            tiles[first + 8 * g : first + 8 * (g + 1), :] = lines[0:8, g * values : (g + 1) * values]
+            tiles[first + 8 * g : first + 8 * (g + 1), :] = lines[:, g * values : (g + 1) * values]
     zero_ends(sensors)
     sensors[8 : 8 + 2 * side + wide, :] = dot(tiles[...].astype(BF16), spread[...])
     vectors = sensor_vectors(sensors, 8 + height, coeffs.shape[0])
     result = branch(vectors, w1, b1, w2, b2, w3, b3)
     coeffs[...] = result
     send_means(result, pool, mean_trunk, lax.axis_index("col"), cells, payload)
-    kx, ky = na // PER_CELL, nb // PER_CELL
-    coarse[0 : kx + 2, :] = edge[2][8 : 10 + kx, :]
-    coarse[8 * (ky + 1) : 8 * (ky + 1) + kx + 2, :] = edge[3][8 : 10 + kx, :]
+
+
+def gather_coarse(kx, ky, c_own, above, below, left, right, coarse):
+    edge = [x[...].astype(F32) for x in (above, below, left, right)]
+    coarse[0:8, :] = edge[2]
+    coarse[8 * (ky + 1) : 8 * (ky + 2), :] = edge[3]
     for j in range(ky):
         at = 8 * (j + 1)
         coarse[at : at + 1, :] = edge[0][HALO + j : HALO + j + 1, :]
         for i in range(kx):
             coarse[at + 1 + i : at + 2 + i, :] = c_own[i * ky + j : i * ky + j + 1, :]
         coarse[at + 1 + kx : at + 2 + kx, :] = edge[1][HALO + j : HALO + j + 1, :]
-    for j in range(ky + 2):
-        at = 8 * j + kx + 2
-        coarse[at : 8 * (j + 1), :] = jnp.zeros((6 - kx, coarse.shape[1]), F32)
+        coarse[at + kx + 2 : at + 8, :] = jnp.zeros((6 - kx, coarse.shape[1]), F32)
+
+
+def second_kernel(
+    na, nb, n_row, n_col, cells, c_own, above, below, left, right, gathered, before, sensor_trunk, *rest
+):
+    *net, coeffs, payload, coarse, sensors, lines = rest
+    gather_coarse(na // PER_CELL, nb // PER_CELL, c_own, above, below, left, right, coarse)
+    next_kernel(
+        2, na, nb, n_row, n_col, cells, gathered, before, sensor_trunk, coarse, *net, coeffs, payload, sensors, lines
+    )
 
 
 def next_kernel(
@@ -420,13 +433,12 @@
     above, below, w_first = lax.optimization_barrier((above, below, w_first))
     mid, to_left, to_right = call(
         part(columns_kernel, na, nb),
-        (shape((nb * height, tile_values), BF16), shape((16, total), BF16), shape((16, total), BF16)),
+        (shape((nb * height, tile_values), BF16), shape((8, total), BF16), shape((8, total), BF16)),
         row_part,
         col_part,
         above,
         below,
-        coarse_matrix,
-        scratch=[pltpu.VMEM((nb * height, tile_values), F32), pltpu.VMEM((16, total), F32)],
+        scratch=[pltpu.VMEM((nb * height, tile_values), F32), pltpu.VMEM((8, total), F32)],
     )
     to_left, to_right, mean_trunk = lax.optimization_barrier((to_left, to_right, mean_trunk))
     left, right = shift(to_right, "col", True), shift(to_left, "col", False)
@@ -440,47 +452,71 @@
         bias_latent.reshape(1, latent),
     )
 
-    sensor_trunk = call(
-        sensor_trunk_kernel, shape((latent, places), BF16), trunk, spread, flops=1 << 30
-    )
-    left, right, sensor_trunk = lax.optimization_barrier((left, right, sensor_trunk))
+    sensor_trunk, c_to_left, c_to_right = call(
+        part(sensor_trunk_kernel, kx, ky),
+        (shape((latent, places), BF16), shape((8, total), BF16), shape((8, total), BF16)),
+        trunk,
+        spread,
+        above,
+        below,
+        coarse_matrix,
+        scratch=[pltpu.VMEM((8, total), F32)],
+        flops=1 << 30,
+    )
+    mid, c_to_left, c_to_right = lax.optimization_barrier((mid, c_to_left, c_to_right))
+    c_left, c_right = shift(c_to_right, "col", True), shift(c_to_left, "col", False)
 
     def region(k):
         return (nb + 2 * HALO - 2 * k) * height
 
     payload_shape = shape((devices, LANES), F32)
-    coeffs, payload, coarse = call(
+    coeffs, payload = call(
         part(first_kernel, na, nb, cells),
-        (shape((region(1), latent), BF16), payload_shape, shape((8 * (ky + 2), total), F32)),
+        (shape((region(1), latent), BF16), payload_shape),
         mid,
         left,
         right,
-        above,
-        below,
-        coarse_matrix,
         spread,
         *net,
         pool_matrix(na, nb, 1, False),
         mean_trunk,
         scratch=[pltpu.VMEM((region(0) + 16, places), F32), pltpu.VMEM((region(0), tile_values), F32)],
     )
+    coarse = None
     for k in range(2, ITERS + 1):
         gathered = exchange(payload)
-        coeffs, payload = call(
-            part(next_kernel, k, na, nb, n_row, n_col, cells),
-            (shape((region(k) if k < ITERS else nb * na, latent), BF16), payload_shape),
-            gathered,
-            coeffs,
-            sensor_trunk,
-            coarse,
-            *net,
-            pool_matrix(na, nb, k, k == ITERS),
-            mean_trunk,
-            scratch=[
-                pltpu.VMEM((region(k - 1) + 16, places), F32),
-                pltpu.VMEM(((ky + 2) * height, places), F32),
-            ],
-        )
+        rest = (*net, pool_matrix(na, nb, k, k == ITERS), mean_trunk)
+        shapes = (shape((region(k) if k < ITERS else nb * na, latent), BF16), payload_shape)
+        scratch = [
+            pltpu.VMEM((region(k - 1) + 16, places), F32),
+            pltpu.VMEM(((ky + 2) * height, places), F32),
+        ]
+        if k == 2:
+            coeffs, payload, coarse = call(
+                part(second_kernel, na, nb, n_row, n_col, cells),
+                (*shapes, shape((8 * (ky + 2), total), F32)),
+                coarse_matrix,
+                above,
+                below,
+                c_left,
+                c_right,
+                gathered,
+                coeffs,
+                sensor_trunk,
+                *rest,
+                scratch=scratch,
+            )
+        else:
+            coeffs, payload = call(
+                part(next_kernel, k, na, nb, n_row, n_col, cells),
+                shapes,
+                gathered,
+                coeffs,
+                sensor_trunk,
+                coarse,
+                *rest,
+                scratch=scratch,
+            )
     gathered = exchange(payload)
     steps = 8
     out = call(

time: 115 us -> 123 us (1.070)
  blocking collectives: 85 us -> 62 us
  starting transfers between devices: 11.1 us -> 33.5 us
  waiting for transfers between devices: 2.83 us -> 10.1 us
    all_to_all x4 -> x3, blocking collectives: 85 us -> 62 us  [exchange(): return lax.all_to_all(x, ('row', 'col'), 0, 0, tiled=True)]
    all_to_all x0 -> x1, starting transfers between devices: none -> 17.5 us  [exchange(): return lax.all_to_all(x, ('row', 'col'), 0, 0, tiled=True)]
    ppermute x4 -> x6, starting transfers between devices: 11.1 us -> 15.9 us  [shift(): return lax.ppermute(x, axis, pairs)]
    all_to_all x0 -> x1, waiting for transfers between devices: none -> 3.91 us  [exchange(): return lax.all_to_all(x, ('row', 'col'), 0, 0, tiled=True)]
    ppermute x4 -> x6, waiting for transfers between devices: 2.83 us -> 6.23 us  [shift(): return lax.ppermute(x, axis, pairs)]
  transfers between devices with their start and end apart: 4 -> 7, of which waited for: 2 -> 4; matrix products, arithmetic and copies ran while one was open for 0% -> 0% of each run, Pallas kernels for 4% -> 4%
where the time goes in v5:
time: 123 us; the launch traced here: 122 us
  blocking collectives  62 us (50%)
  starting transfers between devices  33.5 us (27%)
  Pallas kernels  14.3 us (12%)
  waiting for transfers between devices  10.1 us (8%)
  local copies, waits for them, and re-layouts  2.01 us (2%)
    all_to_all x3, blocking collectives, exchange(): return lax.all_to_all(x, ('row', 'col'), 0, 0, tiled=True)  62 us
    all_to_all x1, starting transfers between devices, exchange(): return lax.all_to_all(x, ('row', 'col'), 0, 0, tiled=True)  17.5 us
    ppermute x6, starting transfers between devices, shift(): return lax.ppermute(x, axis, pairs)  15.9 us
    pallas_call x10, Pallas kernels, call(): pl.pallas_call(kernel, out_shape=out_shape, in_specs=in_specs or [whole]...  14.3 us
    ppermute x6, waiting for transfers between devices, shift(): return lax.ppermute(x, axis, pairs)  6.23 us
    all_to_all x1, waiting for transfers between devices, exchange(): return lax.all_to_all(x, ('row', 'col'), 0, 0, tiled=True)  3.91 us
  transfers between devices with their start and end apart: 7, of which 4 were waited for; matrix products, arithmetic and copies ran while one was open for 0% of the time, Pallas kernels for 4%

profile of v5, /device:TPU:1, one launch (start us, length us, event | category | flops | bytes accessed | tf_op | source)
XLA Modules:
  0.0 122.4 jit_solution(16091990858841425085)
XLA Ops:
  0.0 0.0 copy-start.3
  0.0 0.0 copy-start.4
  0.0 1.9 %copy-done.4 = f32[1024,768]{1,0:T(8,128)S(1)} copy-done((f32[1024,768]{1,0:T(8,128)S(1)}, f32[1024,768]{1,0:T(8,128)}, u32[]{:S(2)}) %copy-start.4) | copy-done | bytes 3145752
  1.9 0.6 shard_map.136
  2.6 0.0 copy-start.5
  2.6 0.0 copy-done.3
  2.6 0.1 shard_map.137
  2.7 4.6 %collective-permute-start = (bf16[8,3072]{1,0:T(8,128)(2,1)S(1)}, bf16[8,3072]{1,0:T(8,128)(2,1)S(1)}, u32[]{:S(2)}, u32[]{:S(2)}) collective-permute-start(bf16[8,3072]{1,0:T(8,128)(2,1)S(1)} %get-tuple-element.38), channel_id=1, source_target_pairs={{0,32},{32,64},{64,96},{96,128},{128,160},{160,192},{192,224},{1,3... | collective-permute-start | bytes 147464 | tf_op jit(solution)/shard_map/ppermute | solution.py:399
  7.3 1.9 %collective-permute-start.1 = (bf16[8,3072]{1,0:T(8,128)(2,1)S(1)}, bf16[8,3072]{1,0:T(8,128)(2,1)S(1)}, u32[]{:S(2)}, u32[]{:S(2)}) collective-permute-start(bf16[8,3072]{1,0:T(8,128)(2,1)S(1)} %get-tuple-element.39), channel_id=1, source_target_pairs={{32,0},{64,32},{96,64},{128,96},{160,128},{192,160},{224,192},{33,... | collective-permute-start | bytes 147464 | tf_op jit(solution)/shard_map/ppermute | solution.py:399
  9.3 0.0 copy-done.5
  9.3 2.9 %shard_map.138 = (bf16[512,4096]{1,0:T(8,128)(2,1)S(1)}, f32[512,128]{1,0:T(8,128)S(1)}, bf16[512,512]{1,0:T(8,128)(2,1)S(1)}) custom-call(bf16[512,4096]{1,0:T(8,128)(2,1)} %trunk_hbm.1, bf16[512,512]{1,0:T(8,128)(2,1)S(1)} %copy-done.5), custom_call_target="tpu_custom_call" | custom-call | flops 4294967296 | bytes 1048576 | tf_op jit(solution)/shard_map/pallas_call | solution.py:39
  12.2 0.0 copy-start
  12.2 0.0 copy-start.2
  12.2 0.0 collective-permute-done.above
  12.3 0.5 collective-permute-done.1.below
  12.7 0.1 shard_map.139
  12.8 0.0 copy-start.6
  12.8 0.0 copy-start.7
  12.8 0.0 copy-start.8
  12.8 0.0 copy-start.9
  12.8 0.0 copy-start.10
  12.8 0.0 copy-start.11
  12.9 3.5 %collective-permute-start.4 = (bf16[8,3072]{1,0:T(8,128)(2,1)S(1)}, bf16[8,3072]{1,0:T(8,128)(2,1)S(1)}, u32[]{:S(2)}, u32[]{:S(2)}) collective-permute-start(bf16[8,3072]{1,0:T(8,128)(2,1)S(1)} %get-tuple-element.53), channel_id=1, source_target_pairs={{0,1},{1,2},{2,3},{3,4},{4,5},{5,6},{6,7},{7,8},{8,9},{9,10},{10,1... | collective-permute-start | bytes 147464 | tf_op jit(solution)/shard_map/ppermute | solution.py:399
  16.3 1.3 %collective-permute-start.5 = (bf16[8,3072]{1,0:T(8,128)(2,1)S(1)}, bf16[8,3072]{1,0:T(8,128)(2,1)S(1)}, u32[]{:S(2)}, u32[]{:S(2)}) collective-permute-start(bf16[8,3072]{1,0:T(8,128)(2,1)S(1)} %get-tuple-element.54), channel_id=1, source_target_pairs={{1,0},{2,1},{3,2},{4,3},{5,4},{6,5},{7,6},{8,7},{9,8},{10,9},{11,1... | collective-permute-start | bytes 147464 | tf_op jit(solution)/shard_map/ppermute | solution.py:399
  17.6 0.0 copy-done.2
  17.6 1.7 %shard_map.140 = (bf16[512,512]{1,0:T(8,128)(2,1)S(1)}, bf16[8,3072]{1,0:T(8,128)(2,1)S(1)}, bf16[8,3072]{1,0:T(8,128)(2,1)S(1)}) custom-call(bf16[512,4096]{1,0:T(8,128)(2,1)S(1)} %get-tuple-element.44.trunk, bf16[256,512]{1,0:T(8,128)(2,1)S(1)} %copy-done.2, bf16[8,3072]{1,0:T(8,128)(2,1)S(1)} %collective-permute-done.above, ...), custom_call_target="tpu_custom_call" | custom-call | flops 1073741824 | bytes 1048576 | tf_op jit(solution)/shard_map/pallas_call | solution.py:39
  19.4 0.0 copy-done
  19.4 0.0 copy-start.13
  19.4 0.0 collective-permute-done.4.left
  19.4 1.8 %collective-permute-done.5.right = bf16[8,3072]{1,0:T(8,128)(2,1)S(1)} collective-permute-done((bf16[8,3072]{1,0:T(8,128)(2,1)S(1)}, bf16[8,3072]{1,0:T(8,128)(2,1)S(1)}, u32[]{:S(2)}, u32[]{:S(2)}) %collective-permute-start.5) | collective-permute-done | bytes 49184 | tf_op jit(solution)/shard_map/ppermute | solution.py:399
  21.2 0.0 copy-done.6
  21.2 0.0 copy-done.7
  21.2 0.0 copy-done.8
  21.2 0.0 copy-done.9
  21.2 0.0 copy-done.10
  21.2 0.0 copy-done.11
  21.2 2.1 %shard_map.141 = (bf16[432,512]{1,0:T(8,128)(2,1)S(1)}, f32[256,128]{1,0:T(8,128)}) custom-call(bf16[288,256]{1,0:T(8,128)(2,1)S(1)} %get-tuple-element.49.mid, bf16[8,3072]{1,0:T(8,128)(2,1)S(1)} %collective-permute-done.4.left, bf16[8,3072]{1,0:T(8,128)(2,1)S(1)} %collective-permute-done.5.right, bf16[256,512]{1,0:T(8,128)(2,1)S(1)} %copy-done.2, ...), custom_call_target="tpu_custom_call" | custom-call | flops 2147483648 | bytes 1048576 | tf_op jit(solution)/shard_map/pallas_call | solution.py:39
  23.3 0.0 copy-start.12
  23.3 17.5 %all-to-all-start = ((f32[256,1,128]{2,1,0:T(1,128)}), f32[256,1,128]{2,1,0:T(1,128)S(1)}, u32[]{:S(2)}, u32[]{:S(2)}) async-start(f32[256,1,128]{2,1,0:T(1,128)} %bitcast.5), calls=%async_computation | async-start | bytes 262144 | tf_op jit(solution)/shard_map/all_to_all | solution.py:402
  40.8 3.3 %collective-permute-start.2 = (bf16[8,3072]{1,0:T(8,128)(2,1)S(1)}, bf16[8,3072]{1,0:T(8,128)(2,1)S(1)}, u32[]{:S(2)}, u32[]{:S(2)}) collective-permute-start(bf16[8,3072]{1,0:T(8,128)(2,1)S(1)} %get-tuple-element.47), channel_id=1, source_target_pairs={{0,1},{1,2},{2,3},{3,4},{4,5},{5,6},{6,7},{7,8},{8,9},{9,10},{10,1... | collective-permute-start | bytes 147464 | tf_op jit(solution)/shard_map/ppermute | solution.py:399
  44.1 1.3 %collective-permute-start.3 = (bf16[8,3072]{1,0:T(8,128)(2,1)S(1)}, bf16[8,3072]{1,0:T(8,128)(2,1)S(1)}, u32[]{:S(2)}, u32[]{:S(2)}) collective-permute-start(bf16[8,3072]{1,0:T(8,128)(2,1)S(1)} %get-tuple-element.48), channel_id=1, source_target_pairs={{1,0},{2,1},{3,2},{4,3},{5,4},{6,5},{7,6},{8,7},{9,8},{10,9},{11,1... | collective-permute-start | bytes 147464 | tf_op jit(solution)/shard_map/ppermute | solution.py:399
  45.4 0.0 collective-permute-done.2.left
  45.4 4.0 %collective-permute-done.3.right = bf16[8,3072]{1,0:T(8,128)(2,1)S(1)} collective-permute-done((bf16[8,3072]{1,0:T(8,128)(2,1)S(1)}, bf16[8,3072]{1,0:T(8,128)(2,1)S(1)}, u32[]{:S(2)}, u32[]{:S(2)}) %collective-permute-start.3) | collective-permute-done | bytes 49184 | tf_op jit(solution)/shard_map/ppermute | solution.py:399
  49.4 3.9 %all-to-all-done = f32[256,1,128]{2,1,0:T(1,128)S(1)} async-done(((f32[256,1,128]{2,1,0:T(1,128)}), f32[256,1,128]{2,1,0:T(1,128)S(1)}, u32[]{:S(2)}, u32[]{:S(2)}) %all-to-all-start) | async-done | bytes 131104 | tf_op jit(solution)/shard_map/all_to_all | solution.py:402
  53.3 0.0 copy-done.13
  53.3 1.6 %shard_map.142 = (bf16[384,512]{1,0:T(8,128)(2,1)S(1)}, f32[256,128]{1,0:T(8,128)S(1)}, f32[40,3072]{1,0:T(8,128)S(1)}) custom-call(f32[12,3072]{1,0:T(8,128)S(1)} %copy-done.3, bf16[8,3072]{1,0:T(8,128)(2,1)S(1)} %collective-permute-done.above, bf16[8,3072]{1,0:T(8,128)(2,1)S(1)} %collective-permute-done.1.below, ...), custom_call_target="tpu_custom_call" | custom-call | flops 2147483648 | bytes 1048576 | tf_op jit(solution)/shard_map/pallas_call | solution.py:39
  55.0 0.0 copy-start.14
  55.0 25.0 %all_to_all.44 = f32[256,1,128]{2,1,0:T(1,128)S(1)} all-to-all(f32[256,1,128]{2,1,0:T(1,128)S(1)} %bitcast.22), channel_id=1, replica_groups=mesh['row'=8,'col'=32] {'row','col'}, dimensions={0} | all-to-all | bytes 262144 | tf_op jit(solution)/shard_map/all_to_all | solution.py:402
  79.9 0.0 copy-done.12
  79.9 1.5 %shard_map.143 = (bf16[336,512]{1,0:T(8,128)(2,1)S(1)}, f32[256,128]{1,0:T(8,128)S(1)}) custom-call(f32[256,128]{1,0:T(8,128)S(1)} %bitcast.25, bf16[384,512]{1,0:T(8,128)(2,1)S(1)} %get-tuple-element.61.before, bf16[512,512]{1,0:T(8,128)(2,1)S(1)} %get-tuple-element.59.sensor_trunk, f32[40,3072]{1,0:T(8,128)S(1)} %get-tuple-element.62.coarse, ...), custom_call_target="tpu_custom_call" | custom-call | flops 2147483648 | bytes 1048576 | tf_op jit(solution)/shard_map/pallas_call | solution.py:39
  81.5 0.0 copy-start.1
  81.5 18.6 %all_to_all.45 = f32[256,1,128]{2,1,0:T(1,128)S(1)} all-to-all(f32[256,1,128]{2,1,0:T(1,128)S(1)} %bitcast.26), channel_id=1, replica_groups=mesh['row'=8,'col'=32] {'row','col'}, dimensions={0} | all-to-all | bytes 262144 | tf_op jit(solution)/shard_map/all_to_all | solution.py:402
  100.0 0.0 copy-done.14
  100.0 1.4 %shard_map.144 = (bf16[192,512]{1,0:T(8,128)(2,1)S(1)}, f32[256,128]{1,0:T(8,128)S(1)}) custom-call(f32[256,128]{1,0:T(8,128)S(1)} %bitcast.23, bf16[336,512]{1,0:T(8,128)(2,1)S(1)} %get-tuple-element.64.before, bf16[512,512]{1,0:T(8,128)(2,1)S(1)} %get-tuple-element.59.sensor_trunk, f32[40,3072]{1,0:T(8,128)S(1)} %get-tuple-element.62.coarse, ...), custom_call_target="tpu_custom_call" | custom-call | flops 2147483648 | bytes 1048576 | tf_op jit(solution)/shard_map/pallas_call | solution.py:39
  101.4 18.5 %all_to_all.46 = f32[256,1,128]{2,1,0:T(1,128)S(1)} all-to-all(f32[256,1,128]{2,1,0:T(1,128)S(1)} %bitcast.24), channel_id=1, replica_groups=mesh['row'=8,'col'=32] {'row','col'}, dimensions={0} | all-to-all | bytes 262144 | tf_op jit(solution)/shard_map/all_to_all | solution.py:402
  119.9 0.0 copy-done.1
  119.9 2.3 %shard_map.145 = f32[16,64,768]{2,1,0:T(8,128)} custom-call(f32[256,128]{1,0:T(8,128)S(1)} %bitcast.27, f32[12,3072]{1,0:T(8,128)S(1)} %copy-done.3, bf16[192,512]{1,0:T(8,128)(2,1)S(1)} %get-tuple-element.66.coeffs, bf16[512,4096]{1,0:T(8,128)(2,1)S(1)} %copy-done.1), custom_call_target="tpu_custom_call" | custom-call | flops 2147483648 | bytes 1048576 | tf_op jit(solution)/shard_map/pallas_call | solution.py:39
Async XLA Ops:
  0.0 2.6 %copy-start.3 = (f32[12,3072]{1,0:T(8,128)S(1)}, f32[12,3072]{1,0:T(8,128)}, u32[]{:S(2)}) copy-start(f32[12,3072]{1,0:T(8,128)} %coarse.5) | copy-start | bytes 442372
  0.0 1.9 %copy-start.4 = (f32[1024,768]{1,0:T(8,128)S(1)}, f32[1024,768]{1,0:T(8,128)}, u32[]{:S(2)}) copy-start(f32[1024,768]{1,0:T(8,128)} %param.14) | copy-start | bytes 9437188
  2.6 6.7 %copy-start.5 = (bf16[512,512]{1,0:T(8,128)(2,1)S(1)}, bf16[512,512]{1,0:T(8,128)(2,1)}, u32[]{:S(2)}) copy-start(bf16[512,512]{1,0:T(8,128)(2,1)} %w_sensor.1) | copy-start | bytes 1572868
  2.7 9.6 %collective-permute-start = (bf16[8,3072]{1,0:T(8,128)(2,1)S(1)}, bf16[8,3072]{1,0:T(8,128)(2,1)S(1)}, u32[]{:S(2)}, u32[]{:S(2)}) collective-permute-start(bf16[8,3072]{1,0:T(8,128)(2,1)S(1)} %get-tuple-element.38), channel_id=1, source_target_pairs={{0,32},{32,64},{64,96},{96,128},{128,160},{160,192},{192,224},{1,3... | collective-permute-start | bytes 147464 | tf_op jit(solution)/shard_map/ppermute | solution.py:399
  7.3 5.4 %collective-permute-start.1 = (bf16[8,3072]{1,0:T(8,128)(2,1)S(1)}, bf16[8,3072]{1,0:T(8,128)(2,1)S(1)}, u32[]{:S(2)}, u32[]{:S(2)}) collective-permute-start(bf16[8,3072]{1,0:T(8,128)(2,1)S(1)} %get-tuple-element.39), channel_id=1, source_target_pairs={{32,0},{64,32},{96,64},{128,96},{160,128},{192,160},{224,192},{33,... | collective-permute-start | bytes 147464 | tf_op jit(solution)/shard_map/ppermute | solution.py:399
  12.2 7.2 %copy-start = (bf16[512,4096]{1,0:T(8,128)(2,1)}, bf16[512,4096]{1,0:T(8,128)(2,1)S(1)}, u32[]{:S(2)}) copy-start(bf16[512,4096]{1,0:T(8,128)(2,1)S(1)} %get-tuple-element.44.trunk) | copy-start | bytes 12582916
  12.2 5.4 %copy-start.2 = (bf16[256,512]{1,0:T(8,128)(2,1)S(1)}, bf16[256,512]{1,0:T(8,128)(2,1)}, u32[]{:S(2)}) copy-start(bf16[256,512]{1,0:T(8,128)(2,1)} %constant.10.clone.spread) | copy-start | bytes 786436
  12.8 8.4 %copy-start.6 = (bf16[512,512]{1,0:T(8,128)(2,1)S(1)}, bf16[512,512]{1,0:T(8,128)(2,1)}, u32[]{:S(2)}) copy-start(bf16[512,512]{1,0:T(8,128)(2,1)} %w2.5) | copy-start | bytes 1572868
  12.8 8.4 %copy-start.7 = (bf16[512,512]{1,0:T(8,128)(2,1)S(1)}, bf16[512,512]{1,0:T(8,128)(2,1)}, u32[]{:S(2)}) copy-start(bf16[512,512]{1,0:T(8,128)(2,1)} %w3.5) | copy-start | bytes 1572868
  12.8 8.4 %copy-start.8 = (f32[512]{0:T(512)S(1)}, f32[512]{0:T(512)}, u32[]{:S(2)}) copy-start(f32[512]{0:T(512)} %param.16) | copy-start | bytes 6148
  12.8 8.4 %copy-start.9 = (f32[512]{0:T(512)S(1)}, f32[512]{0:T(512)}, u32[]{:S(2)}) copy-start(f32[512]{0:T(512)} %param.18) | copy-start | bytes 6148
  12.8 8.4 %copy-start.10 = (f32[512]{0:T(512)S(1)}, f32[512]{0:T(512)}, u32[]{:S(2)}) copy-start(f32[512]{0:T(512)} %param.20) | copy-start | bytes 6148
  12.8 8.4 %copy-start.11 = (bf16[16,432]{1,0:T(8,128)(2,1)S(1)}, bf16[16,432]{1,0:T(8,128)(2,1)}, u32[]{:S(2)}) copy-start(bf16[16,432]{1,0:T(8,128)(2,1)} %constant.11.clone.pool) | copy-start | bytes 41476
  12.9 6.5 %collective-permute-start.4 = (bf16[8,3072]{1,0:T(8,128)(2,1)S(1)}, bf16[8,3072]{1,0:T(8,128)(2,1)S(1)}, u32[]{:S(2)}, u32[]{:S(2)}) collective-permute-start(bf16[8,3072]{1,0:T(8,128)(2,1)S(1)} %get-tuple-element.53), channel_id=1, source_target_pairs={{0,1},{1,2},{2,3},{3,4},{4,5},{5,6},{6,7},{7,8},{8,9},{9,10},{10,1... | collective-permute-start | bytes 147464 | tf_op jit(solution)/shard_map/ppermute | solution.py:399
  16.3 4.8 %collective-permute-start.5 = (bf16[8,3072]{1,0:T(8,128)(2,1)S(1)}, bf16[8,3072]{1,0:T(8,128)(2,1)S(1)}, u32[]{:S(2)}, u32[]{:S(2)}) collective-permute-start(bf16[8,3072]{1,0:T(8,128)(2,1)S(1)} %get-tuple-element.54), channel_id=1, source_target_pairs={{1,0},{2,1},{3,2},{4,3},{5,4},{6,5},{7,6},{8,7},{9,8},{10,9},{11,1... | collective-permute-start | bytes 147464 | tf_op jit(solution)/shard_map/ppermute | solution.py:399
  19.4 34.0 %copy-start.13 = (bf16[16,384]{1,0:T(8,128)(2,1)S(1)}, bf16[16,384]{1,0:T(8,128)(2,1)}, u32[]{:S(2)}) copy-start(bf16[16,384]{1,0:T(8,128)(2,1)} %constant.12.clone.rest_6_) | copy-start | bytes 36868
  23.3 56.7 %copy-start.12 = (bf16[16,336]{1,0:T(8,128)(2,1)S(1)}, bf16[16,336]{1,0:T(8,128)(2,1)}, u32[]{:S(2)}) copy-start(bf16[16,336]{1,0:T(8,128)(2,1)} %constant.13.clone.pool) | copy-start | bytes 32260
  23.3 30.1 %all-to-all-start = ((f32[256,1,128]{2,1,0:T(1,128)}), f32[256,1,128]{2,1,0:T(1,128)S(1)}, u32[]{:S(2)}, u32[]{:S(2)}) async-start(f32[256,1,128]{2,1,0:T(1,128)} %bitcast.5), calls=%async_computation | async-start | bytes 262144 | tf_op jit(solution)/shard_map/all_to_all | solution.py:402
  40.8 4.6 %collective-permute-start.2 = (bf16[8,3072]{1,0:T(8,128)(2,1)S(1)}, bf16[8,3072]{1,0:T(8,128)(2,1)S(1)}, u32[]{:S(2)}, u32[]{:S(2)}) collective-permute-start(bf16[8,3072]{1,0:T(8,128)(2,1)S(1)} %get-tuple-element.47), channel_id=1, source_target_pairs={{0,1},{1,2},{2,3},{3,4},{4,5},{5,6},{6,7},{7,8},{8,9},{9,10},{10,1... | collective-permute-start | bytes 147464 | tf_op jit(solution)/shard_map/ppermute | solution.py:399
  44.1 5.3 %collective-permute-start.3 = (bf16[8,3072]{1,0:T(8,128)(2,1)S(1)}, bf16[8,3072]{1,0:T(8,128)(2,1)S(1)}, u32[]{:S(2)}, u32[]{:S(2)}) collective-permute-start(bf16[8,3072]{1,0:T(8,128)(2,1)S(1)} %get-tuple-element.48), channel_id=1, source_target_pairs={{1,0},{2,1},{3,2},{4,3},{5,4},{6,5},{7,6},{8,7},{9,8},{10,9},{11,1... | collective-permute-start | bytes 147464 | tf_op jit(solution)/shard_map/ppermute | solution.py:399
  55.0 45.1 %copy-start.14 = (bf16[16,192]{1,0:T(8,128)(2,1)S(1)}, bf16[16,192]{1,0:T(8,128)(2,1)}, u32[]{:S(2)}) copy-start(bf16[16,192]{1,0:T(8,128)(2,1)} %constant.14.clone.pool) | copy-start | bytes 18436
  81.5 38.4 %copy-start.1 = (bf16[512,4096]{1,0:T(8,128)(2,1)S(1)}, bf16[512,4096]{1,0:T(8,128)(2,1)}, u32[]{:S(2)}) copy-start(bf16[512,4096]{1,0:T(8,128)(2,1)} %copy-done) | copy-start | bytes 12582916

commit v6 on v4

--- a/solution.py
+++ b/solution.py
@@ -109,10 +109,12 @@
         target[...] = packed[...].astype(BF16)
 
 
-def columns_kernel(na, nb, row_part, col_part, above, below, coarse, both, left, right, tall, packed):
+def columns_kernel(na, nb, n_row, row_part, col_part, above, below, coarse, both, first, second, tall, left, right):
     height, values = na + 2 * HALO, 4 * TILE
     kx, ky = na // PER_CELL, nb // PER_CELL
-    over, under = above[...].astype(F32), below[...].astype(F32)
+    row, even = lax.axis_index("row"), lax.axis_index("col") % 2 == 0
+    over = jnp.where(row == 0, 0.0, above[...].astype(F32))
+    under = jnp.where(row == n_row - 1, 0.0, below[...].astype(F32))
     for b in range(nb):
         at = b * height
         tall[at : at + HALO, :] = over[0:HALO, b * values : (b + 1) * values]
@@ -120,18 +122,19 @@
         tall[at + HALO : at + HALO + na, LANES : 2 * LANES] = col_part[b * na : (b + 1) * na, :]
         tall[at + HALO + na : at + height, :] = under[0:HALO, b * values : (b + 1) * values]
     both[...] = tall[...].astype(BF16)
-    packed[...] = jnp.zeros(packed.shape, F32)
-    for target, first, j in ((left, 0, 0), (right, nb - HALO, ky - 1)):
+    for packed, start, j in ((left, 0, 0), (right, nb - HALO, ky - 1)):
+        packed[...] = jnp.zeros(packed.shape, F32)
         for b in range(HALO):
             for g in range(height // 8):
                 lanes = slice((b * (height // 8) + g) * values, (b * (height // 8) + g + 1) * values)
-                at = (first + b) * height + 8 * g
+                at = (start + b) * height + 8 * g
                 packed[0:8, lanes] = tall[at : at + 8, :]
         packed[8:9, :] = over[HALO + j : HALO + j + 1, :]
         for i in range(kx):
             packed[9 + i : 10 + i, :] = coarse[i * ky + j : i * ky + j + 1, :]
         packed[9 + kx : 10 + kx, :] = under[HALO + j : HALO + j + 1, :]
-        target[...] = packed[...].astype(BF16)
+    first[...] = jnp.where(even, right[...], left[...]).astype(BF16)
+    second[...] = jnp.where(even, left[...], right[...]).astype(BF16)
 
 
 def trunk_kernel(blocks, trunk_hbm, w_sensor, trunk, mean_trunk, w_out, arrived):
@@ -236,17 +239,22 @@
 
 
 def first_kernel(
-    na, nb, cells, mid, left, right, above, below, c_own, spread, w1, b1, w2, b2, w3, b3, pool, mean_trunk,
+    na, nb, n_col, cells, mid, first, second, above, below, c_own, spread, w1, b1, w2, b2, w3, b3, pool, mean_trunk,
     coeffs, payload, coarse, sensors, tiles,
 ):
     height, values = na + 2 * HALO, 4 * TILE
     side = HALO * height
     wide = nb * height
     tiles[side : side + wide, :] = mid[...].astype(F32)
-    edge = [x[...].astype(F32) for x in (above, below, left, right)]
-    for lines, first in ((edge[2], 0), (edge[3], side + wide)):
+    col = lax.axis_index("col")
+    even = col % 2 == 0
+    one, other = first[...].astype(F32), second[...].astype(F32)
+    left = jnp.where(col == 0, 0.0, jnp.where(even, other, one))
+    right = jnp.where(col == n_col - 1, 0.0, jnp.where(even, one, other))
+    edge = [above[...].astype(F32), below[...].astype(F32), left, right]
+    for lines, start in ((left, 0), (right, side + wide)):
         for g in range(side // 8):
-            tiles[first + 8 * g : first + 8 * (g + 1), :] = lines[0:8, g * values : (g + 1) * values]
+            tiles[start + 8 * g : start + 8 * (g + 1), :] = lines[0:8, g * values : (g + 1) * values]
     zero_ends(sensors)
     sensors[8 : 8 + 2 * side + wide, :] = dot(tiles[...].astype(BF16), spread[...])
     vectors = sensor_vectors(sensors, 8 + height, coeffs.shape[0])
@@ -380,10 +388,12 @@
     shape = jax.ShapeDtypeStruct
     part = functools.partial
 
-    def shift(x, axis, forward):
-        count = lax.axis_size(axis)
-        pairs = [(i, i + 1) if forward else (i + 1, i) for i in range(count - 1)]
-        return lax.ppermute(x, axis, pairs)
+    def shift(x, step):
+        return lax.ppermute(x, "row", [(i, (i + step) % n_row) for i in range(n_row)])
+
+    def swap(x, parity):
+        pairs = [(i, (i + 1 if i % 2 == parity else i - 1) % n_col) for i in range(n_col)]
+        return lax.ppermute(x, "col", pairs)
 
     def exchange(x):
         return lax.all_to_all(x, ("row", "col"), 0, 0, tiled=True)
@@ -407,7 +417,7 @@
         coarse_matrix,
         scratch=[pltpu.VMEM((8, total), F32)],
     )
-    above, below = shift(down, "row", True), shift(up, "row", False)
+    above, below = shift(down, 1), shift(up, -1)
     trunk, mean_trunk, w_first = call(
         part(trunk_kernel, blocks),
         (shape(trunk_basis.shape, BF16), shape((latent, LANES), F32), shape(w_sensor.shape, BF16)),
@@ -418,18 +428,17 @@
         flops=1 << 32,
     )
     above, below, w_first = lax.optimization_barrier((above, below, w_first))
-    mid, to_left, to_right = call(
-        part(columns_kernel, na, nb),
+    mid, first, second = call(
+        part(columns_kernel, na, nb, n_row),
         (shape((nb * height, tile_values), BF16), shape((16, total), BF16), shape((16, total), BF16)),
         row_part,
         col_part,
         above,
         below,
         coarse_matrix,
-        scratch=[pltpu.VMEM((nb * height, tile_values), F32), pltpu.VMEM((16, total), F32)],
-    )
-    to_left, to_right, mean_trunk = lax.optimization_barrier((to_left, to_right, mean_trunk))
-    left, right = shift(to_right, "col", True), shift(to_left, "col", False)
+        scratch=[pltpu.VMEM((nb * height, tile_values), F32)] + [pltpu.VMEM((16, total), F32)] * 2,
+    )
+    second, first = swap(second, 1), swap(first, 0)
 
     net = (
         w_first,
@@ -443,18 +452,18 @@
     sensor_trunk = call(
         sensor_trunk_kernel, shape((latent, places), BF16), trunk, spread, flops=1 << 30
     )
-    left, right, sensor_trunk = lax.optimization_barrier((left, right, sensor_trunk))
+    mid, sensor_trunk = lax.optimization_barrier((mid, sensor_trunk))
 
     def region(k):
         return (nb + 2 * HALO - 2 * k) * height
 
     payload_shape = shape((devices, LANES), F32)
     coeffs, payload, coarse = call(
-        part(first_kernel, na, nb, cells),
+        part(first_kernel, na, nb, n_col, cells),
         (shape((region(1), latent), BF16), payload_shape, shape((8 * (ky + 2), total), F32)),
         mid,
-        left,
-        right,
+        first,
+        second,
         above,
         below,
         coarse_matrix,

time: 115 us -> 107 us (0.930)
  blocking collectives: 85 us -> 78.5 us
  waiting for transfers between devices: 2.83 us -> 0.3 us
    all_to_all x4, blocking collectives: 85 us -> 78.5 us  [exchange(): return lax.all_to_all(x, ('row', 'col'), 0, 0, tiled=True)]
    ppermute x4, waiting for transfers between devices: 2.83 us -> 0.3 us  [the longest x2 0.3 us: swap(): return lax.ppermute(x, 'col', pairs)]
  transfers between devices with their start and end apart: 4 -> 4, of which waited for: 2 -> 1; matrix products, arithmetic and copies ran while one was open for 0% -> 0% of each run, Pallas kernels for 4% -> 4%
where the time goes in v6:
time: 107 us
  blocking collectives  78.5 us (73%)
  Pallas kernels  13.6 us (13%)
  starting transfers between devices  11.7 us (11%)
  local copies, waits for them, and re-layouts  2.22 us (2%)
    all_to_all x4, blocking collectives, exchange(): return lax.all_to_all(x, ('row', 'col'), 0, 0, tiled=True)  78.5 us
    pallas_call x10, Pallas kernels, call(): pl.pallas_call(kernel, out_shape=out_shape, in_specs=in_specs or [whole]...  13.6 us
    ppermute x2, starting transfers between devices, swap(): return lax.ppermute(x, 'col', pairs)  8.43 us
    ppermute x2, starting transfers between devices, shift(): lax.ppermute(x, 'row', [(i, (i + step) % n_row) for i in range(n_row)])  3.27 us
    unnamed x26, local copies, waits for them, and re-layouts  2.22 us
  transfers between devices with their start and end apart: 4, of which 1 were waited for; matrix products, arithmetic and copies ran while one was open for 0% of the time, Pallas kernels for 4%

profile of v6, /device:TPU:1, one launch (start us, length us, event | category | flops | bytes accessed | tf_op | source)
XLA Modules:
  0.0 106.7 jit_solution(2521826479485323528)
XLA Ops:
  0.0 0.0 copy-start.1
  0.0 1.9 %copy-done.1 = f32[1024,768]{1,0:T(8,128)S(1)} copy-done((f32[1024,768]{1,0:T(8,128)S(1)}, f32[1024,768]{1,0:T(8,128)}, u32[]{:S(2)}) %copy-start.1) | copy-done | bytes 3145752
  1.9 0.0 copy-start.5
  1.9 0.6 shard_map.136
  2.5 0.0 copy-start.2
  2.6 0.3 copy-done.5
  2.8 0.1 shard_map.137
  2.9 2.6 %collective-permute-start = (bf16[8,3072]{1,0:T(8,128)(2,1)S(1)}, bf16[8,3072]{1,0:T(8,128)(2,1)S(1)}, u32[]{:S(2)}, u32[]{:S(2)}) collective-permute-start(bf16[8,3072]{1,0:T(8,128)(2,1)S(1)} %get-tuple-element.31), channel_id=1, source_target_pairs={{0,32},{32,64},{64,96},{96,128},{128,160},{160,192},{192,224},{224... | collective-permute-start | bytes 147464 | tf_op jit(solution)/shard_map/ppermute | solution.py:392
  5.5 0.7 collective-permute-start.1
  6.1 0.0 copy-done.2
  6.2 3.0 %shard_map.138 = (bf16[512,4096]{1,0:T(8,128)(2,1)S(1)}, f32[512,128]{1,0:T(8,128)S(1)}, bf16[512,512]{1,0:T(8,128)(2,1)S(1)}) custom-call(bf16[512,4096]{1,0:T(8,128)(2,1)} %trunk_hbm.1, bf16[512,512]{1,0:T(8,128)(2,1)S(1)} %copy-done.2), custom_call_target="tpu_custom_call" | custom-call | flops 4294967296 | bytes 1048576 | tf_op jit(solution)/shard_map/pallas_call | solution.py:39
  9.1 0.0 copy-start
  9.1 0.0 collective-permute-done.above
  9.1 0.0 collective-permute-done.1.below
  9.1 0.1 shard_map.139
  9.3 0.0 copy-start.3
  9.3 0.0 copy-start.4
  9.3 0.0 copy-start.6
  9.3 0.0 copy-start.7
  9.3 0.0 copy-start.8
  9.4 0.0 copy-start.9
  9.4 1.2 %collective-permute-start.2 = (bf16[16,3072]{1,0:T(8,128)(2,1)S(1)}, bf16[16,3072]{1,0:T(8,128)(2,1)S(1)}, u32[]{:S(2)}, u32[]{:S(2)}) collective-permute-start(bf16[16,3072]{1,0:T(8,128)(2,1)S(1)} %get-tuple-element.39), channel_id=1, source_target_pairs={{0,1},{1,0},{2,3},{3,2},{4,5},{5,4},{6,7},{7,6},{8,9},{9,8},{10,11... | collective-permute-start | bytes 294920 | tf_op jit(solution)/shard_map/ppermute | solution.py:396
  10.6 7.2 %collective-permute-start.3 = (bf16[16,3072]{1,0:T(8,128)(2,1)S(1)}, bf16[16,3072]{1,0:T(8,128)(2,1)S(1)}, u32[]{:S(2)}, u32[]{:S(2)}) collective-permute-start(bf16[16,3072]{1,0:T(8,128)(2,1)S(1)} %get-tuple-element.40), channel_id=1, source_target_pairs={{0,31},{1,2},{2,1},{3,4},{4,3},{5,6},{6,5},{7,8},{8,7},{9,10},{10,... | collective-permute-start | bytes 294920 | tf_op jit(solution)/shard_map/ppermute | solution.py:396
  17.8 0.0 copy-done
  17.8 1.7 %shard_map.140.sensor_trunk = bf16[512,512]{1,0:T(8,128)(2,1)S(1)} custom-call(bf16[512,4096]{1,0:T(8,128)(2,1)S(1)} %get-tuple-element.37.trunk, bf16[256,512]{1,0:T(8,128)(2,1)S(1)} %copy-done), custom_call_target="tpu_custom_call" | custom-call | flops 1073741824 | bytes 1048576 | tf_op jit(solution)/shard_map/pallas_call | solution.py:39
  19.5 0.0 copy-start.11
  19.5 0.0 collective-permute-done.2.first
  19.5 0.3 collective-permute-done.3.second
  19.8 0.0 copy-done.3
  19.8 0.0 copy-done.4
  19.8 0.0 copy-done.6
  19.8 0.0 copy-done.7
  19.8 0.0 copy-done.8
  19.8 0.0 copy-done.9
  19.8 1.4 %shard_map.141 = (bf16[432,512]{1,0:T(8,128)(2,1)S(1)}, f32[256,128]{1,0:T(8,128)S(1)}, f32[40,3072]{1,0:T(8,128)S(1)}) custom-call(bf16[288,256]{1,0:T(8,128)(2,1)S(1)} %get-tuple-element.38.mid, bf16[16,3072]{1,0:T(8,128)(2,1)S(1)} %collective-permute-done.2.first, bf16[16,3072]{1,0:T(8,128)(2,1)S(1)} %collective-permute-done.3.second, ...), custom_call_target="tpu_custom_call" | custom-call | flops 2147483648 | bytes 1048576 | tf_op jit(solution)/shard_map/pallas_call | solution.py:39
  21.3 0.0 copy-start.10
  21.3 23.6 %all_to_all.44 = f32[256,1,128]{2,1,0:T(1,128)S(1)} all-to-all(f32[256,1,128]{2,1,0:T(1,128)S(1)} %bitcast.21), channel_id=1, replica_groups=mesh['row'=8,'col'=32] {'row','col'}, dimensions={0} | all-to-all | bytes 262144 | tf_op jit(solution)/shard_map/all_to_all | solution.py:399
  44.9 0.0 copy-done.11
  44.9 1.6 %shard_map.142 = (bf16[384,512]{1,0:T(8,128)(2,1)S(1)}, f32[256,128]{1,0:T(8,128)S(1)}) custom-call(f32[256,128]{1,0:T(8,128)S(1)} %bitcast.24, bf16[432,512]{1,0:T(8,128)(2,1)S(1)} %get-tuple-element.44.before, bf16[512,512]{1,0:T(8,128)(2,1)S(1)} %shard_map.140.sensor_trunk, f32[40,3072]{1,0:T(8,128)S(1)} %get-tuple-element.46.coarse, ...), custom_call_target="tpu_custom_call" | custom-call | flops 2147483648 | bytes 1048576 | tf_op jit(solution)/shard_map/pallas_call | solution.py:39
  46.5 0.0 copy-start.12
  46.5 18.3 %all_to_all.45 = f32[256,1,128]{2,1,0:T(1,128)S(1)} all-to-all(f32[256,1,128]{2,1,0:T(1,128)S(1)} %bitcast.26), channel_id=1, replica_groups=mesh['row'=8,'col'=32] {'row','col'}, dimensions={0} | all-to-all | bytes 262144 | tf_op jit(solution)/shard_map/all_to_all | solution.py:399
  64.7 0.0 copy-done.10
  64.8 1.5 %shard_map.143 = (bf16[336,512]{1,0:T(8,128)(2,1)S(1)}, f32[256,128]{1,0:T(8,128)S(1)}) custom-call(f32[256,128]{1,0:T(8,128)S(1)} %bitcast.25, bf16[384,512]{1,0:T(8,128)(2,1)S(1)} %get-tuple-element.48.before, bf16[512,512]{1,0:T(8,128)(2,1)S(1)} %shard_map.140.sensor_trunk, f32[40,3072]{1,0:T(8,128)S(1)} %get-tuple-element.46.coarse, ...), custom_call_target="tpu_custom_call" | custom-call | flops 2147483648 | bytes 1048576 | tf_op jit(solution)/shard_map/pallas_call | solution.py:39
  66.2 18.3 %all_to_all.46 = f32[256,1,128]{2,1,0:T(1,128)S(1)} all-to-all(f32[256,1,128]{2,1,0:T(1,128)S(1)} %bitcast.27), channel_id=1, replica_groups=mesh['row'=8,'col'=32] {'row','col'}, dimensions={0} | all-to-all | bytes 262144 | tf_op jit(solution)/shard_map/all_to_all | solution.py:399
  84.5 0.0 copy-done.12
  84.5 1.4 %shard_map.144 = (bf16[192,512]{1,0:T(8,128)(2,1)S(1)}, f32[256,128]{1,0:T(8,128)S(1)}) custom-call(f32[256,128]{1,0:T(8,128)S(1)} %bitcast.22, bf16[336,512]{1,0:T(8,128)(2,1)S(1)} %get-tuple-element.50.before, bf16[512,512]{1,0:T(8,128)(2,1)S(1)} %shard_map.140.sensor_trunk, f32[40,3072]{1,0:T(8,128)S(1)} %get-tuple-element.46.coarse, ...), custom_call_target="tpu_custom_call" | custom-call | flops 2147483648 | bytes 1048576 | tf_op jit(solution)/shard_map/pallas_call | solution.py:39
  85.9 18.3 %all_to_all.47 = f32[256,1,128]{2,1,0:T(1,128)S(1)} all-to-all(f32[256,1,128]{2,1,0:T(1,128)S(1)} %bitcast.23), channel_id=1, replica_groups=mesh['row'=8,'col'=32] {'row','col'}, dimensions={0} | all-to-all | bytes 262144 | tf_op jit(solution)/shard_map/all_to_all | solution.py:399
  104.2 2.3 %shard_map.145 = f32[16,64,768]{2,1,0:T(8,128)} custom-call(f32[256,128]{1,0:T(8,128)S(1)} %bitcast.28, f32[12,3072]{1,0:T(8,128)S(1)} %copy-done.5, bf16[192,512]{1,0:T(8,128)(2,1)S(1)} %get-tuple-element.52.coeffs, bf16[512,4096]{1,0:T(8,128)(2,1)S(1)} %get-tuple-element.37.trunk), custom_call_target="tpu_custom_call" | custom-call | flops 2147483648 | bytes 1048576 | tf_op jit(solution)/shard_map/pallas_call | solution.py:39
Async XLA Ops:
  0.0 1.9 %copy-start.1 = (f32[1024,768]{1,0:T(8,128)S(1)}, f32[1024,768]{1,0:T(8,128)}, u32[]{:S(2)}) copy-start(f32[1024,768]{1,0:T(8,128)} %param.14) | copy-start | bytes 9437188
  1.9 0.9 copy-start.5
  2.5 3.6 %copy-start.2 = (bf16[512,512]{1,0:T(8,128)(2,1)S(1)}, bf16[512,512]{1,0:T(8,128)(2,1)}, u32[]{:S(2)}) copy-start(bf16[512,512]{1,0:T(8,128)(2,1)} %w_sensor.1) | copy-start | bytes 1572868
  2.9 6.3 %collective-permute-start = (bf16[8,3072]{1,0:T(8,128)(2,1)S(1)}, bf16[8,3072]{1,0:T(8,128)(2,1)S(1)}, u32[]{:S(2)}, u32[]{:S(2)}) collective-permute-start(bf16[8,3072]{1,0:T(8,128)(2,1)S(1)} %get-tuple-element.31), channel_id=1, source_target_pairs={{0,32},{32,64},{64,96},{96,128},{128,160},{160,192},{192,224},{224... | collective-permute-start | bytes 147464 | tf_op jit(solution)/shard_map/ppermute | solution.py:392
  5.5 3.7 %collective-permute-start.1 = (bf16[8,3072]{1,0:T(8,128)(2,1)S(1)}, bf16[8,3072]{1,0:T(8,128)(2,1)S(1)}, u32[]{:S(2)}, u32[]{:S(2)}) collective-permute-start(bf16[8,3072]{1,0:T(8,128)(2,1)S(1)} %get-tuple-element.32), channel_id=1, source_target_pairs={{0,224},{32,0},{64,32},{96,64},{128,96},{160,128},{192,160},{224,1... | collective-permute-start | bytes 147464 | tf_op jit(solution)/shard_map/ppermute | solution.py:392
  9.1 8.7 %copy-start = (bf16[256,512]{1,0:T(8,128)(2,1)S(1)}, bf16[256,512]{1,0:T(8,128)(2,1)}, u32[]{:S(2)}) copy-start(bf16[256,512]{1,0:T(8,128)(2,1)} %constant.10.clone.spread) | copy-start | bytes 786436
  9.3 10.5 %copy-start.3 = (bf16[512,512]{1,0:T(8,128)(2,1)S(1)}, bf16[512,512]{1,0:T(8,128)(2,1)}, u32[]{:S(2)}) copy-start(bf16[512,512]{1,0:T(8,128)(2,1)} %w2.7) | copy-start | bytes 1572868
  9.3 10.5 %copy-start.4 = (bf16[512,512]{1,0:T(8,128)(2,1)S(1)}, bf16[512,512]{1,0:T(8,128)(2,1)}, u32[]{:S(2)}) copy-start(bf16[512,512]{1,0:T(8,128)(2,1)} %w3.7) | copy-start | bytes 1572868
  9.3 10.5 %copy-start.6 = (f32[512]{0:T(512)S(1)}, f32[512]{0:T(512)}, u32[]{:S(2)}) copy-start(f32[512]{0:T(512)} %param.16) | copy-start | bytes 6148
  9.3 10.5 %copy-start.7 = (f32[512]{0:T(512)S(1)}, f32[512]{0:T(512)}, u32[]{:S(2)}) copy-start(f32[512]{0:T(512)} %param.18) | copy-start | bytes 6148
  9.3 10.5 %copy-start.8 = (f32[512]{0:T(512)S(1)}, f32[512]{0:T(512)}, u32[]{:S(2)}) copy-start(f32[512]{0:T(512)} %param.20) | copy-start | bytes 6148
  9.4 10.5 %copy-start.9 = (bf16[16,432]{1,0:T(8,128)(2,1)S(1)}, bf16[16,432]{1,0:T(8,128)(2,1)}, u32[]{:S(2)}) copy-start(bf16[16,432]{1,0:T(8,128)(2,1)} %constant.11.clone.pool) | copy-start | bytes 41476
  9.4 10.1 %collective-permute-start.2 = (bf16[16,3072]{1,0:T(8,128)(2,1)S(1)}, bf16[16,3072]{1,0:T(8,128)(2,1)S(1)}, u32[]{:S(2)}, u32[]{:S(2)}) collective-permute-start(bf16[16,3072]{1,0:T(8,128)(2,1)S(1)} %get-tuple-element.39), channel_id=1, source_target_pairs={{0,1},{1,0},{2,3},{3,2},{4,5},{5,4},{6,7},{7,6},{8,9},{9,8},{10,11... | collective-permute-start | bytes 294920 | tf_op jit(solution)/shard_map/ppermute | solution.py:396
  10.6 9.2 %collective-permute-start.3 = (bf16[16,3072]{1,0:T(8,128)(2,1)S(1)}, bf16[16,3072]{1,0:T(8,128)(2,1)S(1)}, u32[]{:S(2)}, u32[]{:S(2)}) collective-permute-start(bf16[16,3072]{1,0:T(8,128)(2,1)S(1)} %get-tuple-element.40), channel_id=1, source_target_pairs={{0,31},{1,2},{2,1},{3,4},{4,3},{5,6},{6,5},{7,8},{8,7},{9,10},{10,... | collective-permute-start | bytes 294920 | tf_op jit(solution)/shard_map/ppermute | solution.py:396
  19.5 25.4 %copy-start.11 = (bf16[16,384]{1,0:T(8,128)(2,1)S(1)}, bf16[16,384]{1,0:T(8,128)(2,1)}, u32[]{:S(2)}) copy-start(bf16[16,384]{1,0:T(8,128)(2,1)} %constant.12.clone.pool) | copy-start | bytes 36868
  21.3 43.5 %copy-start.10 = (bf16[16,336]{1,0:T(8,128)(2,1)S(1)}, bf16[16,336]{1,0:T(8,128)(2,1)}, u32[]{:S(2)}) copy-start(bf16[16,336]{1,0:T(8,128)(2,1)} %constant.13.clone.pool) | copy-start | bytes 32260
  46.5 38.1 %copy-start.12 = (bf16[16,192]{1,0:T(8,128)(2,1)S(1)}, bf16[16,192]{1,0:T(8,128)(2,1)}, u32[]{:S(2)}) copy-start(bf16[16,192]{1,0:T(8,128)(2,1)} %constant.14.clone.pool) | copy-start | bytes 18436

commit v7 on v6

--- a/solution.py
+++ b/solution.py
@@ -157,7 +157,8 @@
         mean_trunk[rows, :] = dot(trunk[rows, :], share)
 
 
-def sensor_trunk_kernel(trunk, spread, sensor_trunk):
+def sensor_trunk_kernel(trunk, spread, mean_trunk, sensor_trunk, mean_line):
+    mean_line[...] = jnp.transpose(mean_trunk[...])[0:8, :]
     width = 1024
     per = width // TILE
     point = lax.broadcasted_iota(jnp.int32, (width, LANES), 0)
@@ -199,14 +200,25 @@
     return (dot(hidden, w3[...]) + b3[...]).astype(BF16)
 
 
-def send_means(coeffs, pool, mean_trunk, col, cells, payload):
-    pooled = dot(pool[...], coeffs)
-    means = dot(pooled, mean_trunk[...], precision=lax.Precision.HIGHEST)
-    lane = lax.broadcasted_iota(jnp.int32, means.shape, 1)
-    cell = lax.broadcasted_iota(jnp.int32, means.shape, 0)
-    mine = ((lane - cells * col) & (LANES - 1)) == cell
-    line = jnp.sum(jnp.where(mine, means, 0.0), axis=0, keepdims=True)
-    payload[...] = jnp.broadcast_to(line, payload.shape)
+def send_means(coeffs, columns, na, ky, height, mean_line, col, cells, payload):
+    skip = (height - na) // 2
+    share = mean_line[0:1, :] * (1.0 / PER_CELL**2)
+    lane = lax.broadcasted_iota(jnp.int32, (height, LANES), 1)
+    line = lax.broadcasted_iota(jnp.int32, (height, LANES), 0) - skip
+    inside = (line >= 0) & (line < na)
+    place = jnp.where(inside, (line >> 2) * ky, -LANES)
+    total = None
+    for j in range(ky):
+        tiles = None
+        for b in range(PER_CELL * j, PER_CELL * (j + 1)):
+            at = (b - columns) * height
+            part = coeffs[at : at + height, :].astype(F32)
+            tiles = part if tiles is None else tiles + part
+        sums = jnp.sum(tiles * share, axis=1, keepdims=True)
+        mine = ((lane - cells * col) & (LANES - 1)) == place + j
+        part = jnp.where(mine, sums, 0.0)
+        total = part if total is None else total + part
+    payload[...] = jnp.broadcast_to(jnp.sum(total, axis=0, keepdims=True), payload.shape)
 
 
 def corrections(gathered, coarse, n_row, n_col, cells):
@@ -239,7 +251,7 @@
 
 
 def first_kernel(
-    na, nb, n_col, cells, mid, first, second, above, below, c_own, spread, w1, b1, w2, b2, w3, b3, pool, mean_trunk,
+    na, nb, n_col, cells, mid, first, second, above, below, c_own, spread, w1, b1, w2, b2, w3, b3, mean_line,
     coeffs, payload, coarse, sensors, tiles,
 ):
     height, values = na + 2 * HALO, 4 * TILE
@@ -260,7 +272,7 @@
     vectors = sensor_vectors(sensors, 8 + height, coeffs.shape[0])
     result = branch(vectors, w1, b1, w2, b2, w3, b3)
     coeffs[...] = result
-    send_means(result, pool, mean_trunk, lax.axis_index("col"), cells, payload)
+    send_means(result, 1 - HALO, na, nb // PER_CELL, height, mean_line, col, cells, payload)
     kx, ky = na // PER_CELL, nb // PER_CELL
     coarse[0 : kx + 2, :] = edge[2][8 : 10 + kx, :]
     coarse[8 * (ky + 1) : 8 * (ky + 1) + kx + 2, :] = edge[3][8 : 10 + kx, :]
@@ -277,7 +289,7 @@
 
 def next_kernel(
     k, na, nb, n_row, n_col, cells, gathered, before, sensor_trunk, coarse, w1, b1, w2, b2, w3, b3,
-    pool, mean_trunk, coeffs, payload, sensors, lines,
+    mean_line, coeffs, payload, sensors, lines,
 ):
     height = na + 2 * HALO
     predicted = dot(before[...], sensor_trunk[...])
@@ -308,10 +320,11 @@
         vectors = own_vectors(na, nb, sensors, 8 + height)
     result = branch(vectors, w1, b1, w2, b2, w3, b3)
     coeffs[...] = result
-    send_means(result, pool, mean_trunk, col, cells, payload)
-
-
-def field_kernel(na, nb, n_row, n_col, cells, gathered, coarse, coeffs, trunk, out, correction, strip, ready, sent):
+    skip = (k - HALO, height) if k < ITERS else (0, na)
+    send_means(result, skip[0], na, nb // PER_CELL, skip[1], mean_line, col, cells, payload)
+
+
+def field_kernel(na, nb, n_row, n_col, cells, gathered, coarse, coeffs, trunk, out, correction, ready, sent):
     steps = ready.shape[0]
     width = trunk.shape[1] // steps
     per = width // TILE
@@ -330,36 +343,21 @@
         values = dot(coeffs[...], trunk[:, step * width : (step + 1) * width])
         for pair in range(nb // 2):
             for a in range(0, na, 8):
-                add = adds[a, 2 * pair // PER_CELL]
                 even, odd = (2 * pair * na + a, (2 * pair + 1) * na + a)
+                lines = []
                 for r in range(0, per, 2):
                     lanes = slice(r * TILE, r * TILE + LANES)
                     x, y = values[even : even + 8, lanes], values[odd : odd + 8, lanes]
-                    at = (pair * na + a) * per + r
-                    strip[pl.ds(at, 8, stride=per), :] = jnp.where(low, x, pltpu.roll(y, TILE, 1)) + add
-                    strip[pl.ds(at + 1, 8, stride=per), :] = jnp.where(low, pltpu.roll(x, TILE, 1), y) + add
-            done = strip[pair * na * per : (pair + 1) * na * per, :].reshape(na, per, LANES)
-            ready[step, :, :, pair * LANES : (pair + 1) * LANES] = done
+                    lines.append(jnp.where(low, x, pltpu.roll(y, TILE, 1)))
+                    lines.append(jnp.where(low, pltpu.roll(x, TILE, 1), y))
+                block = jnp.stack(lines, axis=0) + adds[a, 2 * pair // PER_CELL][None]
+                ready[step, a : a + 8, :, pair * LANES : (pair + 1) * LANES] = jnp.swapaxes(block, 0, 1)
         copies.append(
             pltpu.make_async_copy(ready.at[step], out.at[:, pl.ds(step * per, per), :], sent.at[step])
         )
         copies[-1].start()
     for copy in copies:
         copy.wait()
-
-
-def pool_matrix(na, nb, first, trimmed):
-    kx, ky = na // PER_CELL, nb // PER_CELL
-    height = na if trimmed else na + 2 * HALO
-    skip_a = 0 if trimmed else HALO
-    skip_b = HALO - first
-    wide = nb + 2 * skip_b
-    pool = np.zeros((16, wide * height), np.float32)
-    for a in range(na):
-        for b in range(nb):
-            cell = (a // PER_CELL) * ky + b // PER_CELL
-            pool[cell, (b + skip_b) * height + a + skip_a] = 1.0 / PER_CELL**2
-    return jnp.asarray(pool, BF16)
 
 
 def body(
@@ -449,8 +447,13 @@
         bias_latent.reshape(1, latent),
     )
 
-    sensor_trunk = call(
-        sensor_trunk_kernel, shape((latent, places), BF16), trunk, spread, flops=1 << 30
+    sensor_trunk, mean_line = call(
+        sensor_trunk_kernel,
+        (shape((latent, places), BF16), shape((8, latent), F32)),
+        trunk,
+        spread,
+        mean_trunk,
+        flops=1 << 30,
     )
     mid, sensor_trunk = lax.optimization_barrier((mid, sensor_trunk))
 
@@ -469,8 +472,7 @@
         coarse_matrix,
         spread,
         *net,
-        pool_matrix(na, nb, 1, False),
-        mean_trunk,
+        mean_line,
         scratch=[pltpu.VMEM((region(0) + 16, places), F32), pltpu.VMEM((region(0), tile_values), F32)],
     )
     for k in range(2, ITERS + 1):
@@ -483,8 +485,7 @@
             sensor_trunk,
             coarse,
             *net,
-            pool_matrix(na, nb, k, k == ITERS),
-            mean_trunk,
+            mean_line,
             scratch=[
                 pltpu.VMEM((region(k - 1) + 16, places), F32),
                 pltpu.VMEM(((ky + 2) * height, places), F32),
@@ -502,7 +503,6 @@
         out_specs=hbm,
         scratch=[
             pltpu.VMEM((cells, LANES), F32),
-            pltpu.VMEM((rows_here * cols_here // steps // LANES, LANES), F32),
             pltpu.VMEM((steps, na, TILE // steps, cols_here), F32),
             pltpu.SemaphoreType.DMA((steps,)),
         ],

time: 107 us -> 106 us (level)
    unnamed x26 -> x18, local copies, waits for them, and re-layouts: 2.22 us -> 2.19 us
where the time goes in v7:
time: 106 us
  blocking collectives  78.5 us (74%)
  Pallas kernels  12.6 us (12%)
  starting transfers between devices  11.7 us (11%)
  local copies, waits for them, and re-layouts  2.19 us (2%)
    all_to_all x4, blocking collectives, exchange(): return lax.all_to_all(x, ('row', 'col'), 0, 0, tiled=True)  78.5 us
    pallas_call x10, Pallas kernels, call(): pl.pallas_call(kernel, out_shape=out_shape, in_specs=in_specs or [whole]...  12.6 us
    ppermute x2, starting transfers between devices, swap(): return lax.ppermute(x, 'col', pairs)  8.43 us
    ppermute x2, starting transfers between devices, shift(): lax.ppermute(x, 'row', [(i, (i + step) % n_row) for i in range(n_row)])  3.27 us
    unnamed x18, local copies, waits for them, and re-layouts  2.19 us
  transfers between devices with their start and end apart: 4, of which 1 were waited for; matrix products, arithmetic and copies ran while one was open for 0% of the time, Pallas kernels for 4%

profile of v7, /device:TPU:1, one launch (start us, length us, event | category | flops | bytes accessed | tf_op | source)
XLA Modules:
  0.0 105.7 jit_solution(12269348314537300374)
XLA Ops:
  0.0 0.0 copy-start.1
  0.0 1.9 %copy-done.1 = f32[1024,768]{1,0:T(8,128)S(1)} copy-done((f32[1024,768]{1,0:T(8,128)S(1)}, f32[1024,768]{1,0:T(8,128)}, u32[]{:S(2)}) %copy-start.1) | copy-done | bytes 3145752
  1.9 0.0 copy-start.5
  1.9 0.6 shard_map.100
  2.5 0.0 copy-start.2
  2.6 0.3 copy-done.5
  2.8 0.1 shard_map.101
  2.9 2.6 %collective-permute-start = (bf16[8,3072]{1,0:T(8,128)(2,1)S(1)}, bf16[8,3072]{1,0:T(8,128)(2,1)S(1)}, u32[]{:S(2)}, u32[]{:S(2)}) collective-permute-start(bf16[8,3072]{1,0:T(8,128)(2,1)S(1)} %get-tuple-element.33), channel_id=1, source_target_pairs={{0,32},{32,64},{64,96},{96,128},{128,160},{160,192},{192,224},{224... | collective-permute-start | bytes 147464 | tf_op jit(solution)/shard_map/ppermute | solution.py:390
  5.5 0.7 collective-permute-start.1
  6.1 0.0 copy-done.2
  6.2 3.0 %shard_map.102 = (bf16[512,4096]{1,0:T(8,128)(2,1)S(1)}, f32[512,128]{1,0:T(8,128)S(1)}, bf16[512,512]{1,0:T(8,128)(2,1)S(1)}) custom-call(bf16[512,4096]{1,0:T(8,128)(2,1)} %trunk_hbm.1, bf16[512,512]{1,0:T(8,128)(2,1)S(1)} %copy-done.2), custom_call_target="tpu_custom_call" | custom-call | flops 4294967296 | bytes 1048576 | tf_op jit(solution)/shard_map/pallas_call | solution.py:39
  9.1 0.0 copy-start
  9.1 0.0 collective-permute-done.above
  9.1 0.0 collective-permute-done.1.below
  9.1 0.1 shard_map.103
  9.3 0.0 copy-start.3
  9.3 0.0 copy-start.4
  9.3 0.0 copy-start.6
  9.3 0.0 copy-start.7
  9.3 0.0 copy-start.8
  9.4 1.2 %collective-permute-start.2 = (bf16[16,3072]{1,0:T(8,128)(2,1)S(1)}, bf16[16,3072]{1,0:T(8,128)(2,1)S(1)}, u32[]{:S(2)}, u32[]{:S(2)}) collective-permute-start(bf16[16,3072]{1,0:T(8,128)(2,1)S(1)} %get-tuple-element.43), channel_id=1, source_target_pairs={{0,1},{1,0},{2,3},{3,2},{4,5},{5,4},{6,7},{7,6},{8,9},{9,8},{10,11... | collective-permute-start | bytes 294920 | tf_op jit(solution)/shard_map/ppermute | solution.py:394
  10.6 7.2 %collective-permute-start.3 = (bf16[16,3072]{1,0:T(8,128)(2,1)S(1)}, bf16[16,3072]{1,0:T(8,128)(2,1)S(1)}, u32[]{:S(2)}, u32[]{:S(2)}) collective-permute-start(bf16[16,3072]{1,0:T(8,128)(2,1)S(1)} %get-tuple-element.44), channel_id=1, source_target_pairs={{0,31},{1,2},{2,1},{3,4},{4,3},{5,6},{6,5},{7,8},{8,7},{9,10},{10,... | collective-permute-start | bytes 294920 | tf_op jit(solution)/shard_map/ppermute | solution.py:394
  17.8 0.0 copy-done
  17.8 1.7 %shard_map.104 = (bf16[512,512]{1,0:T(8,128)(2,1)S(1)}, f32[8,512]{1,0:T(8,128)S(1)}) custom-call(bf16[512,4096]{1,0:T(8,128)(2,1)S(1)} %get-tuple-element.39.trunk, bf16[256,512]{1,0:T(8,128)(2,1)S(1)} %copy-done, f32[512,128]{1,0:T(8,128)S(1)} %get-tuple-element.40.mean_trunk), custom_call_target="tpu_custom_call" | custom-call | flops 1073741824 | bytes 1048576 | tf_op jit(solution)/shard_map/pallas_call | solution.py:39
  19.5 0.0 collective-permute-done.2.first
  19.5 0.3 collective-permute-done.3.second
  19.8 0.0 copy-done.3
  19.8 0.0 copy-done.4
  19.8 0.0 copy-done.6
  19.8 0.0 copy-done.7
  19.8 0.0 copy-done.8
  19.8 1.2 %shard_map.105 = (bf16[432,512]{1,0:T(8,128)(2,1)S(1)}, f32[256,128]{1,0:T(8,128)S(1)}, f32[40,3072]{1,0:T(8,128)S(1)}) custom-call(bf16[288,256]{1,0:T(8,128)(2,1)S(1)} %get-tuple-element.42.mid, bf16[16,3072]{1,0:T(8,128)(2,1)S(1)} %collective-permute-done.2.first, bf16[16,3072]{1,0:T(8,128)(2,1)S(1)} %collective-permute-done.3.second, ...), custom_call_target="tpu_custom_call" | custom-call | flops 2147483648 | bytes 1048576 | tf_op jit(solution)/shard_map/pallas_call | solution.py:39
  21.0 23.6 %all_to_all.44 = f32[256,1,128]{2,1,0:T(1,128)S(1)} all-to-all(f32[256,1,128]{2,1,0:T(1,128)S(1)} %bitcast.21), channel_id=1, replica_groups=mesh['row'=8,'col'=32] {'row','col'}, dimensions={0} | all-to-all | bytes 262144 | tf_op jit(solution)/shard_map/all_to_all | solution.py:397
  44.6 1.3 %shard_map.106 = (bf16[384,512]{1,0:T(8,128)(2,1)S(1)}, f32[256,128]{1,0:T(8,128)S(1)}) custom-call(f32[256,128]{1,0:T(8,128)S(1)} %bitcast.24, bf16[432,512]{1,0:T(8,128)(2,1)S(1)} %get-tuple-element.48.before, bf16[512,512]{1,0:T(8,128)(2,1)S(1)} %get-tuple-element.49.sensor_trunk, f32[40,3072]{1,0:T(8,128)S(1)} %get-tuple-element.50.coarse, ...), custom_call_target="tpu_custom_call" | custom-call | flops 2147483648 | bytes 1048576 | tf_op jit(solution)/shard_map/pallas_call | solution.py:39
  45.9 18.3 %all_to_all.45 = f32[256,1,128]{2,1,0:T(1,128)S(1)} all-to-all(f32[256,1,128]{2,1,0:T(1,128)S(1)} %bitcast.26), channel_id=1, replica_groups=mesh['row'=8,'col'=32] {'row','col'}, dimensions={0} | all-to-all | bytes 262144 | tf_op jit(solution)/shard_map/all_to_all | solution.py:397
  64.2 1.3 %shard_map.107 = (bf16[336,512]{1,0:T(8,128)(2,1)S(1)}, f32[256,128]{1,0:T(8,128)S(1)}) custom-call(f32[256,128]{1,0:T(8,128)S(1)} %bitcast.25, bf16[384,512]{1,0:T(8,128)(2,1)S(1)} %get-tuple-element.52.before, bf16[512,512]{1,0:T(8,128)(2,1)S(1)} %get-tuple-element.49.sensor_trunk, f32[40,3072]{1,0:T(8,128)S(1)} %get-tuple-element.50.coarse, ...), custom_call_target="tpu_custom_call" | custom-call | flops 2147483648 | bytes 1048576 | tf_op jit(solution)/shard_map/pallas_call | solution.py:39
  65.5 18.3 %all_to_all.46 = f32[256,1,128]{2,1,0:T(1,128)S(1)} all-to-all(f32[256,1,128]{2,1,0:T(1,128)S(1)} %bitcast.27), channel_id=1, replica_groups=mesh['row'=8,'col'=32] {'row','col'}, dimensions={0} | all-to-all | bytes 262144 | tf_op jit(solution)/shard_map/all_to_all | solution.py:397
  83.8 1.1 %shard_map.108 = (bf16[192,512]{1,0:T(8,128)(2,1)S(1)}, f32[256,128]{1,0:T(8,128)S(1)}) custom-call(f32[256,128]{1,0:T(8,128)S(1)} %bitcast.22, bf16[336,512]{1,0:T(8,128)(2,1)S(1)} %get-tuple-element.54.before, bf16[512,512]{1,0:T(8,128)(2,1)S(1)} %get-tuple-element.49.sensor_trunk, f32[40,3072]{1,0:T(8,128)S(1)} %get-tuple-element.50.coarse, ...), custom_call_target="tpu_custom_call" | custom-call | flops 2147483648 | bytes 1048576 | tf_op jit(solution)/shard_map/pallas_call | solution.py:39
  84.9 18.3 %all_to_all.47 = f32[256,1,128]{2,1,0:T(1,128)S(1)} all-to-all(f32[256,1,128]{2,1,0:T(1,128)S(1)} %bitcast.23), channel_id=1, replica_groups=mesh['row'=8,'col'=32] {'row','col'}, dimensions={0} | all-to-all | bytes 262144 | tf_op jit(solution)/shard_map/all_to_all | solution.py:397
  103.2 2.3 %shard_map.109 = f32[16,64,768]{2,1,0:T(8,128)} custom-call(f32[256,128]{1,0:T(8,128)S(1)} %bitcast.28, f32[12,3072]{1,0:T(8,128)S(1)} %copy-done.5, bf16[192,512]{1,0:T(8,128)(2,1)S(1)} %get-tuple-element.56.coeffs, bf16[512,4096]{1,0:T(8,128)(2,1)S(1)} %get-tuple-element.39.trunk), custom_call_target="tpu_custom_call" | custom-call | flops 2147483648 | bytes 1048576 | tf_op jit(solution)/shard_map/pallas_call | solution.py:39
Async XLA Ops:
  0.0 1.9 %copy-start.1 = (f32[1024,768]{1,0:T(8,128)S(1)}, f32[1024,768]{1,0:T(8,128)}, u32[]{:S(2)}) copy-start(f32[1024,768]{1,0:T(8,128)} %param.10) | copy-start | bytes 9437188
  1.9 0.9 copy-start.5
  2.5 3.6 %copy-start.2 = (bf16[512,512]{1,0:T(8,128)(2,1)S(1)}, bf16[512,512]{1,0:T(8,128)(2,1)}, u32[]{:S(2)}) copy-start(bf16[512,512]{1,0:T(8,128)(2,1)} %w_sensor.1) | copy-start | bytes 1572868
  2.9 6.3 %collective-permute-start = (bf16[8,3072]{1,0:T(8,128)(2,1)S(1)}, bf16[8,3072]{1,0:T(8,128)(2,1)S(1)}, u32[]{:S(2)}, u32[]{:S(2)}) collective-permute-start(bf16[8,3072]{1,0:T(8,128)(2,1)S(1)} %get-tuple-element.33), channel_id=1, source_target_pairs={{0,32},{32,64},{64,96},{96,128},{128,160},{160,192},{192,224},{224... | collective-permute-start | bytes 147464 | tf_op jit(solution)/shard_map/ppermute | solution.py:390
  5.5 3.7 %collective-permute-start.1 = (bf16[8,3072]{1,0:T(8,128)(2,1)S(1)}, bf16[8,3072]{1,0:T(8,128)(2,1)S(1)}, u32[]{:S(2)}, u32[]{:S(2)}) collective-permute-start(bf16[8,3072]{1,0:T(8,128)(2,1)S(1)} %get-tuple-element.34), channel_id=1, source_target_pairs={{0,224},{32,0},{64,32},{96,64},{128,96},{160,128},{192,160},{224,1... | collective-permute-start | bytes 147464 | tf_op jit(solution)/shard_map/ppermute | solution.py:390
  9.1 8.7 %copy-start = (bf16[256,512]{1,0:T(8,128)(2,1)S(1)}, bf16[256,512]{1,0:T(8,128)(2,1)}, u32[]{:S(2)}) copy-start(bf16[256,512]{1,0:T(8,128)(2,1)} %constant.2.clone.spread) | copy-start | bytes 786436
  9.3 10.5 %copy-start.3 = (bf16[512,512]{1,0:T(8,128)(2,1)S(1)}, bf16[512,512]{1,0:T(8,128)(2,1)}, u32[]{:S(2)}) copy-start(bf16[512,512]{1,0:T(8,128)(2,1)} %w2.7) | copy-start | bytes 1572868
  9.3 10.5 %copy-start.4 = (bf16[512,512]{1,0:T(8,128)(2,1)S(1)}, bf16[512,512]{1,0:T(8,128)(2,1)}, u32[]{:S(2)}) copy-start(bf16[512,512]{1,0:T(8,128)(2,1)} %w3.7) | copy-start | bytes 1572868
  9.3 10.5 %copy-start.6 = (f32[512]{0:T(512)S(1)}, f32[512]{0:T(512)}, u32[]{:S(2)}) copy-start(f32[512]{0:T(512)} %param.12) | copy-start | bytes 6148
  9.3 10.5 %copy-start.7 = (f32[512]{0:T(512)S(1)}, f32[512]{0:T(512)}, u32[]{:S(2)}) copy-start(f32[512]{0:T(512)} %param.14) | copy-start | bytes 6148
  9.3 10.5 %copy-start.8 = (f32[512]{0:T(512)S(1)}, f32[512]{0:T(512)}, u32[]{:S(2)}) copy-start(f32[512]{0:T(512)} %param.16) | copy-start | bytes 6148
  9.4 10.1 %collective-permute-start.2 = (bf16[16,3072]{1,0:T(8,128)(2,1)S(1)}, bf16[16,3072]{1,0:T(8,128)(2,1)S(1)}, u32[]{:S(2)}, u32[]{:S(2)}) collective-permute-start(bf16[16,3072]{1,0:T(8,128)(2,1)S(1)} %get-tuple-element.43), channel_id=1, source_target_pairs={{0,1},{1,0},{2,3},{3,2},{4,5},{5,4},{6,7},{7,6},{8,9},{9,8},{10,11... | collective-permute-start | bytes 294920 | tf_op jit(solution)/shard_map/ppermute | solution.py:394
  10.6 9.2 %collective-permute-start.3 = (bf16[16,3072]{1,0:T(8,128)(2,1)S(1)}, bf16[16,3072]{1,0:T(8,128)(2,1)S(1)}, u32[]{:S(2)}, u32[]{:S(2)}) collective-permute-start(bf16[16,3072]{1,0:T(8,128)(2,1)S(1)} %get-tuple-element.44), channel_id=1, source_target_pairs={{0,31},{1,2},{2,1},{3,4},{4,3},{5,6},{6,5},{7,8},{8,7},{9,10},{10,... | collective-permute-start | bytes 294920 | tf_op jit(solution)/shard_map/ppermute | solution.py:394

commit v8 on v7

--- a/solution.py
+++ b/solution.py
@@ -70,46 +70,50 @@
     return spread, order
 
 
-def extract_kernel(na, nb, cells, row_part, col_part):
-    cols = cells.shape[2]
-    here = 8
+def extract_tiles(nb, cells, row_part, col_part):
+    here, _, cols = cells.shape
     sel_row = lax.broadcasted_iota(jnp.int32, (2 * 16, cols), 0)
     sel_col = lax.broadcasted_iota(jnp.int32, (2 * 16, cols), 1)
-    side, b_of = sel_row // 16, sel_row % 16
+    side, b_of = sel_row >> 4, sel_row & 15
     pick = jnp.where(sel_col == b_of * TILE + (TILE // 2 - 1) + side, 1.0, 0.0).astype(BF16)
     low_row, low_col = low_lanes((here, LANES)), low_lanes((16, LANES))
-    for base in range(0, na, here):
-        chunk = cells[base : base + here]
-        picked = nt_dot(pick, chunk.reshape(here * TILE, cols).astype(BF16))
-        r31 = cells[base : base + here, TILE // 2 - 1, :]
-        r32 = cells[base : base + here, TILE // 2, :]
-        for pair in range(nb // 2):
-            lanes = slice(pair * LANES, (pair + 1) * LANES)
-            x, y = r31[:, lanes], r32[:, lanes]
-            even, odd = 2 * pair * na + base, (2 * pair + 1) * na + base
-            row_part[even : even + here, :] = jnp.where(low_row, x, pltpu.roll(y, TILE, 1))
-            row_part[odd : odd + here, :] = jnp.where(low_row, pltpu.roll(x, TILE, 1), y)
-        for pair in range(here // 2):
-            lanes = slice(pair * LANES, (pair + 1) * LANES)
-            x, y = picked[0:16, lanes], picked[16:32, lanes]
-            even = jnp.where(low_col, x, pltpu.roll(y, TILE, 1))
-            odd = jnp.where(low_col, pltpu.roll(x, TILE, 1), y)
-            col_part[pl.ds(base + 2 * pair, nb, stride=na), :] = even[0:nb]
-            col_part[pl.ds(base + 2 * pair + 1, nb, stride=na), :] = odd[0:nb]
-
-
-def pack_kernel(na, nb, ky, row_part, col_part, coarse, up, down, packed):
+    picked = nt_dot(pick, cells[...].reshape(here * TILE, cols).astype(BF16))
+    r31 = cells[:, TILE // 2 - 1, :]
+    r32 = cells[:, TILE // 2, :]
+    for pair in range(nb // 2):
+        lanes = slice(pair * LANES, (pair + 1) * LANES)
+        x, y = r31[:, lanes], r32[:, lanes]
+        even, odd = 2 * pair * here, (2 * pair + 1) * here
+        row_part[even : even + here, :] = jnp.where(low_row, x, pltpu.roll(y, TILE, 1))
+        row_part[odd : odd + here, :] = jnp.where(low_row, pltpu.roll(x, TILE, 1), y)
+    for pair in range(here // 2):
+        lanes = slice(pair * LANES, (pair + 1) * LANES)
+        x, y = picked[0:16, lanes], picked[16:32, lanes]
+        even = jnp.where(low_col, x, pltpu.roll(y, TILE, 1))
+        odd = jnp.where(low_col, pltpu.roll(x, TILE, 1), y)
+        col_part[pl.ds(2 * pair, nb, stride=here), :] = even[0:nb]
+        col_part[pl.ds(2 * pair + 1, nb, stride=here), :] = odd[0:nb]
+
+
+def outer_kernel(nb, ky, top, bottom, coarse, up, down, top_rows, top_cols, bottom_rows, bottom_cols, packed):
     packed[...] = jnp.zeros(packed.shape, F32)
-    for target, first, line in ((up, 0, 0), (down, na - HALO, coarse.shape[0] - ky)):
+    for target, cells, rows, cols, line in (
+        (up, top, top_rows, top_cols, 0),
+        (down, bottom, bottom_rows, bottom_cols, coarse.shape[0] - ky),
+    ):
+        extract_tiles(nb, cells, rows, cols)
         for b in range(nb):
-            rows = slice(b * na + first, b * na + first + HALO)
-            packed[0:HALO, 2 * b * LANES : (2 * b + 1) * LANES] = row_part[rows, :]
-            packed[0:HALO, (2 * b + 1) * LANES : (2 * b + 2) * LANES] = col_part[rows, :]
+            part = slice(b * HALO, (b + 1) * HALO)
+            packed[0:HALO, 2 * b * LANES : (2 * b + 1) * LANES] = rows[part, :]
+            packed[0:HALO, (2 * b + 1) * LANES : (2 * b + 2) * LANES] = cols[part, :]
         packed[HALO : HALO + ky, :] = coarse[line : line + ky, :]
         target[...] = packed[...].astype(BF16)
 
 
-def columns_kernel(na, nb, n_row, row_part, col_part, above, below, coarse, both, first, second, tall, left, right):
+def columns_kernel(
+    na, nb, n_row, top_rows, top_cols, mid_rows, mid_cols, bottom_rows, bottom_cols, above, below, coarse,
+    both, first, second, tall, left, right,
+):
     height, values = na + 2 * HALO, 4 * TILE
     kx, ky = na // PER_CELL, nb // PER_CELL
     row, even = lax.axis_index("row"), lax.axis_index("col") % 2 == 0
@@ -118,8 +122,12 @@
     for b in range(nb):
         at = b * height
         tall[at : at + HALO, :] = over[0:HALO, b * values : (b + 1) * values]
-        tall[at + HALO : at + HALO + na, 0:LANES] = row_part[b * na : (b + 1) * na, :]
-        tall[at + HALO : at + HALO + na, LANES : 2 * LANES] = col_part[b * na : (b + 1) * na, :]
+        to = at + HALO
+        for rows, cols in ((top_rows, top_cols), (mid_rows, mid_cols), (bottom_rows, bottom_cols)):
+            size = rows.shape[0] // nb
+            tall[to : to + size, 0:LANES] = rows[b * size : (b + 1) * size, :]
+            tall[to : to + size, LANES : 2 * LANES] = cols[b * size : (b + 1) * size, :]
+            to += size
         tall[at + HALO + na : at + height, :] = under[0:HALO, b * values : (b + 1) * values]
     both[...] = tall[...].astype(BF16)
     for packed, start, j in ((left, 0, 0), (right, nb - HALO, ky - 1)):
@@ -402,16 +410,13 @@
     blocks = tuple((int(at), half) for at in order[::half])
     hbm = pl.BlockSpec(memory_space=pltpu.HBM)
 
-    row_part, col_part = call(
-        part(extract_kernel, na, nb),
-        (shape((nb * na, LANES), F32), shape((nb * na, LANES), F32)),
-        field_start.reshape(na, TILE, cols_here),
-    )
-    up, down = call(
-        part(pack_kernel, na, nb, ky),
-        (shape((8, total), BF16), shape((8, total), BF16)),
-        row_part,
-        col_part,
+    side, inner = shape((nb * HALO, LANES), F32), shape((nb * (na - 2 * HALO), LANES), F32)
+    field_rows = field_start.reshape(na, TILE, cols_here)
+    up, down, *outer = call(
+        part(outer_kernel, nb, ky),
+        (shape((8, total), BF16), shape((8, total), BF16), side, side, side, side),
+        field_rows[0:HALO],
+        field_rows[na - HALO :],
         coarse_matrix,
         scratch=[pltpu.VMEM((8, total), F32)],
     )
@@ -425,12 +430,14 @@
         scratch=[pltpu.SemaphoreType.DMA((4,))],
         flops=1 << 32,
     )
+    middle = call(part(extract_tiles, nb), (inner, inner), field_rows[HALO : na - HALO])
     above, below, w_first = lax.optimization_barrier((above, below, w_first))
     mid, first, second = call(
         part(columns_kernel, na, nb, n_row),
         (shape((nb * height, tile_values), BF16), shape((16, total), BF16), shape((16, total), BF16)),
-        row_part,
-        col_part,
+        *outer[:2],
+        *middle,
+        *outer[2:],
         above,
         below,
         coarse_matrix,

time: 106 us -> 105 us (level)
    unnamed x18, local copies, waits for them, and re-layouts: 2.19 us -> 0.05 us
    slice x0 -> x2, local copies, waits for them, and re-layouts: none -> 1.61 us  [the longest x1 1.51 us: body(): field_rows[na - HALO:]]
  transfers between devices with their start and end apart: 4 -> 4, of which waited for: 1 -> 1; matrix products, arithmetic and copies ran while one was open for 0% -> 0% of each run, Pallas kernels for 4% -> 5%
where the time goes in v8:
time: 105 us
  blocking collectives  78.9 us (75%)
  Pallas kernels  12.8 us (12%)
  starting transfers between devices  11.2 us (11%)
  local copies, waits for them, and re-layouts  1.67 us (2%)
    all_to_all x4, blocking collectives, exchange(): return lax.all_to_all(x, ('row', 'col'), 0, 0, tiled=True)  78.9 us
    pallas_call x10, Pallas kernels, call(): pl.pallas_call(kernel, out_shape=out_shape, in_specs=in_specs or [whole]...  12.8 us
    ppermute x2, starting transfers between devices, swap(): return lax.ppermute(x, 'col', pairs)  7.91 us
    ppermute x2, starting transfers between devices, shift(): lax.ppermute(x, 'row', [(i, (i + step) % n_row) for i in range(n_row)])  3.27 us
  transfers between devices with their start and end apart: 4, of which 1 were waited for; matrix products, arithmetic and copies ran while one was open for 0% of the time, Pallas kernels for 5%

profile of v8, /device:TPU:1, one launch (start us, length us, event | category | flops | bytes accessed | tf_op | source)
XLA Modules:
  0.0 105.2 jit_solution(12518722634002720525)
XLA Ops:
  0.0 0.0 copy-start.4
  0.0 1.5 %fusion = (f32[256,768]{1,0:T(8,128)S(1)}, f32[256,768]{1,0:T(8,128)S(1)}) fusion(f32[1024,768]{1,0:T(8,128)} %param.10), kind=kLoop, calls=%fused_computation | loop fusion | bytes 3145728 | tf_op jit(solution)/shard_map/slice | solution.py:419
  1.5 0.0 copy-done.4
  1.5 0.0 copy-start.8
  1.5 0.4 shard_map.100
  2.0 0.0 copy-start.1
  2.0 2.6 %collective-permute-start = (bf16[8,3072]{1,0:T(8,128)(2,1)S(1)}, bf16[8,3072]{1,0:T(8,128)(2,1)S(1)}, u32[]{:S(2)}, u32[]{:S(2)}) collective-permute-start(bf16[8,3072]{1,0:T(8,128)(2,1)S(1)} %get-tuple-element.41), channel_id=1, source_target_pairs={{0,32},{32,64},{64,96},{96,128},{128,160},{160,192},{192,224},{224... | collective-permute-start | bytes 147464 | tf_op jit(solution)/shard_map/ppermute | solution.py:398
  4.6 0.7 collective-permute-start.1
  5.3 0.0 copy-done.8
  5.3 0.1 slice.22
  5.4 0.0 copy-done.1
  5.4 3.0 %shard_map.102 = (bf16[512,4096]{1,0:T(8,128)(2,1)S(1)}, f32[512,128]{1,0:T(8,128)S(1)}, bf16[512,512]{1,0:T(8,128)(2,1)S(1)}) custom-call(bf16[512,4096]{1,0:T(8,128)(2,1)} %trunk_hbm.1, bf16[512,512]{1,0:T(8,128)(2,1)S(1)} %copy-done.1), custom_call_target="tpu_custom_call" | custom-call | flops 4294967296 | bytes 1048576 | tf_op jit(solution)/shard_map/pallas_call | solution.py:39
  8.4 0.4 shard_map.101
  8.8 0.0 collective-permute-done.above
  8.8 0.0 collective-permute-done.1.below
  8.8 0.0 copy-start
  8.8 0.1 shard_map.103
  9.0 0.0 copy-start.2
  9.0 0.0 copy-start.3
  9.0 0.0 copy-start.5
  9.0 0.0 copy-start.6
  9.0 0.0 copy-start.7
  9.0 0.7 collective-permute-start.2
  9.7 7.2 %collective-permute-start.3 = (bf16[16,3072]{1,0:T(8,128)(2,1)S(1)}, bf16[16,3072]{1,0:T(8,128)(2,1)S(1)}, u32[]{:S(2)}, u32[]{:S(2)}) collective-permute-start(bf16[16,3072]{1,0:T(8,128)(2,1)S(1)} %get-tuple-element.52), channel_id=1, source_target_pairs={{0,31},{1,2},{2,1},{3,4},{4,3},{5,6},{6,5},{7,8},{8,7},{9,10},{10,... | collective-permute-start | bytes 294920 | tf_op jit(solution)/shard_map/ppermute | solution.py:402
  16.9 0.0 copy-done
  16.9 1.7 %shard_map.104 = (bf16[512,512]{1,0:T(8,128)(2,1)S(1)}, f32[8,512]{1,0:T(8,128)S(1)}) custom-call(bf16[512,4096]{1,0:T(8,128)(2,1)S(1)} %get-tuple-element.47.trunk, bf16[256,512]{1,0:T(8,128)(2,1)S(1)} %copy-done, f32[512,128]{1,0:T(8,128)S(1)} %get-tuple-element.48.mean_trunk), custom_call_target="tpu_custom_call" | custom-call | flops 1073741824 | bytes 1048576 | tf_op jit(solution)/shard_map/pallas_call | solution.py:39
  18.6 0.0 collective-permute-done.2.first
  18.6 0.3 collective-permute-done.3.second
  18.9 0.0 copy-done.2
  18.9 0.0 copy-done.3
  18.9 0.0 copy-done.5
  19.0 0.0 copy-done.6
  19.0 0.0 copy-done.7
  19.0 1.2 %shard_map.105 = (bf16[432,512]{1,0:T(8,128)(2,1)S(1)}, f32[256,128]{1,0:T(8,128)S(1)}, f32[40,3072]{1,0:T(8,128)S(1)}) custom-call(bf16[288,256]{1,0:T(8,128)(2,1)S(1)} %get-tuple-element.50.mid, bf16[16,3072]{1,0:T(8,128)(2,1)S(1)} %collective-permute-done.2.first, bf16[16,3072]{1,0:T(8,128)(2,1)S(1)} %collective-permute-done.3.second, ...), custom_call_target="tpu_custom_call" | custom-call | flops 2147483648 | bytes 1048576 | tf_op jit(solution)/shard_map/pallas_call | solution.py:39
  20.2 24.0 %all_to_all.44 = f32[256,1,128]{2,1,0:T(1,128)S(1)} all-to-all(f32[256,1,128]{2,1,0:T(1,128)S(1)} %bitcast.26), channel_id=1, replica_groups=mesh['row'=8,'col'=32] {'row','col'}, dimensions={0} | all-to-all | bytes 262144 | tf_op jit(solution)/shard_map/all_to_all | solution.py:405
  44.2 1.3 %shard_map.106 = (bf16[384,512]{1,0:T(8,128)(2,1)S(1)}, f32[256,128]{1,0:T(8,128)S(1)}) custom-call(f32[256,128]{1,0:T(8,128)S(1)} %bitcast.29, bf16[432,512]{1,0:T(8,128)(2,1)S(1)} %get-tuple-element.56.before, bf16[512,512]{1,0:T(8,128)(2,1)S(1)} %get-tuple-element.57.sensor_trunk, f32[40,3072]{1,0:T(8,128)S(1)} %get-tuple-element.58.coarse, ...), custom_call_target="tpu_custom_call" | custom-call | flops 2147483648 | bytes 1048576 | tf_op jit(solution)/shard_map/pallas_call | solution.py:39
  45.5 18.3 %all_to_all.45 = f32[256,1,128]{2,1,0:T(1,128)S(1)} all-to-all(f32[256,1,128]{2,1,0:T(1,128)S(1)} %bitcast.31), channel_id=1, replica_groups=mesh['row'=8,'col'=32] {'row','col'}, dimensions={0} | all-to-all | bytes 262144 | tf_op jit(solution)/shard_map/all_to_all | solution.py:405
  63.8 1.3 %shard_map.107 = (bf16[336,512]{1,0:T(8,128)(2,1)S(1)}, f32[256,128]{1,0:T(8,128)S(1)}) custom-call(f32[256,128]{1,0:T(8,128)S(1)} %bitcast.30, bf16[384,512]{1,0:T(8,128)(2,1)S(1)} %get-tuple-element.60.before, bf16[512,512]{1,0:T(8,128)(2,1)S(1)} %get-tuple-element.57.sensor_trunk, f32[40,3072]{1,0:T(8,128)S(1)} %get-tuple-element.58.coarse, ...), custom_call_target="tpu_custom_call" | custom-call | flops 2147483648 | bytes 1048576 | tf_op jit(solution)/shard_map/pallas_call | solution.py:39
  65.1 18.3 %all_to_all.46 = f32[256,1,128]{2,1,0:T(1,128)S(1)} all-to-all(f32[256,1,128]{2,1,0:T(1,128)S(1)} %bitcast.32), channel_id=1, replica_groups=mesh['row'=8,'col'=32] {'row','col'}, dimensions={0} | all-to-all | bytes 262144 | tf_op jit(solution)/shard_map/all_to_all | solution.py:405
  83.4 1.1 %shard_map.108 = (bf16[192,512]{1,0:T(8,128)(2,1)S(1)}, f32[256,128]{1,0:T(8,128)S(1)}) custom-call(f32[256,128]{1,0:T(8,128)S(1)} %bitcast.27, bf16[336,512]{1,0:T(8,128)(2,1)S(1)} %get-tuple-element.62.before, bf16[512,512]{1,0:T(8,128)(2,1)S(1)} %get-tuple-element.57.sensor_trunk, f32[40,3072]{1,0:T(8,128)S(1)} %get-tuple-element.58.coarse, ...), custom_call_target="tpu_custom_call" | custom-call | flops 2147483648 | bytes 1048576 | tf_op jit(solution)/shard_map/pallas_call | solution.py:39
  84.5 18.3 %all_to_all.47 = f32[256,1,128]{2,1,0:T(1,128)S(1)} all-to-all(f32[256,1,128]{2,1,0:T(1,128)S(1)} %bitcast.28), channel_id=1, replica_groups=mesh['row'=8,'col'=32] {'row','col'}, dimensions={0} | all-to-all | bytes 262144 | tf_op jit(solution)/shard_map/all_to_all | solution.py:405
  102.8 2.3 %shard_map.109 = f32[16,64,768]{2,1,0:T(8,128)} custom-call(f32[256,128]{1,0:T(8,128)S(1)} %bitcast.33, f32[12,3072]{1,0:T(8,128)S(1)} %copy-done.4, bf16[192,512]{1,0:T(8,128)(2,1)S(1)} %get-tuple-element.64.coeffs, bf16[512,4096]{1,0:T(8,128)(2,1)S(1)} %get-tuple-element.47.trunk), custom_call_target="tpu_custom_call" | custom-call | flops 2147483648 | bytes 1048576 | tf_op jit(solution)/shard_map/pallas_call | solution.py:39
Async XLA Ops:
  0.0 1.5 %copy-start.4 = (f32[12,3072]{1,0:T(8,128)S(1)}, f32[12,3072]{1,0:T(8,128)}, u32[]{:S(2)}) copy-start(f32[12,3072]{1,0:T(8,128)} %coarse.5) | copy-start | bytes 442372
  1.5 3.8 %copy-start.8 = (f32[1024,768]{1,0:T(8,128)S(1)}, f32[1024,768]{1,0:T(8,128)}, u32[]{:S(2)}) copy-start(f32[1024,768]{1,0:T(8,128)} %param.10) | copy-start | bytes 9437188
  2.0 3.4 %copy-start.1 = (bf16[512,512]{1,0:T(8,128)(2,1)S(1)}, bf16[512,512]{1,0:T(8,128)(2,1)}, u32[]{:S(2)}) copy-start(bf16[512,512]{1,0:T(8,128)(2,1)} %w_sensor.1) | copy-start | bytes 1572868
  2.0 6.8 %collective-permute-start = (bf16[8,3072]{1,0:T(8,128)(2,1)S(1)}, bf16[8,3072]{1,0:T(8,128)(2,1)S(1)}, u32[]{:S(2)}, u32[]{:S(2)}) collective-permute-start(bf16[8,3072]{1,0:T(8,128)(2,1)S(1)} %get-tuple-element.41), channel_id=1, source_target_pairs={{0,32},{32,64},{64,96},{96,128},{128,160},{160,192},{192,224},{224... | collective-permute-start | bytes 147464 | tf_op jit(solution)/shard_map/ppermute | solution.py:398
  4.6 4.2 %collective-permute-start.1 = (bf16[8,3072]{1,0:T(8,128)(2,1)S(1)}, bf16[8,3072]{1,0:T(8,128)(2,1)S(1)}, u32[]{:S(2)}, u32[]{:S(2)}) collective-permute-start(bf16[8,3072]{1,0:T(8,128)(2,1)S(1)} %get-tuple-element.42), channel_id=1, source_target_pairs={{0,224},{32,0},{64,32},{96,64},{128,96},{160,128},{192,160},{224,1... | collective-permute-start | bytes 147464 | tf_op jit(solution)/shard_map/ppermute | solution.py:398
  8.8 8.1 %copy-start = (bf16[256,512]{1,0:T(8,128)(2,1)S(1)}, bf16[256,512]{1,0:T(8,128)(2,1)}, u32[]{:S(2)}) copy-start(bf16[256,512]{1,0:T(8,128)(2,1)} %constant.2.clone.spread) | copy-start | bytes 786436
  9.0 10.0 %copy-start.2 = (bf16[512,512]{1,0:T(8,128)(2,1)S(1)}, bf16[512,512]{1,0:T(8,128)(2,1)}, u32[]{:S(2)}) copy-start(bf16[512,512]{1,0:T(8,128)(2,1)} %w2.7) | copy-start | bytes 1572868
  9.0 10.0 %copy-start.3 = (bf16[512,512]{1,0:T(8,128)(2,1)S(1)}, bf16[512,512]{1,0:T(8,128)(2,1)}, u32[]{:S(2)}) copy-start(bf16[512,512]{1,0:T(8,128)(2,1)} %w3.7) | copy-start | bytes 1572868
  9.0 10.0 %copy-start.5 = (f32[512]{0:T(512)S(1)}, f32[512]{0:T(512)}, u32[]{:S(2)}) copy-start(f32[512]{0:T(512)} %param.12) | copy-start | bytes 6148
  9.0 10.0 %copy-start.6 = (f32[512]{0:T(512)S(1)}, f32[512]{0:T(512)}, u32[]{:S(2)}) copy-start(f32[512]{0:T(512)} %param.14) | copy-start | bytes 6148
  9.0 10.0 %copy-start.7 = (f32[512]{0:T(512)S(1)}, f32[512]{0:T(512)}, u32[]{:S(2)}) copy-start(f32[512]{0:T(512)} %param.16) | copy-start | bytes 6148
  9.0 9.6 %collective-permute-start.2 = (bf16[16,3072]{1,0:T(8,128)(2,1)S(1)}, bf16[16,3072]{1,0:T(8,128)(2,1)S(1)}, u32[]{:S(2)}, u32[]{:S(2)}) collective-permute-start(bf16[16,3072]{1,0:T(8,128)(2,1)S(1)} %get-tuple-element.51), channel_id=1, source_target_pairs={{0,1},{1,0},{2,3},{3,2},{4,5},{5,4},{6,7},{7,6},{8,9},{9,8},{10,11... | collective-permute-start | bytes 294920 | tf_op jit(solution)/shard_map/ppermute | solution.py:402
  9.7 9.2 %collective-permute-start.3 = (bf16[16,3072]{1,0:T(8,128)(2,1)S(1)}, bf16[16,3072]{1,0:T(8,128)(2,1)S(1)}, u32[]{:S(2)}, u32[]{:S(2)}) collective-permute-start(bf16[16,3072]{1,0:T(8,128)(2,1)S(1)} %get-tuple-element.52), channel_id=1, source_target_pairs={{0,31},{1,2},{2,1},{3,4},{4,3},{5,6},{6,5},{7,8},{8,7},{9,10},{10,... | collective-permute-start | bytes 294920 | tf_op jit(solution)/shard_map/ppermute | solution.py:402

commit v9 on v8

--- a/solution.py
+++ b/solution.py
@@ -165,8 +165,20 @@
         mean_trunk[rows, :] = dot(trunk[rows, :], share)
 
 
-def sensor_trunk_kernel(trunk, spread, mean_trunk, sensor_trunk, mean_line):
-    mean_line[...] = jnp.transpose(mean_trunk[...])[0:8, :]
+def three_parts(line):
+    high = line.astype(BF16).astype(F32)
+    middle = (line - high).astype(BF16).astype(F32)
+    low = line - high - middle
+    at = lax.broadcasted_iota(jnp.int32, (16, line.shape[1]), 0)
+    parts = jnp.where(at == 0, high, jnp.where(at == 1, middle, jnp.where(at == 2, low, 0.0)))
+    return parts.astype(BF16)
+
+
+def sensor_trunk_kernel(trunk, spread, mean_trunk, w3, b3, w_sensors, b_sensors, mean_line, mean_bias):
+    mean = jnp.transpose(mean_trunk[...])[0:8, :]
+    line = jnp.sum(nt_dot(three_parts(mean[0:1, :]), w3[...]), axis=0, keepdims=True)
+    mean_line[...] = jnp.broadcast_to(line, mean_line.shape)
+    mean_bias[...] = jnp.broadcast_to(jnp.sum(mean * b3[...], axis=1, keepdims=True), mean_bias.shape)
     width = 1024
     per = width // TILE
     point = lax.broadcasted_iota(jnp.int32, (width, LANES), 0)
@@ -183,7 +195,11 @@
     row32 = pltpu.roll(trunk[:, middle : middle + LANES].astype(F32), TILE, 1)
     rows = jnp.where(low_lanes(row31.shape), row31, row32)
     unique = jnp.concatenate([rows, total], axis=1).astype(BF16)
-    sensor_trunk[...] = dot(unique, spread[...]).astype(BF16)
+    columns = dot(unique, spread[...]).astype(BF16)
+    both = dot(jnp.concatenate([w3[...], three_parts(b3[...])], axis=0), columns)
+    depth = w_sensors.shape[0]
+    w_sensors[...] = both[0:depth, :].astype(BF16)
+    b_sensors[...] = jnp.broadcast_to(jnp.sum(both[depth:, :], axis=0, keepdims=True), b_sensors.shape)
 
 
 def sensor_vectors(sensors, base, count):
@@ -202,13 +218,12 @@
     return jnp.concatenate([p.astype(BF16) for p in parts], axis=1)
 
 
-def branch(vectors, w1, b1, w2, b2, w3, b3):
+def hidden_two(vectors, w1, b1, w2, b2):
     hidden = jnp.tanh(dot(vectors, w1[...]) + b1[...]).astype(BF16)
-    hidden = jnp.tanh(dot(hidden, w2[...]) + b2[...]).astype(BF16)
-    return (dot(hidden, w3[...]) + b3[...]).astype(BF16)
-
-
-def send_means(coeffs, columns, na, ky, height, mean_line, col, cells, payload):
+    return jnp.tanh(dot(hidden, w2[...]) + b2[...]).astype(BF16)
+
+
+def send_means(hidden, columns, na, ky, height, mean_line, mean_bias, col, cells, payload):
     skip = (height - na) // 2
     share = mean_line[0:1, :] * (1.0 / PER_CELL**2)
     lane = lax.broadcasted_iota(jnp.int32, (height, LANES), 1)
@@ -220,9 +235,9 @@
         tiles = None
         for b in range(PER_CELL * j, PER_CELL * (j + 1)):
             at = (b - columns) * height
-            part = coeffs[at : at + height, :].astype(F32)
+            part = hidden[at : at + height, :].astype(F32)
             tiles = part if tiles is None else tiles + part
-        sums = jnp.sum(tiles * share, axis=1, keepdims=True)
+        sums = jnp.sum(tiles * share, axis=1, keepdims=True) + mean_bias[0:1, 0:1] * (1.0 / PER_CELL)
         mine = ((lane - cells * col) & (LANES - 1)) == place + j
         part = jnp.where(mine, sums, 0.0)
         total = part if total is None else total + part
@@ -259,8 +274,8 @@
 
 
 def first_kernel(
-    na, nb, n_col, cells, mid, first, second, above, below, c_own, spread, w1, b1, w2, b2, w3, b3, mean_line,
-    coeffs, payload, coarse, sensors, tiles,
+    na, nb, n_col, cells, mid, first, second, above, below, c_own, spread, w1, b1, w2, b2, mean_line, mean_bias,
+    hidden, payload, coarse, sensors, tiles,
 ):
     height, values = na + 2 * HALO, 4 * TILE
     side = HALO * height
@@ -277,10 +292,10 @@
             tiles[start + 8 * g : start + 8 * (g + 1), :] = lines[0:8, g * values : (g + 1) * values]
     zero_ends(sensors)
     sensors[8 : 8 + 2 * side + wide, :] = dot(tiles[...].astype(BF16), spread[...])
-    vectors = sensor_vectors(sensors, 8 + height, coeffs.shape[0])
-    result = branch(vectors, w1, b1, w2, b2, w3, b3)
-    coeffs[...] = result
-    send_means(result, 1 - HALO, na, nb // PER_CELL, height, mean_line, col, cells, payload)
+    vectors = sensor_vectors(sensors, 8 + height, hidden.shape[0])
+    result = hidden_two(vectors, w1, b1, w2, b2)
+    hidden[...] = result
+    send_means(result, 1 - HALO, na, nb // PER_CELL, height, mean_line, mean_bias, col, cells, payload)
     kx, ky = na // PER_CELL, nb // PER_CELL
     coarse[0 : kx + 2, :] = edge[2][8 : 10 + kx, :]
     coarse[8 * (ky + 1) : 8 * (ky + 1) + kx + 2, :] = edge[3][8 : 10 + kx, :]
@@ -296,11 +311,11 @@
 
 
 def next_kernel(
-    k, na, nb, n_row, n_col, cells, gathered, before, sensor_trunk, coarse, w1, b1, w2, b2, w3, b3,
-    mean_line, coeffs, payload, sensors, lines,
+    k, na, nb, n_row, n_col, cells, gathered, before, w_sensors, b_sensors, coarse, w1, b1, w2, b2, mean_line,
+    mean_bias, w3, b3, result, payload, sensors, lines,
 ):
     height = na + 2 * HALO
-    predicted = dot(before[...], sensor_trunk[...])
+    predicted = dot(before[...], w_sensors[...]) + b_sensors[0:1, :]
     found = corrections(gathered, coarse, n_row, n_col, cells)
     found = jnp.broadcast_to(found, (found.shape[0], sensors.shape[1]))
     row, col = lax.axis_index("row"), lax.axis_index("col")
@@ -323,13 +338,16 @@
         value = predicted[i * height : (i + 1) * height, :] + lines[cell * height : (cell + 1) * height, :]
         sensors[8 + i * height : 8 + (i + 1) * height, :] = jnp.where(inside > 0.5, value, 0.0)
     if k < ITERS:
-        vectors = sensor_vectors(sensors, 8 + height, coeffs.shape[0])
+        vectors = sensor_vectors(sensors, 8 + height, result.shape[0])
     else:
         vectors = own_vectors(na, nb, sensors, 8 + height)
-    result = branch(vectors, w1, b1, w2, b2, w3, b3)
-    coeffs[...] = result
+    hidden = hidden_two(vectors, w1, b1, w2, b2)
+    if k < ITERS:
+        result[...] = hidden
+    else:
+        result[...] = (dot(hidden, w3[...]) + b3[...]).astype(BF16)
     skip = (k - HALO, height) if k < ITERS else (0, na)
-    send_means(result, skip[0], na, nb // PER_CELL, skip[1], mean_line, col, cells, payload)
+    send_means(hidden, skip[0], na, nb // PER_CELL, skip[1], mean_line, mean_bias, col, cells, payload)
 
 
 def field_kernel(na, nb, n_row, n_col, cells, gathered, coarse, coeffs, trunk, out, correction, ready, sent):
@@ -450,19 +468,25 @@
         bias_sensor.reshape(1, hid),
         w_middle,
         bias_middle.reshape(1, hid),
-        w_latent,
-        bias_latent.reshape(1, latent),
-    )
-
-    sensor_trunk, mean_line = call(
+    )
+
+    b_latent = bias_latent.reshape(1, latent)
+    w_sensors, b_sensors, mean_line, mean_bias = call(
         sensor_trunk_kernel,
-        (shape((latent, places), BF16), shape((8, latent), F32)),
+        (
+            shape((hid, places), BF16),
+            shape((8, places), F32),
+            shape((8, hid), F32),
+            shape((8, LANES), F32),
+        ),
         trunk,
         spread,
         mean_trunk,
+        w_latent,
+        b_latent,
         flops=1 << 30,
     )
-    mid, sensor_trunk = lax.optimization_barrier((mid, sensor_trunk))
+    mid, w_sensors = lax.optimization_barrier((mid, w_sensors))
 
     def region(k):
         return (nb + 2 * HALO - 2 * k) * height
@@ -470,7 +494,7 @@
     payload_shape = shape((devices, LANES), F32)
     coeffs, payload, coarse = call(
         part(first_kernel, na, nb, n_col, cells),
-        (shape((region(1), latent), BF16), payload_shape, shape((8 * (ky + 2), total), F32)),
+        (shape((region(1), hid), BF16), payload_shape, shape((8 * (ky + 2), total), F32)),
         mid,
         first,
         second,
@@ -480,19 +504,24 @@
         spread,
         *net,
         mean_line,
+        mean_bias,
         scratch=[pltpu.VMEM((region(0) + 16, places), F32), pltpu.VMEM((region(0), tile_values), F32)],
     )
     for k in range(2, ITERS + 1):
         gathered = exchange(payload)
         coeffs, payload = call(
             part(next_kernel, k, na, nb, n_row, n_col, cells),
-            (shape((region(k) if k < ITERS else nb * na, latent), BF16), payload_shape),
+            (shape((region(k) if k < ITERS else nb * na, hid if k < ITERS else latent), BF16), payload_shape),
             gathered,
             coeffs,
-            sensor_trunk,
+            w_sensors,
+            b_sensors,
             coarse,
             *net,
             mean_line,
+            mean_bias,
+            w_latent,
+            b_latent,
             scratch=[
                 pltpu.VMEM((region(k - 1) + 16, places), F32),
                 pltpu.VMEM(((ky + 2) * height, places), F32),

time: 105 us -> 105 us (level)
  transfers between devices with their start and end apart: 4 -> 4, of which waited for: 1 -> 0; matrix products, arithmetic and copies ran while one was open for 0% -> 0% of each run, Pallas kernels for 5% -> 6%
where the time goes in v9:
time: 105 us
  blocking collectives  78.3 us (75%)
  Pallas kernels  13.4 us (13%)
  starting transfers between devices  11.2 us (11%)
  local copies, waits for them, and re-layouts  1.67 us (2%)
    all_to_all x4, blocking collectives, exchange(): return lax.all_to_all(x, ('row', 'col'), 0, 0, tiled=True)  78.3 us
    pallas_call x10, Pallas kernels, call(): pl.pallas_call(kernel, out_shape=out_shape, in_specs=in_specs or [whole]...  13.4 us
    ppermute x2, starting transfers between devices, swap(): return lax.ppermute(x, 'col', pairs)  7.91 us
    ppermute x2, starting transfers between devices, shift(): lax.ppermute(x, 'row', [(i, (i + step) % n_row) for i in range(n_row)])  3.27 us
  transfers between devices with their start and end apart: 4, of which 0 were waited for; matrix products, arithmetic and copies ran while one was open for 0% of the time, Pallas kernels for 6%

profile of v9, /device:TPU:1, one launch (start us, length us, event | category | flops | bytes accessed | tf_op | source)
XLA Modules:
  0.0 104.9 jit_solution(10208985354045522596)
XLA Ops:
  0.0 0.0 copy-start.5
  0.0 1.5 %fusion = (f32[256,768]{1,0:T(8,128)S(1)}, f32[256,768]{1,0:T(8,128)S(1)}) fusion(f32[1024,768]{1,0:T(8,128)} %param.10), kind=kLoop, calls=%fused_computation | loop fusion | bytes 3145728 | tf_op jit(solution)/shard_map/slice | solution.py:437
  1.5 0.0 copy-done.5
  1.5 0.0 copy-start.8
  1.5 0.4 shard_map.100
  2.0 0.0 copy-start.3
  2.0 2.6 %collective-permute-start = (bf16[8,3072]{1,0:T(8,128)(2,1)S(1)}, bf16[8,3072]{1,0:T(8,128)(2,1)S(1)}, u32[]{:S(2)}, u32[]{:S(2)}) collective-permute-start(bf16[8,3072]{1,0:T(8,128)(2,1)S(1)} %get-tuple-element.43), channel_id=1, source_target_pairs={{0,32},{32,64},{64,96},{96,128},{128,160},{160,192},{192,224},{224... | collective-permute-start | bytes 147464 | tf_op jit(solution)/shard_map/ppermute | solution.py:416
  4.6 0.7 collective-permute-start.1
  5.3 0.0 copy-done.8
  5.3 0.1 slice.22
  5.4 0.0 copy-done.3
  5.4 3.0 %shard_map.102 = (bf16[512,4096]{1,0:T(8,128)(2,1)S(1)}, f32[512,128]{1,0:T(8,128)S(1)}, bf16[512,512]{1,0:T(8,128)(2,1)S(1)}) custom-call(bf16[512,4096]{1,0:T(8,128)(2,1)} %trunk_hbm.1, bf16[512,512]{1,0:T(8,128)(2,1)S(1)} %copy-done.3), custom_call_target="tpu_custom_call" | custom-call | flops 4294967296 | bytes 1048576 | tf_op jit(solution)/shard_map/pallas_call | solution.py:39
  8.4 0.4 shard_map.101
  8.8 0.0 collective-permute-done.above
  8.8 0.0 collective-permute-done.1.below
  8.8 0.0 copy-start
  8.8 0.0 copy-start.1
  8.8 0.0 copy-start.2
  8.8 0.1 shard_map.103
  9.0 0.0 copy-start.4
  9.0 0.0 copy-start.6
  9.0 0.0 copy-start.7
  9.0 0.7 collective-permute-start.2
  9.7 7.2 %collective-permute-start.3 = (bf16[16,3072]{1,0:T(8,128)(2,1)S(1)}, bf16[16,3072]{1,0:T(8,128)(2,1)S(1)}, u32[]{:S(2)}, u32[]{:S(2)}) collective-permute-start(bf16[16,3072]{1,0:T(8,128)(2,1)S(1)} %get-tuple-element.54), channel_id=1, source_target_pairs={{0,31},{1,2},{2,1},{3,4},{4,3},{5,6},{6,5},{7,8},{8,7},{9,10},{10,... | collective-permute-start | bytes 294920 | tf_op jit(solution)/shard_map/ppermute | solution.py:420
  16.9 0.0 copy-done
  16.9 0.0 copy-done.1
  16.9 0.0 copy-done.2
  16.9 2.7 %shard_map.104 = (bf16[512,512]{1,0:T(8,128)(2,1)S(1)}, f32[8,512]{1,0:T(8,128)S(1)}, f32[8,512]{1,0:T(8,128)S(1)}, f32[8,128]{1,0:T(8,128)S(1)}) custom-call(bf16[512,4096]{1,0:T(8,128)(2,1)S(1)} %get-tuple-element.49.trunk, bf16[256,512]{1,0:T(8,128)(2,1)S(1)} %copy-done.1, f32[512,128]{1,0:T(8,128)S(1)} %get-tuple-element.50.mean_trunk, ...), custom_call_target="tpu_custom_call" | custom-call | flops 1073741824 | bytes 1048576 | tf_op jit(solution)/shard_map/pallas_call | solution.py:39
  19.7 0.0 collective-permute-done.2.first
  19.7 0.0 collective-permute-done.3.second
  19.7 0.0 copy-done.4
  19.7 0.0 copy-done.6
  19.7 0.0 copy-done.7
  19.8 1.0 shard_map.105
  20.8 23.2 %all_to_all.44 = f32[256,1,128]{2,1,0:T(1,128)S(1)} all-to-all(f32[256,1,128]{2,1,0:T(1,128)S(1)} %bitcast.28), channel_id=1, replica_groups=mesh['row'=8,'col'=32] {'row','col'}, dimensions={0} | all-to-all | bytes 262144 | tf_op jit(solution)/shard_map/all_to_all | solution.py:423
  44.0 1.2 %shard_map.106 = (bf16[384,512]{1,0:T(8,128)(2,1)S(1)}, f32[256,128]{1,0:T(8,128)S(1)}) custom-call(f32[256,128]{1,0:T(8,128)S(1)} %bitcast.29, bf16[432,512]{1,0:T(8,128)(2,1)S(1)} %get-tuple-element.59.before, bf16[512,512]{1,0:T(8,128)(2,1)S(1)} %get-tuple-element.60.w_sensors, f32[8,512]{1,0:T(8,128)S(1)} %get-tuple-element.61.b_sensors, ...), custom_call_target="tpu_custom_call" | custom-call | flops 2147483648 | bytes 1048576 | tf_op jit(solution)/shard_map/pallas_call | solution.py:39
  45.2 18.3 %all_to_all.45 = f32[256,1,128]{2,1,0:T(1,128)S(1)} all-to-all(f32[256,1,128]{2,1,0:T(1,128)S(1)} %bitcast.31), channel_id=1, replica_groups=mesh['row'=8,'col'=32] {'row','col'}, dimensions={0} | all-to-all | bytes 262144 | tf_op jit(solution)/shard_map/all_to_all | solution.py:423
  63.5 1.2 %shard_map.107 = (bf16[336,512]{1,0:T(8,128)(2,1)S(1)}, f32[256,128]{1,0:T(8,128)S(1)}) custom-call(f32[256,128]{1,0:T(8,128)S(1)} %bitcast.30, bf16[384,512]{1,0:T(8,128)(2,1)S(1)} %get-tuple-element.64.before, bf16[512,512]{1,0:T(8,128)(2,1)S(1)} %get-tuple-element.60.w_sensors, f32[8,512]{1,0:T(8,128)S(1)} %get-tuple-element.61.b_sensors, ...), custom_call_target="tpu_custom_call" | custom-call | flops 2147483648 | bytes 1048576 | tf_op jit(solution)/shard_map/pallas_call | solution.py:39
  64.7 18.5 %all_to_all.46 = f32[256,1,128]{2,1,0:T(1,128)S(1)} all-to-all(f32[256,1,128]{2,1,0:T(1,128)S(1)} %bitcast.32), channel_id=1, replica_groups=mesh['row'=8,'col'=32] {'row','col'}, dimensions={0} | all-to-all | bytes 262144 | tf_op jit(solution)/shard_map/all_to_all | solution.py:423
  83.2 1.1 %shard_map.108 = (bf16[192,512]{1,0:T(8,128)(2,1)S(1)}, f32[256,128]{1,0:T(8,128)S(1)}) custom-call(f32[256,128]{1,0:T(8,128)S(1)} %bitcast.26, bf16[336,512]{1,0:T(8,128)(2,1)S(1)} %get-tuple-element.66.before, bf16[512,512]{1,0:T(8,128)(2,1)S(1)} %get-tuple-element.60.w_sensors, f32[8,512]{1,0:T(8,128)S(1)} %get-tuple-element.61.b_sensors, ...), custom_call_target="tpu_custom_call" | custom-call | flops 2147483648 | bytes 1048576 | tf_op jit(solution)/shard_map/pallas_call | solution.py:39
  84.2 18.3 %all_to_all.47 = f32[256,1,128]{2,1,0:T(1,128)S(1)} all-to-all(f32[256,1,128]{2,1,0:T(1,128)S(1)} %bitcast.27), channel_id=1, replica_groups=mesh['row'=8,'col'=32] {'row','col'}, dimensions={0} | all-to-all | bytes 262144 | tf_op jit(solution)/shard_map/all_to_all | solution.py:423
  102.5 2.2 %shard_map.109 = f32[16,64,768]{2,1,0:T(8,128)} custom-call(f32[256,128]{1,0:T(8,128)S(1)} %bitcast.33, f32[12,3072]{1,0:T(8,128)S(1)} %copy-done.5, bf16[192,512]{1,0:T(8,128)(2,1)S(1)} %get-tuple-element.68.coeffs, bf16[512,4096]{1,0:T(8,128)(2,1)S(1)} %get-tuple-element.49.trunk), custom_call_target="tpu_custom_call" | custom-call | flops 2147483648 | bytes 1048576 | tf_op jit(solution)/shard_map/pallas_call | solution.py:39
Async XLA Ops:
  0.0 1.5 %copy-start.5 = (f32[12,3072]{1,0:T(8,128)S(1)}, f32[12,3072]{1,0:T(8,128)}, u32[]{:S(2)}) copy-start(f32[12,3072]{1,0:T(8,128)} %coarse.5) | copy-start | bytes 442372
  1.5 3.8 %copy-start.8 = (f32[1024,768]{1,0:T(8,128)S(1)}, f32[1024,768]{1,0:T(8,128)}, u32[]{:S(2)}) copy-start(f32[1024,768]{1,0:T(8,128)} %param.10) | copy-start | bytes 9437188
  2.0 3.4 %copy-start.3 = (bf16[512,512]{1,0:T(8,128)(2,1)S(1)}, bf16[512,512]{1,0:T(8,128)(2,1)}, u32[]{:S(2)}) copy-start(bf16[512,512]{1,0:T(8,128)(2,1)} %w_sensor.1) | copy-start | bytes 1572868
  2.0 6.8 %collective-permute-start = (bf16[8,3072]{1,0:T(8,128)(2,1)S(1)}, bf16[8,3072]{1,0:T(8,128)(2,1)S(1)}, u32[]{:S(2)}, u32[]{:S(2)}) collective-permute-start(bf16[8,3072]{1,0:T(8,128)(2,1)S(1)} %get-tuple-element.43), channel_id=1, source_target_pairs={{0,32},{32,64},{64,96},{96,128},{128,160},{160,192},{192,224},{224... | collective-permute-start | bytes 147464 | tf_op jit(solution)/shard_map/ppermute | solution.py:416
  4.6 4.2 %collective-permute-start.1 = (bf16[8,3072]{1,0:T(8,128)(2,1)S(1)}, bf16[8,3072]{1,0:T(8,128)(2,1)S(1)}, u32[]{:S(2)}, u32[]{:S(2)}) collective-permute-start(bf16[8,3072]{1,0:T(8,128)(2,1)S(1)} %get-tuple-element.44), channel_id=1, source_target_pairs={{0,224},{32,0},{64,32},{96,64},{128,96},{160,128},{192,160},{224,1... | collective-permute-start | bytes 147464 | tf_op jit(solution)/shard_map/ppermute | solution.py:416
  8.8 8.1 %copy-start = (bf16[512,512]{1,0:T(8,128)(2,1)S(1)}, bf16[512,512]{1,0:T(8,128)(2,1)}, u32[]{:S(2)}) copy-start(bf16[512,512]{1,0:T(8,128)(2,1)} %w3.7) | copy-start | bytes 1572868
  8.8 8.1 %copy-start.1 = (bf16[256,512]{1,0:T(8,128)(2,1)S(1)}, bf16[256,512]{1,0:T(8,128)(2,1)}, u32[]{:S(2)}) copy-start(bf16[256,512]{1,0:T(8,128)(2,1)} %constant.2.clone.spread) | copy-start | bytes 786436
  8.8 8.1 %copy-start.2 = (f32[512]{0:T(512)S(1)}, f32[512]{0:T(512)}, u32[]{:S(2)}) copy-start(f32[512]{0:T(512)} %param.16) | copy-start | bytes 6148
  9.0 10.7 %copy-start.4 = (bf16[512,512]{1,0:T(8,128)(2,1)S(1)}, bf16[512,512]{1,0:T(8,128)(2,1)}, u32[]{:S(2)}) copy-start(bf16[512,512]{1,0:T(8,128)(2,1)} %w2.7) | copy-start | bytes 1572868
  9.0 10.7 %copy-start.6 = (f32[512]{0:T(512)S(1)}, f32[512]{0:T(512)}, u32[]{:S(2)}) copy-start(f32[512]{0:T(512)} %param.12) | copy-start | bytes 6148
  9.0 10.7 %copy-start.7 = (f32[512]{0:T(512)S(1)}, f32[512]{0:T(512)}, u32[]{:S(2)}) copy-start(f32[512]{0:T(512)} %param.14) | copy-start | bytes 6148
  9.0 10.7 %collective-permute-start.2 = (bf16[16,3072]{1,0:T(8,128)(2,1)S(1)}, bf16[16,3072]{1,0:T(8,128)(2,1)S(1)}, u32[]{:S(2)}, u32[]{:S(2)}) collective-permute-start(bf16[16,3072]{1,0:T(8,128)(2,1)S(1)} %get-tuple-element.53), channel_id=1, source_target_pairs={{0,1},{1,0},{2,3},{3,2},{4,5},{5,4},{6,7},{7,6},{8,9},{9,8},{10,11... | collective-permute-start | bytes 294920 | tf_op jit(solution)/shard_map/ppermute | solution.py:420
  9.7 10.0 %collective-permute-start.3 = (bf16[16,3072]{1,0:T(8,128)(2,1)S(1)}, bf16[16,3072]{1,0:T(8,128)(2,1)S(1)}, u32[]{:S(2)}, u32[]{:S(2)}) collective-permute-start(bf16[16,3072]{1,0:T(8,128)(2,1)S(1)} %get-tuple-element.54), channel_id=1, source_target_pairs={{0,31},{1,2},{2,1},{3,4},{4,3},{5,6},{6,5},{7,8},{8,7},{9,10},{10,... | collective-permute-start | bytes 294920 | tf_op jit(solution)/shard_map/ppermute | solution.py:420

commit v10 on v9

--- a/solution.py
+++ b/solution.py
@@ -317,7 +317,7 @@
     height = na + 2 * HALO
     predicted = dot(before[...], w_sensors[...]) + b_sensors[0:1, :]
     found = corrections(gathered, coarse, n_row, n_col, cells)
-    found = jnp.broadcast_to(found, (found.shape[0], sensors.shape[1]))
+    found = jnp.broadcast_to(found, (found.shape[0], LANES))
     row, col = lax.axis_index("row"), lax.axis_index("col")
     a_at = row * na - HALO + lax.broadcasted_iota(jnp.int32, (height, 1), 0)
     a_ok = (a_at >= 0) & (a_at < n_row * na)
@@ -335,7 +335,8 @@
         b_at = col * nb - HALO + b
         inside = jnp.where(a_ok & (b_at >= 0) & (b_at < n_col * nb), 1.0, 0.0)
         cell = b // PER_CELL
-        value = predicted[i * height : (i + 1) * height, :] + lines[cell * height : (cell + 1) * height, :]
+        add = lines[cell * height : (cell + 1) * height, :]
+        value = predicted[i * height : (i + 1) * height, :] + jnp.concatenate([add] * (sensors.shape[1] // LANES), axis=1)
         sensors[8 + i * height : 8 + (i + 1) * height, :] = jnp.where(inside > 0.5, value, 0.0)
     if k < ITERS:
         vectors = sensor_vectors(sensors, 8 + height, result.shape[0])
@@ -524,7 +525,7 @@
             b_latent,
             scratch=[
                 pltpu.VMEM((region(k - 1) + 16, places), F32),
-                pltpu.VMEM(((ky + 2) * height, places), F32),
+                pltpu.VMEM(((ky + 2) * height, LANES), F32),
             ],
         )
     gathered = exchange(payload)

time: 105 us -> 105 us (level)
  no operation moved by 1% of the time
where the time goes in v10:
time: 105 us
  blocking collectives  78.3 us (75%)
  Pallas kernels  13.4 us (13%)
  starting transfers between devices  11.2 us (11%)
  local copies, waits for them, and re-layouts  1.67 us (2%)
    all_to_all x4, blocking collectives, exchange(): return lax.all_to_all(x, ('row', 'col'), 0, 0, tiled=True)  78.3 us
    pallas_call x10, Pallas kernels, call(): pl.pallas_call(kernel, out_shape=out_shape, in_specs=in_specs or [whole]...  13.4 us
    ppermute x2, starting transfers between devices, swap(): return lax.ppermute(x, 'col', pairs)  7.91 us
    ppermute x2, starting transfers between devices, shift(): lax.ppermute(x, 'row', [(i, (i + step) % n_row) for i in range(n_row)])  3.27 us
  transfers between devices with their start and end apart: 4, of which 0 were waited for; matrix products, arithmetic and copies ran while one was open for 0% of the time, Pallas kernels for 6%

profile of v10, /device:TPU:1, one launch (start us, length us, event | category | flops | bytes accessed | tf_op | source)
XLA Modules:
  0.0 104.9 jit_solution(4020890530963222240)
XLA Ops:
  0.0 0.0 copy-start.5
  0.0 1.5 %fusion = (f32[256,768]{1,0:T(8,128)S(1)}, f32[256,768]{1,0:T(8,128)S(1)}) fusion(f32[1024,768]{1,0:T(8,128)} %param.10), kind=kLoop, calls=%fused_computation | loop fusion | bytes 3145728 | tf_op jit(solution)/shard_map/slice | solution.py:438
  1.5 0.0 copy-done.5
  1.5 0.0 copy-start.8
  1.5 0.4 shard_map.100
  2.0 0.0 copy-start.3
  2.0 2.6 %collective-permute-start = (bf16[8,3072]{1,0:T(8,128)(2,1)S(1)}, bf16[8,3072]{1,0:T(8,128)(2,1)S(1)}, u32[]{:S(2)}, u32[]{:S(2)}) collective-permute-start(bf16[8,3072]{1,0:T(8,128)(2,1)S(1)} %get-tuple-element.43), channel_id=1, source_target_pairs={{0,32},{32,64},{64,96},{96,128},{128,160},{160,192},{192,224},{224... | collective-permute-start | bytes 147464 | tf_op jit(solution)/shard_map/ppermute | solution.py:417
  4.6 0.7 collective-permute-start.1
  5.3 0.0 copy-done.8
  5.3 0.1 slice.22
  5.4 0.0 copy-done.3
  5.4 3.0 %shard_map.102 = (bf16[512,4096]{1,0:T(8,128)(2,1)S(1)}, f32[512,128]{1,0:T(8,128)S(1)}, bf16[512,512]{1,0:T(8,128)(2,1)S(1)}) custom-call(bf16[512,4096]{1,0:T(8,128)(2,1)} %trunk_hbm.1, bf16[512,512]{1,0:T(8,128)(2,1)S(1)} %copy-done.3), custom_call_target="tpu_custom_call" | custom-call | flops 4294967296 | bytes 1048576 | tf_op jit(solution)/shard_map/pallas_call | solution.py:39
  8.4 0.4 shard_map.101
  8.8 0.0 collective-permute-done.above
  8.8 0.0 collective-permute-done.1.below
  8.8 0.0 copy-start
  8.8 0.0 copy-start.1
  8.8 0.0 copy-start.2
  8.8 0.1 shard_map.103
  9.0 0.0 copy-start.4
  9.0 0.0 copy-start.6
  9.0 0.0 copy-start.7
  9.0 0.7 collective-permute-start.2
  9.7 7.2 %collective-permute-start.3 = (bf16[16,3072]{1,0:T(8,128)(2,1)S(1)}, bf16[16,3072]{1,0:T(8,128)(2,1)S(1)}, u32[]{:S(2)}, u32[]{:S(2)}) collective-permute-start(bf16[16,3072]{1,0:T(8,128)(2,1)S(1)} %get-tuple-element.54), channel_id=1, source_target_pairs={{0,31},{1,2},{2,1},{3,4},{4,3},{5,6},{6,5},{7,8},{8,7},{9,10},{10,... | collective-permute-start | bytes 294920 | tf_op jit(solution)/shard_map/ppermute | solution.py:421
  16.9 0.0 copy-done
  16.9 0.0 copy-done.1
  16.9 0.0 copy-done.2
  16.9 2.7 %shard_map.104 = (bf16[512,512]{1,0:T(8,128)(2,1)S(1)}, f32[8,512]{1,0:T(8,128)S(1)}, f32[8,512]{1,0:T(8,128)S(1)}, f32[8,128]{1,0:T(8,128)S(1)}) custom-call(bf16[512,4096]{1,0:T(8,128)(2,1)S(1)} %get-tuple-element.49.trunk, bf16[256,512]{1,0:T(8,128)(2,1)S(1)} %copy-done.1, f32[512,128]{1,0:T(8,128)S(1)} %get-tuple-element.50.mean_trunk, ...), custom_call_target="tpu_custom_call" | custom-call | flops 1073741824 | bytes 1048576 | tf_op jit(solution)/shard_map/pallas_call | solution.py:39
  19.7 0.0 collective-permute-done.2.first
  19.7 0.0 collective-permute-done.3.second
  19.7 0.0 copy-done.4
  19.7 0.0 copy-done.6
  19.7 0.0 copy-done.7
  19.8 1.0 shard_map.105
  20.8 23.2 %all_to_all.44 = f32[256,1,128]{2,1,0:T(1,128)S(1)} all-to-all(f32[256,1,128]{2,1,0:T(1,128)S(1)} %bitcast.28), channel_id=1, replica_groups=mesh['row'=8,'col'=32] {'row','col'}, dimensions={0} | all-to-all | bytes 262144 | tf_op jit(solution)/shard_map/all_to_all | solution.py:424
  44.0 1.2 %shard_map.106 = (bf16[384,512]{1,0:T(8,128)(2,1)S(1)}, f32[256,128]{1,0:T(8,128)S(1)}) custom-call(f32[256,128]{1,0:T(8,128)S(1)} %bitcast.29, bf16[432,512]{1,0:T(8,128)(2,1)S(1)} %get-tuple-element.59.before, bf16[512,512]{1,0:T(8,128)(2,1)S(1)} %get-tuple-element.60.w_sensors, f32[8,512]{1,0:T(8,128)S(1)} %get-tuple-element.61.b_sensors, ...), custom_call_target="tpu_custom_call" | custom-call | flops 2147483648 | bytes 1048576 | tf_op jit(solution)/shard_map/pallas_call | solution.py:39
  45.2 18.3 %all_to_all.45 = f32[256,1,128]{2,1,0:T(1,128)S(1)} all-to-all(f32[256,1,128]{2,1,0:T(1,128)S(1)} %bitcast.31), channel_id=1, replica_groups=mesh['row'=8,'col'=32] {'row','col'}, dimensions={0} | all-to-all | bytes 262144 | tf_op jit(solution)/shard_map/all_to_all | solution.py:424
  63.5 1.2 %shard_map.107 = (bf16[336,512]{1,0:T(8,128)(2,1)S(1)}, f32[256,128]{1,0:T(8,128)S(1)}) custom-call(f32[256,128]{1,0:T(8,128)S(1)} %bitcast.30, bf16[384,512]{1,0:T(8,128)(2,1)S(1)} %get-tuple-element.64.before, bf16[512,512]{1,0:T(8,128)(2,1)S(1)} %get-tuple-element.60.w_sensors, f32[8,512]{1,0:T(8,128)S(1)} %get-tuple-element.61.b_sensors, ...), custom_call_target="tpu_custom_call" | custom-call | flops 2147483648 | bytes 1048576 | tf_op jit(solution)/shard_map/pallas_call | solution.py:39
  64.7 18.5 %all_to_all.46 = f32[256,1,128]{2,1,0:T(1,128)S(1)} all-to-all(f32[256,1,128]{2,1,0:T(1,128)S(1)} %bitcast.32), channel_id=1, replica_groups=mesh['row'=8,'col'=32] {'row','col'}, dimensions={0} | all-to-all | bytes 262144 | tf_op jit(solution)/shard_map/all_to_all | solution.py:424
  83.2 1.0 shard_map.108
  84.2 18.3 %all_to_all.47 = f32[256,1,128]{2,1,0:T(1,128)S(1)} all-to-all(f32[256,1,128]{2,1,0:T(1,128)S(1)} %bitcast.27), channel_id=1, replica_groups=mesh['row'=8,'col'=32] {'row','col'}, dimensions={0} | all-to-all | bytes 262144 | tf_op jit(solution)/shard_map/all_to_all | solution.py:424
  102.5 2.2 %shard_map.109 = f32[16,64,768]{2,1,0:T(8,128)} custom-call(f32[256,128]{1,0:T(8,128)S(1)} %bitcast.33, f32[12,3072]{1,0:T(8,128)S(1)} %copy-done.5, bf16[192,512]{1,0:T(8,128)(2,1)S(1)} %get-tuple-element.68.coeffs, bf16[512,4096]{1,0:T(8,128)(2,1)S(1)} %get-tuple-element.49.trunk), custom_call_target="tpu_custom_call" | custom-call | flops 2147483648 | bytes 1048576 | tf_op jit(solution)/shard_map/pallas_call | solution.py:39
Async XLA Ops:
  0.0 1.5 %copy-start.5 = (f32[12,3072]{1,0:T(8,128)S(1)}, f32[12,3072]{1,0:T(8,128)}, u32[]{:S(2)}) copy-start(f32[12,3072]{1,0:T(8,128)} %coarse.5) | copy-start | bytes 442372
  1.5 3.8 %copy-start.8 = (f32[1024,768]{1,0:T(8,128)S(1)}, f32[1024,768]{1,0:T(8,128)}, u32[]{:S(2)}) copy-start(f32[1024,768]{1,0:T(8,128)} %param.10) | copy-start | bytes 9437188
  2.0 3.4 %copy-start.3 = (bf16[512,512]{1,0:T(8,128)(2,1)S(1)}, bf16[512,512]{1,0:T(8,128)(2,1)}, u32[]{:S(2)}) copy-start(bf16[512,512]{1,0:T(8,128)(2,1)} %w_sensor.1) | copy-start | bytes 1572868
  2.0 6.8 %collective-permute-start = (bf16[8,3072]{1,0:T(8,128)(2,1)S(1)}, bf16[8,3072]{1,0:T(8,128)(2,1)S(1)}, u32[]{:S(2)}, u32[]{:S(2)}) collective-permute-start(bf16[8,3072]{1,0:T(8,128)(2,1)S(1)} %get-tuple-element.43), channel_id=1, source_target_pairs={{0,32},{32,64},{64,96},{96,128},{128,160},{160,192},{192,224},{224... | collective-permute-start | bytes 147464 | tf_op jit(solution)/shard_map/ppermute | solution.py:417
  4.6 4.2 %collective-permute-start.1 = (bf16[8,3072]{1,0:T(8,128)(2,1)S(1)}, bf16[8,3072]{1,0:T(8,128)(2,1)S(1)}, u32[]{:S(2)}, u32[]{:S(2)}) collective-permute-start(bf16[8,3072]{1,0:T(8,128)(2,1)S(1)} %get-tuple-element.44), channel_id=1, source_target_pairs={{0,224},{32,0},{64,32},{96,64},{128,96},{160,128},{192,160},{224,1... | collective-permute-start | bytes 147464 | tf_op jit(solution)/shard_map/ppermute | solution.py:417
  8.8 8.1 %copy-start = (bf16[512,512]{1,0:T(8,128)(2,1)S(1)}, bf16[512,512]{1,0:T(8,128)(2,1)}, u32[]{:S(2)}) copy-start(bf16[512,512]{1,0:T(8,128)(2,1)} %w3.7) | copy-start | bytes 1572868
  8.8 8.1 %copy-start.1 = (bf16[256,512]{1,0:T(8,128)(2,1)S(1)}, bf16[256,512]{1,0:T(8,128)(2,1)}, u32[]{:S(2)}) copy-start(bf16[256,512]{1,0:T(8,128)(2,1)} %constant.2.clone.spread) | copy-start | bytes 786436
  8.8 8.1 %copy-start.2 = (f32[512]{0:T(512)S(1)}, f32[512]{0:T(512)}, u32[]{:S(2)}) copy-start(f32[512]{0:T(512)} %param.16) | copy-start | bytes 6148
  9.0 10.7 %copy-start.4 = (bf16[512,512]{1,0:T(8,128)(2,1)S(1)}, bf16[512,512]{1,0:T(8,128)(2,1)}, u32[]{:S(2)}) copy-start(bf16[512,512]{1,0:T(8,128)(2,1)} %w2.7) | copy-start | bytes 1572868
  9.0 10.7 %copy-start.6 = (f32[512]{0:T(512)S(1)}, f32[512]{0:T(512)}, u32[]{:S(2)}) copy-start(f32[512]{0:T(512)} %param.12) | copy-start | bytes 6148
  9.0 10.7 %copy-start.7 = (f32[512]{0:T(512)S(1)}, f32[512]{0:T(512)}, u32[]{:S(2)}) copy-start(f32[512]{0:T(512)} %param.14) | copy-start | bytes 6148
  9.0 10.7 %collective-permute-start.2 = (bf16[16,3072]{1,0:T(8,128)(2,1)S(1)}, bf16[16,3072]{1,0:T(8,128)(2,1)S(1)}, u32[]{:S(2)}, u32[]{:S(2)}) collective-permute-start(bf16[16,3072]{1,0:T(8,128)(2,1)S(1)} %get-tuple-element.53), channel_id=1, source_target_pairs={{0,1},{1,0},{2,3},{3,2},{4,5},{5,4},{6,7},{7,6},{8,9},{9,8},{10,11... | collective-permute-start | bytes 294920 | tf_op jit(solution)/shard_map/ppermute | solution.py:421
  9.7 10.0 %collective-permute-start.3 = (bf16[16,3072]{1,0:T(8,128)(2,1)S(1)}, bf16[16,3072]{1,0:T(8,128)(2,1)S(1)}, u32[]{:S(2)}, u32[]{:S(2)}) collective-permute-start(bf16[16,3072]{1,0:T(8,128)(2,1)S(1)} %get-tuple-element.54), channel_id=1, source_target_pairs={{0,31},{1,2},{2,1},{3,4},{4,3},{5,6},{6,5},{7,8},{8,7},{9,10},{10,... | collective-permute-start | bytes 294920 | tf_op jit(solution)/shard_map/ppermute | solution.py:421
